TPU v7x, 32 devices: a whole 2x2x4 slice. The times are simulated.
32 devices in a mesh: ctx: 8 (over z, y), head: 4 (over x, core).
Axes of the slice: x: 2, y: 2, z: 4, core: 2. Of those that a mesh axis runs over, the one named last changes fastest.
Arguments:
- queries: bfloat16 [12288, 2048], P('ctx', 'head'), may hold values from -20 to 20
- keys: bfloat16 [12288, 2048], P('ctx', 'head'), may hold values from -20 to 20
- values: bfloat16 [12288, 2048], P('ctx', 'head'), may hold values from -6 to 6
- offsets: int32 [3, 16], replicated, may hold values from 0 to 7, as said below
- out_weight: bfloat16 [2048, 2048], replicated, may hold values from -1.1953125 to 1.1953125
Outputs:
- mixed: bfloat16 [12288, 2048], P(('ctx', 'head'))
Inputs may be any that keep to these rules, and one draw needn't show every extreme that they name: `offsets`: each offset of row k - 1 lies in 0 to 2^k - 1; in the last row every value of that range occurs.
All inputs are finite; a program needn't handle non-finite values.
Results may differ from a plain program's by a relative error of at most 0.0053.
Values may be sent and summed in bfloat16 or wider, within the bound.
No kernel may reach another device: no remote copies, remote signals or barrier semaphores. Data moves between devices by JAX's collectives and lax.ppermute only.
A program may use at most 192 MiB of HBM per device.

v0:
```python
import math

import jax
import jax.numpy as jnp
from jax import lax
from jax.sharding import PartitionSpec as P

DH = 128
LEVELS = 4


NEG_FILL = -1e30


def swapped(value, axis, bit):
    mask = 2**bit
    pairs = [(source, source ^ mask) for source in range(lax.axis_size(axis))]
    return lax.ppermute(value, axis, pairs)


def pick_rows(source, shifts, dilation):
    hits = jnp.arange(dilation)[:, None] == shifts[None, :]
    shaped = source.reshape(source.shape[0] // dilation, dilation, source.shape[1], source.shape[2])
    return jnp.sum(jnp.where(hits[None, :, :, None], shaped, jnp.zeros((), source.dtype)), axis=1)


def block_attend(query_rows, key_rows, value_rows, query_pos):
    number = query_rows.shape[0]
    heads_here = query_rows.shape[1]
    width_head = query_rows.shape[2]
    height = 512 if number % 512 == 0 else number
    blocks = number // height
    key_pos = jnp.arange(key_rows.shape[0])
    factor = 1.0 / math.sqrt(width_head)

    def one_block(items):
        rows_now, pos_now = items
        scores = (
            jnp.einsum("qhd,khd->hqk", rows_now, key_rows, preferred_element_type=jnp.float32)
            * factor
        )
        scores = jnp.where(pos_now[None, :, None] >= key_pos[None, None, :], scores, NEG_FILL)
        row_max = jnp.max(scores, axis=2)
        weights = jnp.exp(scores - row_max[:, :, None])
        row_sum = jnp.sum(weights, axis=2)
        weighted = jnp.einsum(
            "hqk,khd->qhd",
            weights.astype(jnp.bfloat16),
            value_rows,
            preferred_element_type=jnp.float32,
        )
        return (row_max.T, row_sum.T, weighted)

    shaped_rows = query_rows.reshape(blocks, height, heads_here, width_head)
    maxima, sums_all, outputs = lax.map(one_block, (shaped_rows, query_pos.reshape(blocks, height)))
    return (
        maxima.reshape(number, heads_here),
        sums_all.reshape(number, heads_here),
        outputs.reshape(number, heads_here, width_head),
    )


def spread_rows(parts, shifts, dilation):
    row_max, row_sum, weighted = parts
    hits = jnp.arange(dilation)[:, None] == shifts[None, :]
    number = row_max.shape[0] * dilation
    heads_here = row_max.shape[1]
    full_max = jnp.where(hits[None], row_max[:, None, :], NEG_FILL).reshape(number, heads_here)
    full_sum = jnp.where(hits[None], row_sum[:, None, :], 0.0).reshape(number, heads_here)
    full_out = jnp.where(hits[None, :, :, None], weighted[:, None], 0.0).reshape(
        number, heads_here, weighted.shape[2]
    )
    return (full_max, full_sum, full_out)


def merge_levels(running, fresh):
    new_max = jnp.maximum(running[0], fresh[0])
    old_scale = jnp.exp(running[0] - new_max)
    new_scale = jnp.exp(fresh[0] - new_max)
    new_sum = running[1] * old_scale + fresh[1] * new_scale
    new_out = running[2] * old_scale[:, :, None] + fresh[2] * new_scale[:, :, None]
    return (new_max, new_sum, new_out)


def join_pair(mine, partner, ctx_index, bit_index):
    upper = ctx_index // 2**bit_index % 2 == 1
    joined = []
    for mine_part, other_part in zip(mine, partner):
        joined.append(
            jnp.where(
                upper,
                jnp.concatenate([other_part, mine_part], 0),
                jnp.concatenate([mine_part, other_part], 0),
            )
        )
    return tuple(joined)


def collect_level(pair, level_index, ctx_index):
    for bit_index in range(level_index):
        partner = swapped((pair[0], pair[1]), "ctx", bit_index)
        pair = join_pair(pair, partner, ctx_index, bit_index)
    return pair


def body(queries, keys, values, offsets, out_weight):
    rows_here = queries.shape[0]
    head_count = lax.axis_size("head")
    heads_here = offsets.shape[1] // head_count
    query_heads = queries.reshape(rows_here, heads_here, DH)
    key_heads = keys.reshape(rows_here, heads_here, DH)
    value_heads = values.reshape(rows_here, heads_here, DH)
    ctx_index = lax.axis_index("ctx")
    shifts_here = lax.dynamic_slice_in_dim(
        offsets, lax.axis_index("head") * heads_here, heads_here, 1
    )
    running = block_attend(query_heads, key_heads, value_heads, jnp.arange(rows_here))
    sources = []
    for level_index in range(1, LEVELS):
        dilation = 2**level_index
        own_pair = (
            pick_rows(key_heads, shifts_here[level_index - 1], dilation),
            pick_rows(value_heads, shifts_here[level_index - 1], dilation),
        )
        sources.append(collect_level(own_pair, level_index, ctx_index))
    for level_index in range(1, LEVELS):
        dilation = 2**level_index
        shifts_now = shifts_here[level_index - 1]
        query_rows = pick_rows(query_heads, shifts_now, dilation)
        span = rows_here // dilation
        query_pos = ctx_index % dilation * span + jnp.arange(span)
        parts = block_attend(
            query_rows, sources[level_index - 1][0], sources[level_index - 1][1], query_pos
        )
        running = merge_levels(running, spread_rows(parts, shifts_now, dilation))
    attended = (
        (running[2] / running[1][:, :, None])
        .astype(jnp.bfloat16)
        .reshape(rows_here, heads_here * DH)
    )
    regrouped = lax.all_to_all(attended, "head", split_axis=0, concat_axis=1, tiled=True)
    mixed = jnp.dot(regrouped, out_weight, preferred_element_type=jnp.float32)
    return mixed.astype(jnp.bfloat16)


def solution(mesh):
    placed = (P("ctx", "head"), P("ctx", "head"), P("ctx", "head"), P(), P())
    return jax.shard_map(
        body, mesh=mesh, in_specs=placed, out_specs=P(("ctx", "head"), None), check_vma=False
    )
```

profile of v0, /device:TPU:0, one launch (start us, length us, event | category | flops | bytes accessed | tf_op | source)
XLA Modules:
  0.0 430.1 jit_solution(5003775941416040465)
XLA Ops:
  0.8 6.8 %fusion.35 = (bf16[192,4,128]{2,1,0:T(4,128)(2,1)}, bf16[192,4,128]{2,1,0:T(4,128)(2,1)}, bf16[192,4,128]{2,1,0:T(4,128)(2,1)}) fusion(bf16[1536,512]{1,0:T(8,128)(2,1)} %param.9, pred[8,4]{0,1:T(4,128)(4,1)S(1)} %iota_compare_fusion.4, bf16[1536,512]{1,0:T(8,128)(2,1)} %param.8, bf16[1536,512]{1,0:T(8,128)(2,1)} %param.7), kind=kLoop, calls=%fused_computation.54 | loop fusion | flops 4423680 | bytes 5308448 | tf_op jit(solution)/shard_map/reduce_sum | solution.py:24
  18.3 7.8 %select_reduce_fusion.3 = (bf16[768,4,128]{2,1,0:T(4,128)(2,1)}, bf16[768,4,128]{2,1,0:T(4,128)(2,1)}, bf16[768,4,128]{2,1,0:T(4,128)(2,1)}) fusion(bf16[768,2,4,128]{3,2,1,0:T(4,128)(2,1)} %reshape_reshape.33, pred[2,4]{1,0:T(4,128)(4,1)S(1)} %copy.72, bf16[768,2,4,128]{3,2,1,0:T(4,128)(2,1)} %reshape_reshape.32, bf16[768,2,4,128]{3,2,1,0:T(4,128)(2,1)} %reshape_reshape.31), kind=kLoop, calls=%fused_computation.71 | loop fusion | flops 3538944 | bytes 7077896 | tf_op jit(solution)/shard_map/reduce_sum | solution.py:24
  35.6 7.0 %select_reduce_fusion = (bf16[384,4,128]{2,1,0:T(4,128)(2,1)}, bf16[384,4,128]{2,1,0:T(4,128)(2,1)}, bf16[384,4,128]{2,1,0:T(4,128)(2,1)}) fusion(bf16[384,4,4,128]{3,2,1,0:T(4,128)(2,1)} %reshape_reshape.36, pred[4,4]{1,0:T(4,128)(4,1)S(1)} %copy.82, bf16[384,4,4,128]{3,2,1,0:T(4,128)(2,1)} %reshape_reshape.35, bf16[384,4,4,128]{3,2,1,0:T(4,128)(2,1)} %reshape_reshape.34), kind=kLoop, calls=%fused_computation.68 | loop fusion | flops 4128768 | bytes 5898256 | tf_op jit(solution)/shard_map/reduce_sum | solution.py:24
  57.2 45.7 %while.3 = (s32[]{:T(128)}, f32[3,512,4]{1,2,0:T(4,128)S(1)}, f32[3,512,4]{1,2,0:T(4,128)}, f32[3,512,4,128]{3,2,1,0:T(4,128)}, s32[3,512]{1,0:T(4,128)S(1)}, /*...) while((s32[]{:T(128)}, f32[3,512,4]{1,2,0:T(4,128)S(1)}, ...), condition=%wide.region_3.4_spmd.clone, body=%wide.region_0.3_spmd.clone.sunk | while | flops 1645998080 | bytes 48830580 | solution.py:55
  66.0 4.5 %fusion.90 = f32[1,512,4,128]{3,1,2,0:T(8,128)S(1)} fusion(bf16[1536,4,128]{2,0,1:T(8,128)(2,1)} %get-tuple-element.307, f32[4,512,1536]{2,1,0:T(8,128)S(1)} %get-tuple-element.278, f32[4,512]{1,0:T(4,128)S(1)} %get-tuple-element.279, pred[512,1536]{1,0:T(8,128)(4,1)S(1)} %iota_compare_fusion.8), kind=kOutput, calls=%fused_computation.9.clone.1 | convolution fusion | flops 817889280 | bytes 15998976 | tf_op jit(solution)/shard_map/while/body/eval_jaxpr/hqk,khd->qhd/dot_general | solution.py:46
  81.0 4.5 %fusion.90 = f32[1,512,4,128]{3,1,2,0:T(8,128)S(1)} fusion(bf16[1536,4,128]{2,0,1:T(8,128)(2,1)} %get-tuple-element.307, f32[4,512,1536]{2,1,0:T(8,128)S(1)} %get-tuple-element.278, f32[4,512]{1,0:T(4,128)S(1)} %get-tuple-element.279, pred[512,1536]{1,0:T(8,128)(4,1)S(1)} %iota_compare_fusion.8), kind=kOutput, calls=%fused_computation.9.clone.1 | convolution fusion | flops 817889280 | bytes 15998976 | tf_op jit(solution)/shard_map/while/body/eval_jaxpr/hqk,khd->qhd/dot_general | solution.py:46
  107.8 4.8 %broadcast_in_dim.400 = pred[1536,4,128]{2,1,0:T(4,128)(4,1)S(1)} broadcast(pred[1536,4]{1,0:T(8,128)(4,1)S(1)} %copy.78), dimensions={0,1} | broadcast | bytes 792576 | tf_op jit(solution)/shard_map/jit(_where)/broadcast_in_dim | solution.py:24
  114.6 4.8 %broadcast_in_dim.425 = pred[1536,4,128]{2,1,0:T(4,128)(4,1)S(1)} broadcast(pred[1536,4]{1,0:T(8,128)(4,1)S(1)} %copy.93), dimensions={0,1} | broadcast | bytes 792576 | tf_op jit(solution)/shard_map/jit(_where)/broadcast_in_dim | solution.py:24
  121.3 4.8 %broadcast_in_dim.413 = pred[1536,4,128]{2,1,0:T(4,128)(4,1)S(1)} broadcast(pred[1536,4]{1,0:T(8,128)(4,1)S(1)} %copy.86), dimensions={0,1} | broadcast | bytes 792576 | tf_op jit(solution)/shard_map/jit(_where)/broadcast_in_dim | solution.py:24
  149.0 21.5 %collective-permute-done.7 = bf16[384,4,128]{2,1,0:T(4,128)(2,1)S(1)} collective-permute-done((bf16[384,4,128]{2,1,0:T(4,128)(2,1)S(1)}, bf16[384,4,128]{2,1,0:T(4,128)(2,1)S(1)}, u32[]{:S(2)}, u32[]{:S(2)}) %collective-permute-start.7) | collective-permute-done | bytes 393248 | tf_op jit(solution)/shard_map/ppermute | solution.py:18
  175.2 5.8 %maximum_select_fusion = bf16[1536,4,128]{2,1,0:T(4,128)(2,1)S(1)} fusion(bf16[768,4,128]{2,1,0:T(4,128)(2,1)} %get-tuple-element.181, bf16[768,4,128]{2,1,0:T(4,128)(2,1)} %collective-permute-done, pred[]{:T(512)S(6)} %eq.61), kind=kLoop, calls=%fused_computation.47 | loop fusion | flops 2359296 | bytes 3145729 | tf_op jit(solution)/shard_map/jit(_where)/select_n | solution.py:90
  181.0 9.1 %fusion.14 = (f32[4,768]{1,0:T(4,128)S(1)}, f32[4,768,1536]{2,1,0:T(8,128)}) fusion(pred[768,1536]{1,0:T(8,128)(4,1)S(1)} %copy-done.7, bf16[1536,4,128]{2,1,0:T(4,128)(2,1)S(1)} %maximum_select_fusion, bf16[768,4,128]{2,1,0:T(4,128)(2,1)S(1)} %copy-done.11), kind=kOutput, calls=%fused_computation.21 | convolution fusion | flops 1222112256 | bytes 22425600 | tf_op jit(solution)/shard_map/while/body/eval_jaxpr/qhd,khd->hqk/dot_general | solution.py:39
  190.1 5.8 %maximum_select_fusion.1 = bf16[1536,4,128]{2,1,0:T(4,128)(2,1)S(1)} fusion(bf16[768,4,128]{2,1,0:T(4,128)(2,1)} %get-tuple-element.180, bf16[768,4,128]{2,1,0:T(4,128)(2,1)} %collective-permute-done.1, pred[]{:T(512)S(6)} %eq.61), kind=kLoop, calls=%fused_computation.48 | loop fusion | flops 2359296 | bytes 3145729 | tf_op jit(solution)/shard_map/jit(_where)/select_n | solution.py:90
  195.9 10.6 %fusion.47 = f32[768,4,128]{0,2,1:T(8,128)} fusion(f32[4,768,1536]{2,1,0:T(8,128)} %get-tuple-element.224, f32[4,768]{1,0:T(4,128)S(1)} %get-tuple-element.223, pred[768,1536]{1,0:T(8,128)(4,1)S(1)} %copy-done.7, bf16[1536,4,128]{2,1,0:T(4,128)(2,1)S(1)} %maximum_select_fusion.1), kind=kOutput, calls=%fused_computation.74 | convolution fusion | flops 1226833920 | bytes 23212032 | tf_op jit(solution)/shard_map/while/body/eval_jaxpr/hqk,khd->qhd/dot_general | solution.py:46
  210.0 10.2 %fusion.15 = f32[4,768]{1,0:T(4,128)} fusion(f32[4,768,1536]{2,1,0:T(8,128)} %get-tuple-element.224, f32[4,768]{1,0:T(4,128)} %copy-done.15, pred[768,1536]{1,0:T(8,128)(4,1)} %iota_compare_fusion.1), kind=kLoop, calls=%fused_computation.22 | loop fusion | flops 18871296 | bytes 20078592 | tf_op jit(solution)/shard_map/while/body/eval_jaxpr/reduce_sum | solution.py:45
  232.6 5.0 %broadcast_in_dim.403 = f32[4,384,512]{2,1,0:T(8,128)} reshape(f32[768,2,4,128]{3,2,1,0:T(4,128)} %broadcast_in_dim.402) | data formatting | bytes 6291456 | tf_op jit(solution)/shard_map/jit(_where)/broadcast_in_dim | solution.py:70
  237.6 6.2 %maximum_select_fusion.2 = bf16[1536,4,128]{2,1,0:T(4,128)(2,1)S(1)} fusion(bf16[768,4,128]{2,1,0:T(4,128)(2,1)} %maximum_select_fusion.6, bf16[768,4,128]{2,1,0:T(4,128)(2,1)} %collective-permute-done.3, pred[]{:T(512)S(6)} %eq.65), kind=kLoop, calls=%fused_computation.49 | loop fusion | flops 2359296 | bytes 3145729 | tf_op jit(solution)/shard_map/jit(_where)/select_n | solution.py:90
  246.2 7.1 %maximum_select_fusion.3 = bf16[1536,4,128]{2,1,0:T(4,128)(2,1)S(1)} fusion(bf16[768,4,128]{2,1,0:T(4,128)(2,1)} %maximum_select_fusion.7, bf16[768,4,128]{2,1,0:T(4,128)(2,1)} %collective-permute-done.5, pred[]{:T(512)S(6)} %eq.65), kind=kLoop, calls=%fused_computation.50 | loop fusion | flops 2359296 | bytes 3145729 | tf_op jit(solution)/shard_map/jit(_where)/select_n | solution.py:90
  262.8 6.5 %fusion.21 = f32[4,384]{1,0:T(4,128)S(1)} fusion(f32[4,384,1536]{2,1,0:T(8,128)} %copy-done.6, f32[4,384]{1,0:T(4,128)S(1)} %get-tuple-element.221, pred[384,1536]{1,0:T(8,128)(4,1)} %iota_compare_fusion.2), kind=kLoop, calls=%fused_computation.29 | loop fusion | flops 9435648 | bytes 10039296 | tf_op jit(solution)/shard_map/while/body/eval_jaxpr/reduce_sum | solution.py:45
  275.8 5.0 %broadcast_in_dim.416 = f32[4,384,512]{2,1,0:T(8,128)} reshape(f32[384,4,4,128]{3,2,1,0:T(4,128)} %broadcast_in_dim.415) | data formatting | bytes 6291456 | tf_op jit(solution)/shard_map/jit(_where)/broadcast_in_dim | solution.py:70
  280.9 6.0 %maximum_select_fusion.4 = bf16[1536,4,128]{2,1,0:T(4,128)(2,1)S(1)} fusion(bf16[768,4,128]{2,1,0:T(4,128)(2,1)} %maximum_select_fusion.8, bf16[768,4,128]{2,1,0:T(4,128)(2,1)} %collective-permute-done.8, pred[]{:T(512)S(6)} %eq.69), kind=kLoop, calls=%fused_computation.51 | loop fusion | flops 2359296 | bytes 3145729 | tf_op jit(solution)/shard_map/jit(_where)/select_n | solution.py:90
  290.2 5.8 %maximum_select_fusion.5 = bf16[1536,4,128]{2,1,0:T(4,128)(2,1)S(1)} fusion(bf16[768,4,128]{2,1,0:T(4,128)(2,1)} %maximum_select_fusion.9, bf16[768,4,128]{2,1,0:T(4,128)(2,1)} %collective-permute-done.11, pred[]{:T(512)S(6)} %eq.69), kind=kLoop, calls=%fused_computation.52 | loop fusion | flops 2359296 | bytes 3145729 | tf_op jit(solution)/shard_map/jit(_where)/select_n | solution.py:90
  323.4 5.1 %mul.164 = f32[4,384,512]{2,1,0:T(8,128)} reshape(f32[1536,4,128]{2,1,0:T(4,128)} %mul.163) | data formatting | bytes 6291456 | tf_op jit(solution)/shard_map/mul | solution.py:81
  332.7 5.1 %mul.161 = f32[4,384,512]{2,1,0:T(8,128)} reshape(f32[1536,4,128]{2,1,0:T(4,128)} %mul.160) | data formatting | bytes 6291456 | tf_op jit(solution)/shard_map/mul | solution.py:81
  342.1 5.0 %mul.156 = f32[4,384,512]{2,1,0:T(8,128)} reshape(f32[1536,4,128]{2,1,0:T(4,128)} %mul.155) | data formatting | bytes 6291456 | tf_op jit(solution)/shard_map/mul | solution.py:81
  351.4 5.3 %mul.153 = f32[4,384,512]{2,1,0:T(8,128)} reshape(f32[1536,4,128]{2,1,0:T(4,128)} %mul.152) | data formatting | bytes 6291456 | tf_op jit(solution)/shard_map/mul | solution.py:81
  361.0 5.0 %mul.148 = f32[4,384,512]{2,1,0:T(8,128)} reshape(f32[1536,4,128]{2,1,0:T(4,128)} %mul.147) | data formatting | bytes 6291456 | tf_op jit(solution)/shard_map/mul | solution.py:81
  370.3 5.0 %mul.145 = f32[4,384,512]{2,1,0:T(8,128)} reshape(f32[1536,4,128]{2,1,0:T(4,128)} %mul.144) | data formatting | bytes 6291456 | tf_op jit(solution)/shard_map/mul | solution.py:81
  379.5 5.0 %div.38 = f32[4,384,512]{2,1,0:T(8,128)} reshape(f32[1536,4,128]{2,1,0:T(4,128)} %div.37) | data formatting | bytes 6291456 | tf_op jit(solution)/shard_map/div | solution.py:137
  386.5 11.3 %divide_convert_fusion = bf16[4,384,512]{2,1,0:T(8,128)(2,1)S(1)} fusion(f32[4,384,512]{2,1,0:T(8,128)} %div.38, f32[4,384,512]{2,1,0:T(8,128)} %mul.164, pred[4,384,512]{2,1,0:T(8,128)(4,1)} %broadcast_in_dim.426, f32[4,384,512]{2,1,0:T(8,128)S(1)} %bitcast.87, f32[4,384,512]{2,1,0:T(8,128)} %mul.161, f32[4,384,512]{2,1,0:T(8,128)} %mul.156, ...), kind=kLoop, calls=%fused_computation.39 | loop fusion | flops 11010048 | bytes 38535168 | tf_op jit(solution)/shard_map/convert_element_type | solution.py:138
  397.8 23.1 %all_to_all.16 = bf16[4,384,512]{2,1,0:T(8,128)(2,1)S(1)} all-to-all(bf16[4,384,512]{2,1,0:T(8,128)(2,1)S(1)} %divide_convert_fusion), channel_id=1, replica_groups=mesh['ctx'=8,'head'=4] {'head'}, dimensions={0} | all-to-all | bytes 3145728 | tf_op jit(solution)/shard_map/all_to_all | solution.py:141
  421.8 8.0 %convolution_convert_fusion = bf16[384,2048]{1,0:T(8,128)(2,1)} fusion(bf16[384,2048]{0,1:T(8,128)(2,1)S(1)} %bitcast.93, bf16[2048,2048]{1,0:T(8,128)(2,1)} %param.11), kind=kOutput, calls=%fused_computation.40 | convolution fusion | flops 3222011904 | bytes 11534336 | tf_op jit(solution)/shard_map/dot_general | solution.py:142
  (167 shorter events, 201.2 us)
Async XLA Ops:
  0.0 0.7 copy-start
  0.0 10.6 %copy-start.2 = (bf16[1536,512]{1,0:T(8,128)(2,1)S(1)}, bf16[1536,512]{1,0:T(8,128)(2,1)}, u32[]{:S(2)}) copy-start(bf16[1536,512]{1,0:T(8,128)(2,1)} %param.7) | copy-start | bytes 4718596
  0.8 11.9 %copy-start.3 = (bf16[1536,512]{1,0:T(8,128)(2,1)S(1)}, bf16[1536,512]{1,0:T(8,128)(2,1)}, u32[]{:S(2)}) copy-start(bf16[1536,512]{1,0:T(8,128)(2,1)} %param.8) | copy-start | bytes 4718596
  7.6 123.6 %collective-permute-start.9 = (bf16[192,4,128]{2,1,0:T(4,128)(2,1)}, bf16[192,4,128]{2,1,0:T(4,128)(2,1)}, u32[]{:S(2)}, u32[]{:S(2)}) collective-permute-start(bf16[192,4,128]{2,1,0:T(4,128)(2,1)} %get-tuple-element.186), channel_id=1, source_target_pairs={{0,4},{4,0},{8,12},{12,8},{16,20},{20,16},{24,28},{28,24},{1,5},{5... | collective-permute-start | bytes 589832 | tf_op jit(solution)/shard_map/ppermute | solution.py:18
  10.6 122.5 %collective-permute-start.6 = (bf16[192,4,128]{2,1,0:T(4,128)(2,1)}, bf16[192,4,128]{2,1,0:T(4,128)(2,1)}, u32[]{:S(2)}, u32[]{:S(2)}) collective-permute-start(bf16[192,4,128]{2,1,0:T(4,128)(2,1)} %get-tuple-element.187), channel_id=1, source_target_pairs={{0,4},{4,0},{8,12},{12,8},{16,20},{20,16},{24,28},{28,24},{1,5},{5... | collective-permute-start | bytes 589832 | tf_op jit(solution)/shard_map/ppermute | solution.py:18
  26.1 164.0 %collective-permute-start.1 = (bf16[768,4,128]{2,1,0:T(4,128)(2,1)}, bf16[768,4,128]{2,1,0:T(4,128)(2,1)}, u32[]{:S(2)}, u32[]{:S(2)}) collective-permute-start(bf16[768,4,128]{2,1,0:T(4,128)(2,1)} %get-tuple-element.180), channel_id=1, source_target_pairs={{0,4},{4,0},{8,12},{12,8},{16,20},{20,16},{24,28},{28,24},{1,5},{5... | collective-permute-start | bytes 2359304 | tf_op jit(solution)/shard_map/ppermute | solution.py:18
  28.1 146.3 %collective-permute-start = (bf16[768,4,128]{2,1,0:T(4,128)(2,1)}, bf16[768,4,128]{2,1,0:T(4,128)(2,1)}, u32[]{:S(2)}, u32[]{:S(2)}) collective-permute-start(bf16[768,4,128]{2,1,0:T(4,128)(2,1)} %get-tuple-element.181), channel_id=1, source_target_pairs={{0,4},{4,0},{8,12},{12,8},{16,20},{20,16},{24,28},{28,24},{1,5},{5... | collective-permute-start | bytes 2359304 | tf_op jit(solution)/shard_map/ppermute | solution.py:18
  42.6 94.2 %collective-permute-start.2 = (bf16[384,4,128]{2,1,0:T(4,128)(2,1)}, bf16[384,4,128]{2,1,0:T(4,128)(2,1)}, u32[]{:S(2)}, u32[]{:S(2)}) collective-permute-start(bf16[384,4,128]{2,1,0:T(4,128)(2,1)} %get-tuple-element.184), channel_id=1, source_target_pairs={{0,4},{4,0},{8,12},{12,8},{16,20},{20,16},{24,28},{28,24},{1,5},{5... | collective-permute-start | bytes 1179656 | tf_op jit(solution)/shard_map/ppermute | solution.py:18
  46.4 1.6 copy-start.4
  102.9 18.3 %copy-start.16 = (f32[3,512,4]{1,2,0:T(4,128)}, f32[3,512,4]{1,2,0:T(4,128)S(1)}, u32[]{:S(2)}) copy-start(f32[3,512,4]{1,2,0:T(4,128)S(1)} %get-tuple-element.116) | copy-start | bytes 73732
  106.8 0.6 copy-start.14
  127.9 3.4 copy-start.9
  131.3 9.5 %collective-permute-start.4 = (bf16[384,4,128]{2,1,0:T(4,128)(2,1)S(1)}, bf16[384,4,128]{2,1,0:T(4,128)(2,1)S(1)}, u32[]{:S(2)}, u32[]{:S(2)}) collective-permute-start(bf16[384,4,128]{2,1,0:T(4,128)(2,1)S(1)} %copy-done.9), channel_id=1, source_target_pairs={{0,4},{4,0},{8,12},{12,8},{16,20},{20,16},{24,28},{28,24},{1,5},{5... | collective-permute-start | bytes 1179656 | tf_op jit(solution)/shard_map/ppermute | solution.py:18
  133.1 12.1 %collective-permute-start.10 = (bf16[384,4,128]{2,1,0:T(4,128)(2,1)S(1)}, bf16[384,4,128]{2,1,0:T(4,128)(2,1)S(1)}, u32[]{:S(2)}, u32[]{:S(2)}) collective-permute-start(bf16[384,4,128]{2,1,0:T(4,128)(2,1)S(1)} %maximum_select_fusion.11), channel_id=1, source_target_pairs={{0,8},{4,12},{8,0},{12,4},{16,24},{20,28},{24,16},{28,20},{1,9},{5... | collective-permute-start | bytes 1179656 | tf_op jit(solution)/shard_map/ppermute | solution.py:18
  136.8 33.6 %collective-permute-start.7 = (bf16[384,4,128]{2,1,0:T(4,128)(2,1)S(1)}, bf16[384,4,128]{2,1,0:T(4,128)(2,1)S(1)}, u32[]{:S(2)}, u32[]{:S(2)}) collective-permute-start(bf16[384,4,128]{2,1,0:T(4,128)(2,1)S(1)} %maximum_select_fusion.10), channel_id=1, source_target_pairs={{0,8},{4,12},{8,0},{12,4},{16,24},{20,28},{24,16},{28,20},{1,9},{5... | collective-permute-start | bytes 1179656 | tf_op jit(solution)/shard_map/ppermute | solution.py:18
  140.8 96.8 %collective-permute-start.3 = (bf16[768,4,128]{2,1,0:T(4,128)(2,1)}, bf16[768,4,128]{2,1,0:T(4,128)(2,1)}, u32[]{:S(2)}, u32[]{:S(2)}) collective-permute-start(bf16[768,4,128]{2,1,0:T(4,128)(2,1)} %maximum_select_fusion.6), channel_id=1, source_target_pairs={{0,8},{4,12},{8,0},{12,4},{16,24},{20,28},{24,16},{28,20},{1,9},{5... | collective-permute-start | bytes 2359304 | tf_op jit(solution)/shard_map/ppermute | solution.py:18
  144.1 36.9 %copy-start.7 = (pred[768,1536]{1,0:T(8,128)(4,1)S(1)}, pred[768,1536]{1,0:T(8,128)(4,1)}, u32[]{:S(2)}) copy-start(pred[768,1536]{1,0:T(8,128)(4,1)} %iota_compare_fusion.1) | copy-start | bytes 3538948
  144.1 36.9 %copy-start.11 = (bf16[768,4,128]{2,1,0:T(4,128)(2,1)S(1)}, bf16[768,4,128]{2,1,0:T(4,128)(2,1)}, u32[]{:S(2)}) copy-start(bf16[768,4,128]{2,1,0:T(4,128)(2,1)} %get-tuple-element.182) | copy-start | bytes 2359300
  145.2 101.0 %collective-permute-start.5 = (bf16[768,4,128]{2,1,0:T(4,128)(2,1)}, bf16[768,4,128]{2,1,0:T(4,128)(2,1)}, u32[]{:S(2)}, u32[]{:S(2)}) collective-permute-start(bf16[768,4,128]{2,1,0:T(4,128)(2,1)} %maximum_select_fusion.7), channel_id=1, source_target_pairs={{0,8},{4,12},{8,0},{12,4},{16,24},{20,28},{24,16},{28,20},{1,9},{5... | collective-permute-start | bytes 2359304 | tf_op jit(solution)/shard_map/ppermute | solution.py:18
  170.5 119.7 %collective-permute-start.11 = (bf16[768,4,128]{2,1,0:T(4,128)(2,1)}, bf16[768,4,128]{2,1,0:T(4,128)(2,1)}, u32[]{:S(2)}, u32[]{:S(2)}) collective-permute-start(bf16[768,4,128]{2,1,0:T(4,128)(2,1)} %maximum_select_fusion.9), channel_id=1, source_target_pairs={{0,16},{4,20},{8,24},{12,28},{16,0},{20,4},{24,8},{28,12},{1,17},{... | collective-permute-start | bytes 2359304 | tf_op jit(solution)/shard_map/ppermute | solution.py:18
  174.4 106.4 %collective-permute-start.8 = (bf16[768,4,128]{2,1,0:T(4,128)(2,1)}, bf16[768,4,128]{2,1,0:T(4,128)(2,1)}, u32[]{:S(2)}, u32[]{:S(2)}) collective-permute-start(bf16[768,4,128]{2,1,0:T(4,128)(2,1)} %maximum_select_fusion.8), channel_id=1, source_target_pairs={{0,16},{4,20},{8,24},{12,28},{16,0},{20,4},{24,8},{28,12},{1,17},{... | collective-permute-start | bytes 2359304 | tf_op jit(solution)/shard_map/ppermute | solution.py:18
  190.1 16.4 %copy-start.15 = (f32[4,768]{1,0:T(4,128)}, f32[4,768]{1,0:T(4,128)S(1)}, u32[]{:S(2)}) copy-start(f32[4,768]{1,0:T(4,128)S(1)} %get-tuple-element.223) | copy-start | bytes 36868
  237.6 6.2 %copy-start.8 = (pred[384,1536]{1,0:T(8,128)(4,1)S(1)}, pred[384,1536]{1,0:T(8,128)(4,1)}, u32[]{:S(2)}) copy-start(pred[384,1536]{1,0:T(8,128)(4,1)} %iota_compare_fusion.2) | copy-start | bytes 1769476
  237.6 6.2 %copy-start.12 = (bf16[384,4,128]{2,1,0:T(4,128)(2,1)S(1)}, bf16[384,4,128]{2,1,0:T(4,128)(2,1)}, u32[]{:S(2)}) copy-start(bf16[384,4,128]{2,1,0:T(4,128)(2,1)} %get-tuple-element.185) | copy-start | bytes 1179652
  246.2 7.2 %copy-start.6 = (f32[4,384,1536]{2,1,0:T(8,128)}, f32[4,384,1536]{2,1,0:T(8,128)S(1)}, u32[]{:S(2)}) copy-start(f32[4,384,1536]{2,1,0:T(8,128)S(1)} %get-tuple-element.222) | copy-start | bytes 28311556
  280.8 6.1 %copy-start.10 = (pred[192,1536]{1,0:T(8,128)(4,1)S(1)}, pred[192,1536]{1,0:T(8,128)(4,1)}, u32[]{:S(2)}) copy-start(pred[192,1536]{1,0:T(8,128)(4,1)} %iota_compare_fusion.3) | copy-start | bytes 884740
  280.8 6.1 %copy-start.13 = (bf16[192,4,128]{2,1,0:T(4,128)(2,1)S(1)}, bf16[192,4,128]{2,1,0:T(4,128)(2,1)}, u32[]{:S(2)}) copy-start(bf16[192,4,128]{2,1,0:T(4,128)(2,1)} %get-tuple-element.188) | copy-start | bytes 589828
  384.6 1.9 copy-start.5
  421.8 8.0 %copy-start.1 = (s32[3,16]{1,0:T(4,128)S(1)}, s32[3,16]{1,0:T(4,128)}, u32[]{:S(2)}) copy-start(s32[3,16]{1,0:T(4,128)} %param.10) | copy-start | bytes 580
where the time goes:
time: 436 us; the launch traced here: 430 us
  local copies, waits for them, and re-layouts  190 us (44%)
  other arithmetic  118 us (27%)
  matrix products  58.9 us (14%)
  waiting for transfers between devices  23.3 us (5%)
  blocking collectives  23.1 us (5%)
  starting transfers between devices  15.8 us (4%)
    select_n x12, other arithmetic, join_pair(): jnp.where(upper, jnp.concatenate([other_part, mine_part], 0), jnp.concate...  48.4 us
    reduce_sum x6, other arithmetic, one_block(): row_sum = jnp.sum(weights, axis=2)  29.5 us
    dot_general x6, matrix products, one_block(): jnp.einsum('hqk,khd->qhd', weights.astype(jnp.bfloat16), value_rows, pref...  29.5 us
    mul x6, local copies, waits for them, and re-layouts, merge_levels(): running[2] * old_scale[:, :, None] + fresh[2] * new_scale[:, :, None]  28.2 us
    mul x6, local copies, waits for them, and re-layouts, merge_levels(): fresh[2] * new_scale[:, :, None]  28 us
    ppermute x12, waiting for transfers between devices, swapped(): return lax.ppermute(value, axis, pairs)  23.3 us
    all_to_all x1, blocking collectives, body(): lax.all_to_all(attended, 'head', split_axis=0, concat_axis=1, tiled=True)  23.1 us
    reduce_sum x3, other arithmetic, pick_rows(): jnp.sum(jnp.where(hits[None, :, :, None], shaped, jnp.zeros((), source.dt...  21.6 us
  transfers between devices with their start and end apart: 12, of which 3 were waited for; matrix products, arithmetic and copies ran while one was open for 56% of the time, Pallas kernels for 0%

commit v1 on v0

v1 whole, which is shorter than its diff:
```python
import functools
import math

import jax
import jax.numpy as jnp
from jax import lax
from jax.experimental import pallas as pl
from jax.experimental.pallas import tpu as pltpu
from jax.sharding import PartitionSpec as P

DH = 128
RES = 8
SUB = 16
BLK = RES * SUB
NEG = -1e30
RATE = math.log2(math.e) / math.sqrt(DH)
BF16 = jnp.bfloat16
F32 = jnp.float32
VMEM_LIMIT = 48 * 1024 * 1024


def iota(shape, dim):
    return lax.broadcasted_iota(jnp.int32, shape, dim)


def regroup_matrix(inverse):
    row, col = iota((BLK, BLK), 0), iota((BLK, BLK), 1)
    if inverse:
        hit = col == (row % RES) * SUB + row // RES
    else:
        hit = col == (row % SUB) * RES + row // SUB
    return jnp.where(hit, 1.0, 0.0).astype(BF16)


def causal_bias(position, size):
    rows = position(iota((size, size), 0))
    cols = position(iota((size, size), 1))
    return jnp.where(cols <= rows, 0.0, NEG)


def attend(q, blocks):
    scores, top = [], None
    for k, _, bias in blocks:
        s = lax.dot_general(q, k, (((1,), (1,)), ((), ())), preferred_element_type=F32)
        if bias is not None:
            s = s + bias
        scores.append(s)
    if all(s.shape == scores[0].shape for s in scores):
        wide = scores[0]
        for s in scores[1:]:
            wide = jnp.maximum(wide, s)
        top = jnp.max(wide, axis=1, keepdims=True)
    else:
        for s in scores:
            m = jnp.max(s, axis=1, keepdims=True)
            top = m if top is None else jnp.maximum(top, m)
    total = None
    for s, (_, v, _) in zip(scores, blocks):
        p = jnp.exp2((s - top) * RATE).astype(BF16)
        with_ones = jnp.concatenate([v, jnp.ones(v.shape, BF16)], axis=1)
        part = jnp.dot(p, with_ones, preferred_element_type=F32)
        total = part if total is None else total + part
    row_sum = total[:, DH:]
    return total[:, :DH] / row_sum, top * RATE + jnp.log2(row_sum)


def merge(parts):
    top = parts[0][1]
    for _, lse in parts[1:]:
        top = jnp.maximum(top, lse)
    out, weight = 0.0, 0.0
    for o, lse in parts:
        w = jnp.exp2(lse - top)
        out += o * w
        weight += w
    return out / weight, top + jnp.log2(weight)


def rows_of(ref, level, shift, first=0, count=None):
    count = ref.shape[0] - first if count is None else count
    return [
        ref[pl.ds(first, count), shift + j * 2**level].reshape(count * SUB, DH)
        for j in range(RES // 2**level)
    ]


def prep_kernel(off_ref, q_ref, k_ref, v_ref, qt, kt, vt, *sends):
    groups = len(sends) // 4
    heads = qt.shape[0]
    blocks = qt.shape[1]
    first = lax.axis_index("head") * heads
    turn = regroup_matrix(False)
    for src, dst in ((q_ref, qt), (k_ref, kt), (v_ref, vt)):
        for b in range(blocks):
            x = jnp.dot(turn, src[b * BLK : (b + 1) * BLK, :], preferred_element_type=F32)
            x = x.astype(BF16)
            for h in range(heads):
                dst[h, b] = x[:, h * DH : (h + 1) * DH].reshape(RES, SUB, DH)
    per = heads // groups
    for g in range(groups):
        q1, q23, kv2, kv3 = sends[4 * g : 4 * g + 4]
        for n in range(per):
            h = g * per + n
            o1, o2, o3 = (off_ref[lv, first + h] for lv in range(3))
            for j, x in enumerate(rows_of(qt.at[h], 1, o1)):
                q1[n, j] = x
            for j, x in enumerate(rows_of(qt.at[h], 2, o2) + rows_of(qt.at[h], 3, o3)):
                q23[n, j] = x
            for i, src in enumerate((kt, vt)):
                for j, x in enumerate(rows_of(src.at[h], 2, o2)):
                    kv2[n, i, j] = x
                kv3[n, i] = rows_of(src.at[h], 3, o3)[0]


def own_kernel(first_head, off_ref, qt, kt, vt, out, lse):
    qt, kt, vt, out, lse = (r.at[0] for r in (qt, kt, vt, out, lse))
    blocks = qt.shape[0]
    head = lax.axis_index("head") * HEADS_HERE + first_head + pl.program_id(0)
    step = 2
    size = step * BLK
    bias = causal_bias(lambda r: r // BLK * BLK + r % SUB * RES + r % BLK // SUB, size)
    load = lambda ref, n: ref[n * step : (n + 1) * step].reshape(size, DH)
    for n in range(blocks // step):
        parts = [
            (load(kt, i), load(vt, i), bias if i == n else None) for i in range(n + 1)
        ]
        o, s = attend(load(qt, n), parts)
        out[n * step : (n + 1) * step] = o.reshape(step, RES, SUB, DH)
        lse[n * step : (n + 1) * step] = s.reshape(step, RES, SUB, DH)
    shift = off_ref[0, head]
    step = 4
    rows = step * SUB
    slices = RES // 2
    size = rows * slices
    bias = causal_bias(lambda r: r % rows * slices + r // rows, size)
    load = lambda ref, n: jnp.concatenate(rows_of(ref, 1, shift, n * step, step), axis=0)
    for n in range(blocks // step):
        parts = [
            (load(kt, i), load(vt, i), bias if i == n else None) for i in range(n + 1)
        ]
        o, s = attend(load(qt, n), parts)
        o, s = merge([(o, s), (load(out, n), load(lse, n))])
        for j in range(slices):
            at = (pl.ds(n * step, step), shift + 2 * j)
            out[at] = o[j * rows : (j + 1) * rows].reshape(step, SUB, DH)
            lse[at] = s[j * rows : (j + 1) * rows].reshape(step, SUB, DH)


def put_stat(slab, stat, place):
    lane = iota(stat.shape, 1)
    rest = stat
    now = slab[...]
    for i in range(3):
        piece = rest.astype(BF16)
        rest = rest - piece.astype(F32)
        now = jnp.where(lane == place + 32 * i, piece, now)
    slab[...] = now


def get_stat(slab, place):
    lane = iota(slab.shape, 1)
    hit = (lane == place) | (lane == place + 32) | (lane == place + 64)
    return jnp.sum(jnp.where(hit, slab[...].astype(F32), 0.0), axis=1, keepdims=True)


def lower_kernel(first_head, off_ref, q1, kt, vt, msg):
    here = pl.program_id(0)
    head = lax.axis_index("head") * HEADS_HERE + first_head + here

    @pl.when(here == 0)
    def _():
        msg[msg.shape[0] - 1] = jnp.zeros(msg.shape[1:], BF16)

    @pl.when(lax.axis_index("ctx") % 2 == 0)
    def _():
        shift = off_ref[0, head]
        count = RES // 2
        k = jnp.concatenate(rows_of(kt.at[0], 1, shift), axis=0)
        v = jnp.concatenate(rows_of(vt.at[0], 1, shift), axis=0)
        rows = q1.shape[2]
        for pair in range(count // 2):
            q = q1[0, 2 * pair : 2 * pair + 2].reshape(2 * rows, DH)
            o, s = attend(q, [(k, v, None)])
            for i in range(2):
                j = 2 * pair + i
                place = here * count + j
                msg[place] = o[i * rows : (i + 1) * rows].astype(BF16)
                put_stat(msg.at[msg.shape[0] - 1], s[i * rows : (i + 1) * rows], place)


def level_kernel(level, first_head, off_ref, qt, kt, vt, q23, before, out, lse, msg):
    here = pl.program_id(0)
    head = lax.axis_index("head") * HEADS_HERE + first_head + here
    ctx = lax.axis_index("ctx")
    shift = off_ref[level - 1, head]
    count = RES // 2**level
    rows = q23.shape[2]
    size = count * rows

    @pl.when(here == 0)
    def _():
        msg[msg.shape[0] - 1] = jnp.zeros(msg.shape[1:], BF16)

    def whole(ref):
        return jnp.concatenate(rows_of(ref.at[0], level, shift), axis=0)

    own_k, own_v = whole(kt), whole(vt)
    base = 0 if level == 2 else 2
    past = []
    if level == 2:
        allowed = ctx // 2 % 2 == 1
        past.append(
            (
                before[0, 0].reshape(size, DH),
                before[0, 1].reshape(size, DH),
                jnp.where(allowed, 0.0, NEG),
            )
        )
    else:
        for z in range(before.shape[0] - 1):
            past.append((before[z, 0, 0], before[z, 0, 1], jnp.where(z < ctx // 2 % 4, 0.0, NEG)))
    triangle = causal_bias(lambda r: r % rows * count + r // rows, size)
    o, s = attend(whole(qt), past + [(own_k, own_v, triangle)])
    for j in range(count):
        out[0, j] = o[j * rows : (j + 1) * rows]
        lse[0, j] = s[j * rows : (j + 1) * rows]
    later = jnp.where(ctx % 2 == 0, 0.0, NEG)
    q = q23[0, base : base + count].reshape(size, DH)
    o, s = attend(q, past + [(own_k, own_v, later)])
    for j in range(count):
        place = here * count + j
        msg[place] = o[j * rows : (j + 1) * rows].astype(BF16)
        put_stat(msg.at[msg.shape[0] - 1], s[j * rows : (j + 1) * rows], place)


def merge_kernel(
    first_head, off_ref, o0, s0, o2, s2, o3, s3, m1, m2, m3, dest0, dest1, dest2, dest3, acc, sums
):
    here = pl.program_id(0)
    head = lax.axis_index("head") * HEADS_HERE + first_head + here
    ctx = lax.axis_index("ctx")
    blocks, rows = o0.shape[1], o0.shape[1] * SUB
    shifts = [off_ref[lv, head] for lv in range(3)]
    acc[...] = o0[0]
    sums[...] = s0[0]
    for level, msg, own in ((1, m1, None), (2, m2, (o2, s2)), (3, m3, (o3, s3))):
        count = RES // 2**level
        slab = msg.at[msg.shape[0] - 1]
        for j in range(count):
            at = shifts[level - 1] + j * 2**level
            place = here * count + j
            stat = get_stat(slab, place)
            if level == 1:
                stat = jnp.where(ctx % 2 == 1, stat, NEG)
            parts = [
                (acc[:, at].reshape(rows, DH), sums[:, at].reshape(rows, DH)),
                (msg[place].astype(F32), jnp.broadcast_to(stat, (rows, DH))),
            ]
            if own is not None:
                parts.append((own[0][0, j], own[1][0, j]))
            o, s = merge(parts)
            acc[:, at] = o.reshape(blocks, SUB, DH)
            sums[:, at] = s.reshape(blocks, SUB, DH)
    mine = lax.axis_index("head")
    per = blocks // 4
    for t, dest in enumerate((dest0, dest1, dest2, dest3)):
        at = (mine ^ t) * per
        dest[...] = acc[pl.ds(at, per)].reshape(per * BLK, DH).astype(BF16)


def project_kernel(a0, a1, a2, a3, w_ref, out, plain):
    size = a0.shape[1]

    @pl.when(pl.program_id(0) == 0)
    def _():
        back = regroup_matrix(True)
        for t, src in enumerate((a0, a1, a2, a3)):
            for b in range(src.shape[0] // BLK):
                at = slice(b * BLK, (b + 1) * BLK)
                x = jnp.dot(back, src[at, :], preferred_element_type=F32)
                plain[at, t * size : (t + 1) * size] = x.astype(BF16)

    mine = lax.axis_index("head")
    total = None
    for t in range(4):
        w = w_ref[pl.ds(pl.multiple_of((mine ^ t) * size, size), size), :]
        part = jnp.dot(
            plain[:, t * size : (t + 1) * size], w, preferred_element_type=F32
        )
        total = part if total is None else total + part
    out[...] = total.astype(BF16)


HEADS_HERE = 4
SMEM = pl.BlockSpec(memory_space=pltpu.SMEM)


def shape(*dims, dtype=BF16):
    return jax.ShapeDtypeStruct(dims, dtype)


def per_head(array):
    rest = array.shape[1:]
    return pl.BlockSpec((1, *rest), lambda h, n=len(rest): (h,) + (0,) * n)


def from_head(array, first):
    rest = array.shape[1:]
    return pl.BlockSpec((1, *rest), lambda h, n=len(rest): (h + first,) + (0,) * n)


def whole(array):
    return pl.BlockSpec(array.shape, lambda h, n=len(array.shape): (0,) * n)


def params():
    return pltpu.CompilerParams(vmem_limit_bytes=VMEM_LIMIT)


def cost(macs, moved):
    return pl.CostEstimate(flops=2 * macs, bytes_accessed=moved, transcendentals=0)


GROUPS = 1


def body(queries, keys, values, offsets, out_weight):
    rows_here, width = queries.shape
    blocks = rows_here // BLK
    heads = width // DH
    per = heads // GROUPS
    slots = rows_here // RES
    regrouped = shape(heads, blocks, RES, SUB, DH)
    sends = []
    for _ in range(GROUPS):
        sends += [
            shape(per, 4, slots, DH),
            shape(per, 3, slots, DH),
            shape(per, 2, 2, slots, DH),
            shape(per, 2, slots, DH),
        ]
    vmem = pl.BlockSpec(memory_space=pltpu.VMEM)
    qt, kt, vt, *sends = pl.pallas_call(
        prep_kernel,
        in_specs=[SMEM, vmem, vmem, vmem],
        out_specs=[vmem] * (3 + 4 * GROUPS),
        out_shape=[regrouped] * 3 + sends,
        compiler_params=params(),
        cost_estimate=cost(3 * rows_here * BLK * width, 12 * 2**20),
        name="prep",
    )(offsets, queries, keys, values)

    ctx_size = lax.axis_size("ctx")
    swap = [(i, i ^ 1) for i in range(ctx_size)]
    down = [(i + 1, i) for i in range(0, ctx_size, 2)]
    up = [(i, i + 1) for i in range(0, ctx_size, 2)]
    column2 = [(i, i + 2) for i in range(ctx_size) if i // 2 % 2 == 0]
    column4 = [
        [s + y + 2 * z for z in range(4)] for s in range(0, ctx_size, 8) for y in range(2)
    ]
    pieces = []
    for g in range(GROUPS):
        q1, q23, kv2, kv3 = sends[4 * g : 4 * g + 4]
        first = g * per
        q1 = lax.ppermute(q1, "ctx", down)
        q23 = lax.ppermute(q23, "ctx", swap)
        kv2 = lax.ppermute(kv2, "ctx", column2)
        kv3 = lax.all_gather(kv3, "ctx", axis_index_groups=column4)
        o0, s0 = pl.pallas_call(
            functools.partial(own_kernel, first),
            grid=(per,),
            in_specs=[SMEM] + [from_head(x, first) for x in (qt, kt, vt)],
            out_specs=[per_head(shape(per, blocks, RES, SUB, DH))] * 2,
            out_shape=[shape(per, blocks, RES, SUB, DH, dtype=F32)] * 2,
            compiler_params=params(),
            cost_estimate=cost(per * 6 * 2**28, 10 * 2**20),
            name="own",
        )(offsets, qt, kt, vt)
        msg1 = shape(per * 4 + 1, slots, DH)
        m1 = pl.pallas_call(
            functools.partial(lower_kernel, first),
            grid=(per,),
            in_specs=[SMEM, per_head(q1)] + [from_head(x, first) for x in (kt, vt)],
            out_specs=whole(msg1),
            out_shape=msg1,
            compiler_params=params(),
            cost_estimate=cost(per * 3 * 2**28, 4 * 2**20),
            name="lower",
        )(offsets, q1, kt, vt)
        m1 = lax.ppermute(m1, "ctx", up)
        levels = []
        for level, before in ((2, kv2), (3, kv3)):
            count = RES // 2**level
            own = shape(per, count, slots, DH, dtype=F32)
            msg = shape(per * count + 1, slots, DH)
            if level == 2:
                spec = per_head(before)
            else:
                spec = pl.BlockSpec(
                    (before.shape[0], 1, *before.shape[2:]), lambda h: (0, h, 0, 0, 0)
                )
            o, s, m = pl.pallas_call(
                functools.partial(level_kernel, level, first),
                grid=(per,),
                in_specs=[SMEM]
                + [from_head(x, first) for x in (qt, kt, vt)]
                + [per_head(q23), spec],
                out_specs=[per_head(own)] * 2 + [whole(msg)],
                out_shape=[own, own, msg],
                compiler_params=params(),
                cost_estimate=cost(per * 3 * 2**27, 4 * 2**20),
                name="level%d" % level,
            )(offsets, qt, kt, vt, q23, before)
            levels.append((o, s, lax.ppermute(m, "ctx", swap)))
        (o2, s2, m2), (o3, s3, m3) = levels
        dest = shape(rows_here // 4, per * DH)
        pieces.append(
            pl.pallas_call(
                functools.partial(merge_kernel, first),
                grid=(per,),
                in_specs=[SMEM]
                + [per_head(x) for x in (o0, s0, o2, s2, o3, s3)]
                + [whole(x) for x in (m1, m2, m3)],
                out_specs=[pl.BlockSpec((rows_here // 4, DH), lambda h: (0, h))] * 4,
                out_shape=[dest] * 4,
                scratch_shapes=[pltpu.VMEM((blocks, RES, SUB, DH), F32)] * 2,
                compiler_params=params(),
                cost_estimate=cost(2**28, 10 * 2**20),
                name="merge",
            )(offsets, o0, s0, o2, s2, o3, s3, m1, m2, m3)
        )
    if GROUPS == 1:
        parts = list(pieces[0])
        for t in range(1, 4):
            parts[t] = lax.ppermute(parts[t], "head", [(i, i ^ t) for i in range(4)])
    model = out_weight.shape[1]
    tile = 512
    return pl.pallas_call(
        project_kernel,
        grid=(model // tile,),
        in_specs=[whole(parts[0])] * 4
        + [pl.BlockSpec((out_weight.shape[0], tile), lambda n: (0, n))],
        out_specs=pl.BlockSpec((rows_here // 4, tile), lambda n: (0, n)),
        out_shape=shape(rows_here // 4, model),
        scratch_shapes=[pltpu.VMEM((rows_here // 4, out_weight.shape[0]), BF16)],
        compiler_params=params(),
        cost_estimate=cost(rows_here // 4 * 2048 * 2048, 12 * 2**20),
        name="project",
    )(*parts, out_weight)


def solution(mesh):
    placed = (P("ctx", "head"), P("ctx", "head"), P("ctx", "head"), P(), P())
    return jax.shard_map(
        body, mesh=mesh, in_specs=placed, out_specs=P(("ctx", "head"), None), check_vma=False
    )
```

time: 436 us -> 144 us (0.33)
  the two profiles are of different devices: /device:TPU:0 before, /device:TPU:31 now
where the time goes in v1:
time: 144 us
  waiting for transfers between devices  55.3 us (38%)
  Pallas kernels  48.9 us (34%)
  starting transfers between devices  18.9 us (13%)
  between operations  13.5 us (9%)
  local copies, waits for them, and re-layouts  7.23 us (5%)
    ppermute x1, waiting for transfers between devices, body(): kv2 = lax.ppermute(kv2, 'ctx', column2)  26.8 us
    ppermute x3, waiting for transfers between devices, body(): parts[t] = lax.ppermute(parts[t], 'head', [(i, i ^ t) for i in range(4)])  17.6 us
    pallas_call x1, Pallas kernels, body(): pl.pallas_call(functools.partial(own_kernel, first), grid=(per,), in_spec...  16.5 us
    pallas_call x2, Pallas kernels, body(): pl.pallas_call(functools.partial(level_kernel, level, first), grid=(per,)...  12.8 us
    ppermute x1, waiting for transfers between devices, body(): q23 = lax.ppermute(q23, 'ctx', swap)  10.9 us
    pallas_call x1, Pallas kernels, body(): pl.pallas_call(project_kernel, grid=(model // tile,), in_specs=[whole(par...  7.76 us
    unnamed x20, local copies, waits for them, and re-layouts  7.23 us
    ppermute x2, starting transfers between devices, body(): levels.append((o, s, lax.ppermute(m, 'ctx', swap)))  6.65 us
  transfers between devices with their start and end apart: 10, of which 4 were waited for; matrix products, arithmetic and copies ran while one was open for 0% of the time, Pallas kernels for 22%

profile of v1, /device:TPU:31, one launch (start us, length us, event | category | flops | bytes accessed | tf_op | source)
XLA Modules:
  0.0 143.7 jit_solution(9699000424888562107)
XLA Ops:
  6.5 0.7 copy-done
  7.2 5.2 %prep.1 = (bf16[4,12,8,16,128]{4,3,2,1,0:T(8,128)(2,1)S(1)}, bf16[4,12,8,16,128]{4,3,2,1,0:T(8,128)(2,1)S(1)}, bf16[4,12,8,16,128]{4,3,2,1,0:T(8,128)(2,1)}, bf1...) custom-call(s32[3,16]{1,0:T(4,128)S(1)} %copy-done, ...), custom_call_target="tpu_custom_call" | custom-call | flops 603979776 | bytes 12582912 | tf_op jit(solution)/shard_map/prep/pallas_call | solution.py:343
  12.4 1.1 copy-done.2
  13.5 1.2 copy-done.5
  14.7 0.0 all-gather.3.cloned.1.call-update
  14.7 1.3 collective-permute-start.1
  16.0 0.3 collective-permute-start
  16.3 3.2 %collective-permute-start.2 = (bf16[4,4,192,128]{3,2,1,0:T(8,128)(2,1)S(1)}, bf16[4,4,192,128]{3,2,1,0:T(8,128)(2,1)S(1)}, u32[]{:S(2)}, u32[]{:S(2)}) collective-permute-start(bf16[4,4,192,128]{3,2,1,0:T(8,128)(2,1)S(1)} %get-tuple-element.36), channel_id=1, source_target_pairs={{4,0},{12,8},{20,16},{28,24},{5,1},{13,9},{21,17},{29,25},{6,2},{1... | collective-permute-start | bytes 2359304 | tf_op jit(solution)/shard_map/ppermute | solution.py:365
  19.5 10.9 %collective-permute-done.q23 = bf16[4,3,192,128]{3,2,1,0:T(8,128)(2,1)S(1)} collective-permute-done((bf16[4,3,192,128]{3,2,1,0:T(8,128)(2,1)S(1)}, bf16[4,3,192,128]{3,2,1,0:T(8,128)(2,1)S(1)}, u32[]{:S(2)}, u32[]{:S(2)}) %collective-permute-start) | collective-permute-done | bytes 589856 | tf_op jit(solution)/shard_map/ppermute | solution.py:366
  30.4 26.8 %collective-permute-done.1.before = bf16[4,2,2,192,128]{4,3,2,1,0:T(8,128)(2,1)S(1)} collective-permute-done((bf16[4,2,2,192,128]{4,3,2,1,0:T(8,128)(2,1)S(1)}, bf16[4,2,2,192,128]{4,3,2,1,0:T(8,128)(2,1)S(1)}, u32[]{:S(2)}, u32[]{:S(2)}) %collective-permute-start.1) | collective-permute-done | bytes 786464 | tf_op jit(solution)/shard_map/ppermute | solution.py:367
  57.2 1.4 copy-done.3
  58.6 7.4 %level2.1 = (f32[4,2,192,128]{3,2,1,0:T(8,128)S(1)}, f32[4,2,192,128]{3,2,1,0:T(8,128)S(1)}, bf16[9,192,128]{2,1,0:T(8,128)(2,1)}) custom-call(s32[3,16]{1,0:T(4,128)S(1)} %copy-done.1, bf16[4,12,8,16,128]{4,3,2,1,0:T(8,128)(2,1)S(1)} %copy-done.3, bf16[4,12,8,16,128]{4,3,2,1,0:T(8,128)(2,1)} %copy-done.5, ...), custom_call_target="tpu_custom_call" | custom-call | flops 3221225472 | bytes 4194304 | tf_op jit(solution)/shard_map/level2/pallas_call | solution.py:402
  66.0 0.2 collective-permute-start.4
  66.2 0.0 collective-permute-done.2.q1
  66.2 1.7 %lower.1 = bf16[17,192,128]{2,1,0:T(8,128)(2,1)} custom-call(s32[3,16]{1,0:T(4,128)S(1)} %copy-done.1, bf16[4,4,192,128]{3,2,1,0:T(8,128)(2,1)S(1)} %collective-permute-done.2.q1, bf16[4,12,8,16,128]{4,3,2,1,0:T(8,128)(2,1)S(1)} %copy-done.6, bf16[4,12,8,16,128]{4,3,2,1,0:T(8,128)(2,1)S(1)} %copy-done.8), custom_call_target="tpu_custom_call" | custom-call | flops 6442450944 | bytes 4194304 | tf_op jit(solution)/shard_map/lower/pallas_call | solution.py:380
  67.9 1.3 collective-permute-start.3
  69.2 0.0 all-gather.3.cloned.1.call-done
  69.2 1.4 copy-done.4
  70.6 1.4 copy-done.7
  72.0 5.5 %level3.1 = (f32[4,1,192,128]{3,2,1,0:T(8,128)S(1)}, f32[4,1,192,128]{3,2,1,0:T(8,128)S(1)}, bf16[5,192,128]{2,1,0:T(8,128)(2,1)S(1)}) custom-call(s32[3,16]{1,0:T(4,128)S(1)} %copy-done.1, bf16[4,12,8,16,128]{4,3,2,1,0:T(8,128)(2,1)S(1)} %copy-done.4, bf16[4,12,8,16,128]{4,3,2,1,0:T(8,128)(2,1)S(1)} %copy-done.7, ...), custom_call_target="tpu_custom_call" | custom-call | flops 3221225472 | bytes 4194304 | tf_op jit(solution)/shard_map/level3/pallas_call | solution.py:402
  77.5 6.5 %collective-permute-start.5 = (bf16[5,192,128]{2,1,0:T(8,128)(2,1)S(1)}, bf16[5,192,128]{2,1,0:T(8,128)(2,1)S(1)}, u32[]{:S(2)}, u32[]{:S(2)}) collective-permute-start(bf16[5,192,128]{2,1,0:T(8,128)(2,1)S(1)} %get-tuple-element.38), channel_id=1, source_target_pairs={{0,4},{4,0},{8,12},{12,8},{16,20},{20,16},{24,28},{28,24},{1,5},{5... | collective-permute-start | bytes 737288 | tf_op jit(solution)/shard_map/ppermute | solution.py:414
  83.9 16.5 %own.1 = (f32[4,12,8,16,128]{4,3,2,1,0:T(8,128)}, f32[4,12,8,16,128]{4,3,2,1,0:T(8,128)}) custom-call(s32[3,16]{1,0:T(4,128)S(1)} %copy-done.1, bf16[4,12,8,16,128]{4,3,2,1,0:T(8,128)(2,1)S(1)} %copy-done.4, bf16[4,12,8,16,128]{4,3,2,1,0:T(8,128)(2,1)S(1)} %copy-done.7, bf16[4,12,8,16,128]{4,3,2,1,0:T(8,128)(2,1)S(1)} %copy-done.9), custom_call_target="tpu_custom_call" | custom-call | flops 12884901888 | bytes 10485760 | tf_op jit(solution)/shard_map/own/pallas_call | solution.py:369
  100.4 0.0 collective-permute-done.4.m2
  100.4 0.0 collective-permute-done.3.m1
  100.4 0.0 collective-permute-done.5.m3
  100.4 5.0 %merge.1 = (bf16[384,512]{1,0:T(8,128)(2,1)S(1)}, bf16[384,512]{1,0:T(8,128)(2,1)S(1)}, bf16[384,512]{1,0:T(8,128)(2,1)S(1)}, bf16[384,512]{1,0:T(8,128)(2,1)S(1)}) custom-call(s32[3,16]{1,0:T(4,128)S(1)} %copy-done.1, f32[4,12,8,16,128]{4,3,2,1,0:T(8,128)} %get-tuple-element.27.o0, f32[4,12,8,16,128]{4,3,2,1,0:T(8,128)} %get-tuple-element.28.s0, ...), custom_call_target="tpu_custom_call" | custom-call | flops 536870912 | bytes 10485760 | tf_op jit(solution)/shard_map/merge/pallas_call | solution.py:418
  105.4 4.4 %collective-permute-start.6 = (bf16[384,512]{1,0:T(8,128)(2,1)S(1)}, bf16[384,512]{1,0:T(8,128)(2,1)S(1)}, u32[]{:S(2)}, u32[]{:S(2)}) collective-permute-start(bf16[384,512]{1,0:T(8,128)(2,1)S(1)} %get-tuple-element.40), channel_id=1, source_target_pairs={{0,1},{1,0},{2,3},{3,2},{4,5},{5,4},{6,7},{7,6},{8,9},{9,8},{10,11... | collective-permute-start | bytes 1179656 | tf_op jit(solution)/shard_map/ppermute | solution.py:435
  109.9 0.2 collective-permute-start.7
  110.0 1.5 %collective-permute-start.8 = (bf16[384,512]{1,0:T(8,128)(2,1)S(1)}, bf16[384,512]{1,0:T(8,128)(2,1)S(1)}, u32[]{:S(2)}, u32[]{:S(2)}) collective-permute-start(bf16[384,512]{1,0:T(8,128)(2,1)S(1)} %get-tuple-element.42), channel_id=1, source_target_pairs={{0,3},{1,2},{2,1},{3,0},{4,7},{5,6},{6,5},{7,4},{8,11},{9,10},{10,... | collective-permute-start | bytes 1179656 | tf_op jit(solution)/shard_map/ppermute | solution.py:435
  111.6 9.0 %collective-permute-done.7.a2 = bf16[384,512]{1,0:T(8,128)(2,1)S(1)} collective-permute-done((bf16[384,512]{1,0:T(8,128)(2,1)S(1)}, bf16[384,512]{1,0:T(8,128)(2,1)S(1)}, u32[]{:S(2)}, u32[]{:S(2)}) %collective-permute-start.7) | collective-permute-done | bytes 393248 | tf_op jit(solution)/shard_map/ppermute | solution.py:435
  120.6 8.6 %collective-permute-done.8.a3 = bf16[384,512]{1,0:T(8,128)(2,1)S(1)} collective-permute-done((bf16[384,512]{1,0:T(8,128)(2,1)S(1)}, bf16[384,512]{1,0:T(8,128)(2,1)S(1)}, u32[]{:S(2)}, u32[]{:S(2)}) %collective-permute-start.8) | collective-permute-done | bytes 393248 | tf_op jit(solution)/shard_map/ppermute | solution.py:435
  129.1 7.8 %project.1 = bf16[384,2048]{1,0:T(8,128)(2,1)} custom-call(bf16[384,512]{1,0:T(8,128)(2,1)S(1)} %get-tuple-element.39.a0, bf16[384,512]{1,0:T(8,128)(2,1)S(1)} %collective-permute-done.6.a1, bf16[384,512]{1,0:T(8,128)(2,1)S(1)} %collective-permute-done.7.a2, bf16[384,512]{1,0:T(8,128)(2,1)S(1)} %collective-permute-done.8.a3, bf16[2048,2048]{1,0:T(8,128)(2,1)} %w_ref.1), custom_call_target="tpu_custom_call" | custom-call | flops 3221225472 | bytes 12582912 | tf_op jit(solution)/shard_map/project/pallas_call | solution.py:438
  (16 shorter events, 0.0 us)
Async XLA Ops:
  6.5 62.7 %all-gather.3.cloned.1.call-start = ((), (), s32[]{:S(2)}) async-start(), calls=%async_computation | async-start | bytes 1966080 | tf_op jit(solution)/shard_map/all_gather | solution.py:368
  6.5 0.7 copy-start
  7.2 50.0 %copy-start.1 = (s32[3,16]{1,0:T(4,128)S(1)}, s32[3,16]{1,0:T(4,128)}, u32[]{:S(2)}) copy-start(s32[3,16]{1,0:T(4,128)} %off_ref.11) | copy-start | bytes 580
  12.4 1.1 copy-start.2
  13.5 1.2 copy-start.5
  14.7 42.5 %collective-permute-start.1 = (bf16[4,2,2,192,128]{4,3,2,1,0:T(8,128)(2,1)S(1)}, bf16[4,2,2,192,128]{4,3,2,1,0:T(8,128)(2,1)S(1)}, u32[]{:S(2)}, u32[]{:S(2)}) collective-permute-start(bf16[4,2,2,192,128]{4,3,2,1,0:T(8,128)(2,1)S(1)} %get-tuple-element.30), channel_id=1, source_target_pairs={{0,8},{4,12},{16,24},{20,28},{1,9},{5,13},{17,25},{21,29},{2,10},{... | collective-permute-start | bytes 2359304 | tf_op jit(solution)/shard_map/ppermute | solution.py:367
  16.0 14.4 %collective-permute-start = (bf16[4,3,192,128]{3,2,1,0:T(8,128)(2,1)S(1)}, bf16[4,3,192,128]{3,2,1,0:T(8,128)(2,1)S(1)}, u32[]{:S(2)}, u32[]{:S(2)}) collective-permute-start(bf16[4,3,192,128]{3,2,1,0:T(8,128)(2,1)S(1)} %get-tuple-element.29), channel_id=1, source_target_pairs={{0,4},{4,0},{8,12},{12,8},{16,20},{20,16},{24,28},{28,24},{1,5},{5... | collective-permute-start | bytes 1769480 | tf_op jit(solution)/shard_map/ppermute | solution.py:366
  16.3 49.9 %collective-permute-start.2 = (bf16[4,4,192,128]{3,2,1,0:T(8,128)(2,1)S(1)}, bf16[4,4,192,128]{3,2,1,0:T(8,128)(2,1)S(1)}, u32[]{:S(2)}, u32[]{:S(2)}) collective-permute-start(bf16[4,4,192,128]{3,2,1,0:T(8,128)(2,1)S(1)} %get-tuple-element.36), channel_id=1, source_target_pairs={{4,0},{12,8},{20,16},{28,24},{5,1},{13,9},{21,17},{29,25},{6,2},{1... | collective-permute-start | bytes 2359304 | tf_op jit(solution)/shard_map/ppermute | solution.py:365
  57.2 1.4 copy-start.3
  58.6 7.6 %copy-start.6 = (bf16[4,12,8,16,128]{4,3,2,1,0:T(8,128)(2,1)S(1)}, bf16[4,12,8,16,128]{4,3,2,1,0:T(8,128)(2,1)}, u32[]{:S(2)}) copy-start(bf16[4,12,8,16,128]{4,3,2,1,0:T(8,128)(2,1)} %copy-done.5) | copy-start | bytes 4718596
  58.6 7.6 %copy-start.8 = (bf16[4,12,8,16,128]{4,3,2,1,0:T(8,128)(2,1)S(1)}, bf16[4,12,8,16,128]{4,3,2,1,0:T(8,128)(2,1)}, u32[]{:S(2)}) copy-start(bf16[4,12,8,16,128]{4,3,2,1,0:T(8,128)(2,1)} %get-tuple-element.26.vt) | copy-start | bytes 4718596
  66.0 34.4 %collective-permute-start.4 = (bf16[9,192,128]{2,1,0:T(8,128)(2,1)}, bf16[9,192,128]{2,1,0:T(8,128)(2,1)S(1)}, u32[]{:S(2)}, u32[]{:S(2)}) collective-permute-start(bf16[9,192,128]{2,1,0:T(8,128)(2,1)} %get-tuple-element.37), channel_id=1, source_target_pairs={{0,4},{4,0},{8,12},{12,8},{16,20},{20,16},{24,28},{28,24},{1,5},{5... | collective-permute-start | bytes 1327112 | tf_op jit(solution)/shard_map/ppermute | solution.py:414
  67.9 32.5 %collective-permute-start.3 = (bf16[17,192,128]{2,1,0:T(8,128)(2,1)}, bf16[17,192,128]{2,1,0:T(8,128)(2,1)S(1)}, u32[]{:S(2)}, u32[]{:S(2)}) collective-permute-start(bf16[17,192,128]{2,1,0:T(8,128)(2,1)} %lower.1), channel_id=1, source_target_pairs={{0,4},{8,12},{16,20},{24,28},{1,5},{9,13},{17,21},{25,29},{2,6},{1... | collective-permute-start | bytes 2506760 | tf_op jit(solution)/shard_map/ppermute | solution.py:390
  69.2 1.4 copy-start.4
  70.6 1.4 copy-start.7
  72.0 11.9 %copy-start.9 = (bf16[4,12,8,16,128]{4,3,2,1,0:T(8,128)(2,1)S(1)}, bf16[4,12,8,16,128]{4,3,2,1,0:T(8,128)(2,1)}, u32[]{:S(2)}) copy-start(bf16[4,12,8,16,128]{4,3,2,1,0:T(8,128)(2,1)} %get-tuple-element.26.vt) | copy-start | bytes 4718596
  77.5 22.9 %collective-permute-start.5 = (bf16[5,192,128]{2,1,0:T(8,128)(2,1)S(1)}, bf16[5,192,128]{2,1,0:T(8,128)(2,1)S(1)}, u32[]{:S(2)}, u32[]{:S(2)}) collective-permute-start(bf16[5,192,128]{2,1,0:T(8,128)(2,1)S(1)} %get-tuple-element.38), channel_id=1, source_target_pairs={{0,4},{4,0},{8,12},{12,8},{16,20},{20,16},{24,28},{28,24},{1,5},{5... | collective-permute-start | bytes 737288 | tf_op jit(solution)/shard_map/ppermute | solution.py:414
  105.4 6.2 %collective-permute-start.6 = (bf16[384,512]{1,0:T(8,128)(2,1)S(1)}, bf16[384,512]{1,0:T(8,128)(2,1)S(1)}, u32[]{:S(2)}, u32[]{:S(2)}) collective-permute-start(bf16[384,512]{1,0:T(8,128)(2,1)S(1)} %get-tuple-element.40), channel_id=1, source_target_pairs={{0,1},{1,0},{2,3},{3,2},{4,5},{5,4},{6,7},{7,6},{8,9},{9,8},{10,11... | collective-permute-start | bytes 1179656 | tf_op jit(solution)/shard_map/ppermute | solution.py:435
  109.9 10.7 %collective-permute-start.7 = (bf16[384,512]{1,0:T(8,128)(2,1)S(1)}, bf16[384,512]{1,0:T(8,128)(2,1)S(1)}, u32[]{:S(2)}, u32[]{:S(2)}) collective-permute-start(bf16[384,512]{1,0:T(8,128)(2,1)S(1)} %get-tuple-element.41), channel_id=1, source_target_pairs={{0,2},{1,3},{2,0},{3,1},{4,6},{5,7},{6,4},{7,5},{8,10},{9,11},{10,... | collective-permute-start | bytes 1179656 | tf_op jit(solution)/shard_map/ppermute | solution.py:435
  110.0 19.1 %collective-permute-start.8 = (bf16[384,512]{1,0:T(8,128)(2,1)S(1)}, bf16[384,512]{1,0:T(8,128)(2,1)S(1)}, u32[]{:S(2)}, u32[]{:S(2)}) collective-permute-start(bf16[384,512]{1,0:T(8,128)(2,1)S(1)} %get-tuple-element.42), channel_id=1, source_target_pairs={{0,3},{1,2},{2,1},{3,0},{4,7},{5,6},{6,5},{7,4},{8,11},{9,10},{10,... | collective-permute-start | bytes 1179656 | tf_op jit(solution)/shard_map/ppermute | solution.py:435
Sparse Core Ops, SparseCore 0:
  14.9 46.9 all-gather.2

commit v2 on v0

v2 whole, which is shorter than its diff:
```python
import functools
import math

import jax
import jax.numpy as jnp
from jax import lax
from jax.experimental import pallas as pl
from jax.experimental.pallas import tpu as pltpu
from jax.sharding import PartitionSpec as P

DH = 128
HEADS_HERE = 4
PER = 2
RES = 8
SUB = 16
BLK = RES * SUB
NEG = -1e30
RATE = math.log2(math.e) / math.sqrt(DH)
BF16 = jnp.bfloat16
F32 = jnp.float32
VMEM_LIMIT = 20 * 1024 * 1024


def iota(shape, dim):
    return lax.broadcasted_iota(jnp.int32, shape, dim)


def regroup_matrix(inverse):
    row, col = iota((BLK, BLK), 0), iota((BLK, BLK), 1)
    if inverse:
        hit = col == (row % RES) * SUB + row // RES
    else:
        hit = col == (row % SUB) * RES + row // SUB
    return jnp.where(hit, 1.0, 0.0).astype(BF16)


def causal_bias(position, size):
    rows = position(iota((size, size), 0))
    cols = position(iota((size, size), 1))
    return jnp.where(cols <= rows, 0.0, NEG)


def scores_of(q, blocks):
    scores = []
    for k, _, bias in blocks:
        s = lax.dot_general(q, k, (((1,), (1,)), ((), ())), preferred_element_type=F32)
        scores.append(s if bias is None else s + bias)
    return scores


def finish(scores, blocks):
    wide = scores[0]
    for s in scores[1:]:
        wide = jnp.maximum(wide, s)
    top = jnp.max(wide, axis=1, keepdims=True)
    total = None
    for s, (_, v, _) in zip(scores, blocks):
        p = jnp.exp2((s - top) * RATE).astype(BF16)
        with_ones = jnp.concatenate([v, jnp.ones(v.shape, BF16)], axis=1)
        part = jnp.dot(p, with_ones, preferred_element_type=F32)
        total = part if total is None else total + part
    row_sum = total[:, DH:]
    return total[:, :DH] / row_sum, top * RATE + jnp.log2(row_sum)


def attend_all(tasks):
    held = None
    for load, blocks, put in tasks:
        blocks = blocks()
        scores = scores_of(load(), blocks)
        if held is not None:
            held[2](*finish(held[0], held[1]))
        held = (scores, blocks, put)
    held[2](*finish(held[0], held[1]))


def merge(parts):
    top = parts[0][1]
    for _, lse in parts[1:]:
        top = jnp.maximum(top, lse)
    out, weight = 0.0, 0.0
    for o, lse in parts:
        w = jnp.exp2(lse - top)
        out += o * w
        weight += w
    return out / weight, top + jnp.log2(weight)


def rows_of(ref, level, shift, first=0, count=None):
    count = ref.shape[0] - first if count is None else count
    return [
        ref[pl.ds(first, count), shift + j * 2**level].reshape(count * SUB, DH)
        for j in range(RES // 2**level)
    ]


def shift_of(off_ref, level, head):
    return off_ref[level - 1, lax.axis_index("head") * HEADS_HERE + head]


def prep_kernel(off_ref, q_hbm, k_hbm, v_hbm, qt, kt, vt, first, q23, kv2a, kv2b, kv3, held, sems):
    heads, blocks = qt.shape[:2]
    parts = 2
    rows = held.shape[1] // parts
    copies = {}
    for i, src in enumerate((k_hbm, q_hbm, v_hbm)):
        for n in range(parts):
            at = pl.ds(n * rows, rows)
            copies[i, n] = pltpu.make_async_copy(src.at[at], held.at[i, at], sems.at[i, n])
            copies[i, n].start()
    turn = regroup_matrix(False)
    for i, dst in enumerate((kt, qt, vt)):
        for n in range(parts):
            copies[i, n].wait()
            for b in range(n * blocks // parts, (n + 1) * blocks // parts):
                x = held[i, b * BLK : (b + 1) * BLK, :]
                x = jnp.dot(turn, x, preferred_element_type=F32).astype(BF16)
                for h in range(heads):
                    dst[h, b] = x[:, h * DH : (h + 1) * DH].reshape(RES, SUB, DH)
    for h in range(heads):
        o2, o3 = (shift_of(off_ref, level, h) for level in (2, 3))
        g, n = divmod(h, PER)
        for j, x in enumerate(rows_of(qt.at[h], 2, o2) + rows_of(qt.at[h], 3, o3)):
            q23[h, j] = x
        for i, src in enumerate((kt, vt)):
            for j, x in enumerate(rows_of(src.at[h], 2, o2)):
                (kv2a, kv2b)[g][n, i, j] = x
            kv3[h, i] = rows_of(src.at[h], 3, o3)[0]

    @pl.when(lax.axis_index("ctx") % 2 == 1)
    def _():
        for h in range(2):
            for j, x in enumerate(rows_of(qt.at[h], 1, shift_of(off_ref, 1, h))):
                first[4 * h + j] = x

    @pl.when(lax.axis_index("ctx") % 2 == 0)
    def _():
        for i, src in enumerate((kt, vt)):
            for j, x in enumerate(rows_of(src.at[3], 1, shift_of(off_ref, 1, 3))):
                first[4 * i + j] = x


def own_kernel(group, off_ref, qt, kt, vt, token, out, lse):
    blocks = qt.shape[1]
    tasks = []

    def level0(h, n, step):
        head = group * PER + h
        size = step * BLK
        bias = causal_bias(lambda r: r // BLK * BLK + r % SUB * RES + r % BLK // SUB, size)
        load = lambda ref, n: ref[head, n * step : (n + 1) * step].reshape(size, DH)

        def put(o, s):
            out[h, n * step : (n + 1) * step] = o.reshape(step, RES, SUB, DH)
            lse[h, n * step : (n + 1) * step] = s.reshape(step, RES, SUB, DH)

        tasks.append(
            (
                lambda: load(qt, n),
                lambda: [
                    (load(kt, i), load(vt, i), bias if i == n else None) for i in range(n + 1)
                ],
                put,
            )
        )

    def level1(h, n, step):
        head = group * PER + h
        shift = shift_of(off_ref, 1, head)
        rows = step * SUB
        slices = RES // 2
        size = rows * slices
        bias = causal_bias(lambda r: r % rows * slices + r // rows, size)

        def load(ref, n):
            return jnp.concatenate(rows_of(ref.at[head], 1, shift, n * step, step), axis=0)

        def put(o, s):
            for j in range(slices):
                at = (h, pl.ds(n * step, step), shift + 2 * j)
                was = (out[at].reshape(rows, DH), lse[at].reshape(rows, DH))
                fresh = (o[j * rows : (j + 1) * rows], s[j * rows : (j + 1) * rows])
                both, total = merge([was, fresh])
                out[at] = both.reshape(step, SUB, DH)
                lse[at] = total.reshape(step, SUB, DH)

        tasks.append(
            (
                lambda: load(qt, n),
                lambda: [
                    (load(kt, i), load(vt, i), bias if i == n else None) for i in range(n + 1)
                ],
                put,
            )
        )

    for n in range(blocks // 2):
        for h in range(PER):
            level0(h, n, 2)
    for n in range(blocks // 4):
        for h in range(PER):
            level1(h, n, 4)
    attend_all(tasks)


def put_stat(slab, stat, place):
    lane = iota(stat.shape, 1)
    rest = stat
    now = slab[...]
    for i in range(3):
        piece = rest.astype(BF16)
        rest = rest - piece.astype(F32)
        now = jnp.where(lane == place + 32 * i, piece, now)
    slab[...] = now


def get_stat(slab, place):
    lane = iota(slab.shape, 1)
    hit = (lane == place) | (lane == place + 32) | (lane == place + 64)
    return jnp.sum(jnp.where(hit, slab[...].astype(F32), 0.0), axis=1, keepdims=True)


def put_message(msg, place, o, s, count):
    rows = msg.shape[1]
    for j in range(count):
        at = slice(j * rows, (j + 1) * rows)
        msg[place + j] = o[at].astype(BF16)
        put_stat(msg.at[msg.shape[0] - 1], s[at], place + j)


def pair_tasks(off_ref, head, load, keys, values, put):
    count = RES // 2

    def blocks():
        k, v = keys(), values()
        return [
            (jnp.concatenate(k[i : i + 2], axis=0), jnp.concatenate(v[i : i + 2], axis=0), None)
            for i in range(0, count, 2)
        ]

    return [
        (
            lambda j=j: jnp.concatenate(load()[j : j + 2], axis=0),
            blocks,
            lambda o, s, j=j: put(j, o, s),
        )
        for j in range(0, count, 2)
    ]


def lower_kernel(heads, off_ref, got, qt, kt, vt, token, msg, *local):
    last = msg.shape[0] - 1
    count = RES // 2
    rows = msg.shape[1]
    later = lax.axis_index("ctx") % 2 == 1
    msg[...] = jnp.zeros(msg.shape, BF16)

    @pl.when(jnp.logical_not(later))
    def _():
        tasks = []
        for n, head in enumerate(heads):
            shift = shift_of(off_ref, 1, head)
            tasks += pair_tasks(
                off_ref,
                head,
                lambda n=n: [got[n * count + j] for j in range(count)],
                lambda head=head, shift=shift: rows_of(kt.at[head], 1, shift),
                lambda head=head, shift=shift: rows_of(vt.at[head], 1, shift),
                lambda j, o, s, n=n: put_message(msg, n * count + j, o, s, 2),
            )
        attend_all(tasks)
        for ref, fill in zip(local, (0.0, NEG)):
            ref[...] = jnp.full(ref.shape, fill, F32)

    if not local:
        return

    @pl.when(later)
    def _():
        for j, x in enumerate(rows_of(qt.at[2], 1, shift_of(off_ref, 1, 2))):
            msg[j] = x
        shift = shift_of(off_ref, 1, 3)

        def put(j, o, s):
            for i in range(2):
                local[0][j + i] = o[i * rows : (i + 1) * rows]
                local[1][j + i] = s[i * rows : (i + 1) * rows]

        attend_all(
            pair_tasks(
                off_ref,
                3,
                lambda: rows_of(qt.at[3], 1, shift),
                lambda: [got[j] for j in range(count)],
                lambda: [got[count + j] for j in range(count)],
                put,
            )
        )


def levels_kernel(group, levels, partner, off_ref, qt, kt, vt, q23, *rest):
    token, rest = rest[0], rest[1:]
    before, outs = {}, {}
    for level in levels:
        number = 1 if level == 2 else 2
        before[level], rest = rest[:number], rest[number:]
    if partner:
        (msg,) = rest
        msg[msg.shape[0] - 1] = jnp.zeros(msg.shape[1:], BF16)
    else:
        for level in levels:
            outs[level], rest = rest[:2], rest[2:]
    ctx = lax.axis_index("ctx")
    z = ctx // 2
    rows = q23.shape[2]
    tasks = []
    place = 0
    for level in levels:
        count = RES // 2**level
        size = count * rows
        base = 0 if level == 2 else 2
        triangle = causal_bias(lambda r, c=count: r % rows * c + r // rows, size)
        later = jnp.where(ctx % 2 == 0, 0.0, NEG)
        for h in range(PER):
            head = group * PER + h
            shift = shift_of(off_ref, level, head)

            def whole(ref, head=head, shift=shift, level=level):
                return jnp.concatenate(rows_of(ref.at[head], level, shift), axis=0)

            def past(h=h, head=head, level=level, size=size):
                if level == 2:
                    kv = before[2][0]
                    bias = jnp.where(z % 2 == 1, 0.0, NEG)
                    return [(kv[h, 0].reshape(size, DH), kv[h, 1].reshape(size, DH), bias)]
                near, far = before[3]
                odd = jnp.where(z % 2 == 1, 0.0, NEG)
                high = jnp.where(z % 4 >= 2, 0.0, NEG)
                return [
                    (near[head, 0], near[head, 1], odd),
                    (far[0, h, 0], far[0, h, 1], high),
                    (far[1, h, 0], far[1, h, 1], high),
                ]

            def own(o, s, h=h, count=count, level=level):
                for j in range(count):
                    at = slice(j * rows, (j + 1) * rows)
                    outs[level][0][h, j] = o[at]
                    outs[level][1][h, j] = s[at]

            if partner:
                load = lambda h=head, b=base, c=count, n=size: q23[h, b : b + c].reshape(n, DH)
                put = lambda o, s, p=place, c=count: put_message(msg, p, o, s, c)
                bias = later
            else:
                load = lambda whole=whole: whole(qt)
                put = own
                bias = triangle
            tasks.append(
                (
                    load,
                    lambda whole=whole, past=past, b=bias: past() + [(whole(kt), whole(vt), b)],
                    put,
                )
            )
            place += count
    attend_all(tasks)


def merge_kernel(group, off_ref, o0, s0, o2, s2, o3, s3, m1, m23, *rest):
    if group:
        o1, s1, *rest = rest
    token, d0, d1, d2, d3, acc, sums = rest
    ctx = lax.axis_index("ctx")
    blocks = o0.shape[1]
    rows = blocks * SUB
    for h in range(PER):
        for level in (1, 2, 3):
            shift = shift_of(off_ref, level, group * PER + h)
            count = RES // 2**level
            msg = m1 if level == 1 else m23
            for j in range(count):
                at = (h, slice(None), shift + j * 2**level)
                place = h * count + j + (2 * PER if level == 3 else 0)
                parts = [(acc[at].reshape(rows, DH), sums[at].reshape(rows, DH))]
                if level == 1 and group and h:
                    parts.append((o1[j], s1[j]))
                else:
                    stat = get_stat(msg.at[msg.shape[0] - 1], place)
                    if level == 1:
                        stat = jnp.where(ctx % 2 == 1, stat, NEG)
                    parts.append((msg[place].astype(F32), jnp.broadcast_to(stat, (rows, DH))))
                if level > 1:
                    own = (o2, s2) if level == 2 else (o3, s3)
                    parts.append((own[0][h, j], own[1][h, j]))
                o, s = merge(parts)
                acc[at] = o.reshape(blocks, SUB, DH)
                sums[at] = s.reshape(blocks, SUB, DH)
    mine = lax.axis_index("head")
    per = blocks // 4
    for t, dest in enumerate((d0, d1, d2, d3)):
        for h in range(PER):
            x = acc[h, pl.ds((mine ^ t) * per, per)].reshape(per * BLK, DH)
            dest[:, h * DH : (h + 1) * DH] = x.astype(BF16)


def project_kernel(group, a0, a1, a2, a3, w_ref, *rest):
    *before, out, plain = rest
    width = a0.shape[1]
    stride = HEADS_HERE * DH
    back = regroup_matrix(True)
    for t, src in enumerate((a0, a1, a2, a3)):
        for b in range(src.shape[0] // BLK):
            at = slice(b * BLK, (b + 1) * BLK)
            x = jnp.dot(back, src[at, :], preferred_element_type=F32)
            plain[at, t * width : (t + 1) * width] = x.astype(BF16)
    mine = lax.axis_index("head")
    tile = 512

    @pl.loop(0, out.shape[1] // tile)
    def _(n):
        cols = pl.ds(pl.multiple_of(n * tile, tile), tile)
        total = before[0][:, cols] if group else None
        for t in range(4):
            first = pl.multiple_of((mine ^ t) * stride + group * width, width)
            part = jnp.dot(
                plain[:, t * width : (t + 1) * width],
                w_ref[pl.ds(first, width), cols],
                preferred_element_type=F32,
            )
            total = part if total is None else total + part
        out[:, cols] = total.astype(out.dtype)


SMEM = pl.BlockSpec(memory_space=pltpu.SMEM)
VMEM = pl.BlockSpec(memory_space=pltpu.VMEM)
ANY = pl.BlockSpec(memory_space=pl.ANY)
HBM = pl.BlockSpec(memory_space=pltpu.HBM)


def shape(*dims, dtype=BF16):
    return jax.ShapeDtypeStruct(dims, dtype)


def call(kernel, specs, outs, name, macs, moved=4 * 2**20, scratch=(), aliases={}):
    return pl.pallas_call(
        kernel,
        in_specs=specs,
        out_specs=jax.tree.map(lambda _: VMEM, outs),
        out_shape=outs,
        scratch_shapes=scratch,
        input_output_aliases=aliases,
        compiler_params=pltpu.CompilerParams(vmem_limit_bytes=VMEM_LIMIT),
        cost_estimate=pl.CostEstimate(
            flops=int(2 * macs), bytes_accessed=moved, transcendentals=0
        ),
        name=name,
    )


def body(queries, keys, values, offsets, out_weight):
    rows_here, width = queries.shape
    blocks = rows_here // BLK
    heads = width // DH
    slots = rows_here // RES
    piece = (slots, DH)
    regrouped = shape(heads, blocks, RES, SUB, DH)
    ctx_size = lax.axis_size("ctx")
    swap = [(i, i ^ 1) for i in range(ctx_size)]
    down = [(i + 1, i) for i in range(0, ctx_size, 2)]
    up = [(i, i + 1) for i in range(0, ctx_size, 2)]
    near = [(i, i ^ 2) for i in range(ctx_size)]
    even = [(i, i + 2) for i in range(ctx_size) if i & 2 == 0]
    far = [(i, i + 4) for i in range(ctx_size) if i & 4 == 0]
    over = [[(i, i ^ t) for i in range(4)] for t in range(4)]

    qt, kt, vt, first, q23, kv2a, kv2b, kv3 = call(
        prep_kernel,
        [SMEM, HBM, HBM, HBM],
        [
            regrouped,
            regrouped,
            regrouped,
            shape(8, *piece),
            shape(heads, 3, *piece),
            shape(PER, 2, 2, *piece),
            shape(PER, 2, 2, *piece),
            shape(heads, 2, *piece),
        ],
        "prep",
        2**30,
        scratch=[pltpu.VMEM((3, rows_here, width), BF16), pltpu.SemaphoreType.DMA((3, 2))],
    )(offsets, queries, keys, values)

    def own(group, token):
        part = shape(PER, blocks, RES, SUB, DH, dtype=F32)
        return call(
            functools.partial(own_kernel, group),
            [SMEM, VMEM, VMEM, VMEM, ANY],
            [part, part],
            "own%d" % group,
            5 * 2**30,
        )(offsets, qt, kt, vt, token)

    def lower(which, got, token):
        outs = [shape(len(which) * 4 + 1, *piece)]
        if len(which) == 2:
            outs += [shape(4, *piece, dtype=F32)] * 2
        return call(
            functools.partial(lower_kernel, which),
            [SMEM] + [VMEM] * 4 + [ANY],
            outs,
            "lower%d" % which[0],
            1.5 * 2**30,
        )(offsets, got, qt, kt, vt, token)

    def levels(group, partner, before, token):
        if partner:
            outs = [shape(PER * 3 + 1, *piece)]
        else:
            outs = [shape(PER, 2, *piece, dtype=F32)] * 2 + [shape(PER, 1, *piece, dtype=F32)] * 2
        return call(
            functools.partial(levels_kernel, group, (2, 3), partner),
            [SMEM] + [VMEM] * 4 + [ANY] + [VMEM] * len(before),
            outs,
            ("partner%d" if partner else "mine%d") % group,
            1.5 * 2**30,
        )(offsets, qt, kt, vt, q23, token, *before)

    def merged(group, parts, token):
        part = shape(PER, blocks, RES, SUB, DH, dtype=F32)
        dest = shape(rows_here // 4, PER * DH)
        return call(
            functools.partial(merge_kernel, group),
            [SMEM] + [VMEM] * len(parts) + [ANY],
            [dest] * 4 + [part] * 2,
            "merge%d" % group,
            2**29,
            aliases={1: 4, 2: 5},
        )(offsets, *parts, token)[:4]

    def spread(rows):
        return [rows[0]] + [lax.ppermute(rows[t], "head", over[t]) for t in (1, 2, 3)]

    def both(group):
        cut = slice(group * PER, (group + 1) * PER)
        return jnp.stack([kv3[cut], kv3_near[cut]])

    kv3_near = lax.ppermute(kv3, "ctx", near)
    first = lax.ppermute(first, "ctx", swap)
    q23 = lax.ppermute(q23, "ctx", swap)
    o0a, s0a = own(0, kv3)
    far_a = both(0)
    kv2a, far_a = lax.optimization_barrier((kv2a, far_a))
    o0b, s0b = own(1, far_a)
    far_a = lax.ppermute(far_a, "ctx", far)
    kv2a = lax.ppermute(kv2a, "ctx", even)
    msg1a, o1, s1 = lower((0, 1), first, s0b)
    turn = lax.ppermute(msg1a, "ctx", swap)
    before_a = [kv2a, kv3_near, far_a]
    (msg_a,) = levels(0, True, before_a, msg1a)
    got_a = lax.ppermute(msg_a, "ctx", swap)
    far_b, kv2b, msg_a = lax.optimization_barrier((both(1), kv2b, msg_a))
    far_b = lax.ppermute(far_b, "ctx", far)
    kv2b = lax.ppermute(kv2b, "ctx", even)
    (msg1b,) = lower((2,), turn, msg_a)
    got1b = lax.ppermute(msg1b, "ctx", up)
    mine_a = levels(0, False, before_a, msg1b)
    rows_a = merged(0, (o0a, s0a, *mine_a, turn, got_a), mine_a[0])
    rows_a_all = spread(rows_a)
    before_b = [kv2b, kv3_near, far_b]
    (msg_b,) = levels(1, True, before_b, rows_a[0])
    got_b = lax.ppermute(msg_b, "ctx", swap)
    mine_b = levels(1, False, before_b, msg_b)
    model = out_weight.shape[1]
    plain = [pltpu.VMEM((rows_here // 4, 4 * PER * DH), BF16)]
    half = call(
        functools.partial(project_kernel, 0),
        [VMEM] * 5 + [ANY],
        shape(rows_here // 4, model, dtype=F32),
        "project0",
        2**30,
        scratch=plain,
    )(*rows_a_all, out_weight, mine_b[0])
    rows_b = merged(1, (o0b, s0b, *mine_b, got1b, got_b, o1, s1), half)
    rows_b_all = spread(rows_b)
    return call(
        functools.partial(project_kernel, 1),
        [VMEM] * 6,
        shape(rows_here // 4, model),
        "project1",
        2**30,
        scratch=plain,
    )(*rows_b_all, out_weight, half)


def solution(mesh):
    placed = (P("ctx", "head"), P("ctx", "head"), P("ctx", "head"), P(), P())
    return jax.shard_map(
        body, mesh=mesh, in_specs=placed, out_specs=P(("ctx", "head"), None), check_vma=False
    )
```

time: 436 us -> 94.5 us (0.22); the launches traced: 430 us -> 93.9 us
  local copies, waits for them, and re-layouts: 190 us -> 4.97 us
  other arithmetic: 118 us -> 0.08 us
  matrix products: 58.9 us -> 0 us
  Pallas kernels: 0 us -> 38.5 us
  blocking collectives: 23.1 us -> 0 us
  starting transfers between devices: 15.8 us -> 28.5 us
    broadcast_in_dim x32 -> x0, local copies, waits for them, and re-layouts: 60.6 us -> none  [the longest x6 20.1 us: pick_rows(): jnp.where(hits[None, :, :, None], shaped, jnp.zeros((), source.dtype))]
    dot_general x13 -> x0, matrix products: 58.9 us -> none  [the longest x6 29.5 us: one_block(): jnp.einsum('hqk,khd->qhd', weights.astype(jnp.bfloat16), value_rows, pref...]
    mul x12 -> x0, local copies, waits for them, and re-layouts: 56.3 us -> none  [the longest x6 28.2 us: merge_levels(): running[2] * old_scale[:, :, None] + fresh[2] * new_scale[:, :, None]]
    reduce_sum x9 -> x0, other arithmetic: 51.2 us -> none  [the longest x6 29.5 us: one_block(): row_sum = jnp.sum(weights, axis=2)]
    select_n x12 -> x0, other arithmetic: 48.4 us -> none  [join_pair(): jnp.where(upper, jnp.concatenate([other_part, mine_part], 0), jnp.concate...]
    pallas_call x0 -> x13, Pallas kernels: none -> 38.5 us  [the longest x2 11.2 us: own(): call(functools.partial(own_kernel, group), [SMEM, VMEM, VMEM, VMEM, ANY],...]
    all_to_all x1 -> x0, blocking collectives: 23.1 us -> none  [body(): lax.all_to_all(attended, 'head', split_axis=0, concat_axis=1, tiled=True)]
    another operation x7 -> x2, local copies, waits for them, and re-layouts: 16.6 us -> 0.05 us  [both(): return jnp.stack([kv3[cut], kv3_near[cut]])]
  transfers between devices with their start and end apart: 12 -> 17, of which waited for: 3 -> 6; matrix products, arithmetic and copies ran while one was open for 56% -> 0% of each run, Pallas kernels for 0% -> 32%
where the time goes in v2:
time: 94.5 us; the launch traced here: 93.9 us
  Pallas kernels  38.5 us (41%)
  starting transfers between devices  28.5 us (30%)
  waiting for transfers between devices  21.6 us (23%)
  local copies, waits for them, and re-layouts  4.97 us (5%)
    ppermute x6, waiting for transfers between devices, spread(): lax.ppermute(rows[t], 'head', over[t])  13.7 us
    pallas_call x2, Pallas kernels, own(): call(functools.partial(own_kernel, group), [SMEM, VMEM, VMEM, VMEM, ANY],...  11.2 us
    pallas_call x4, Pallas kernels, levels(): call(functools.partial(levels_kernel, group, (2, 3), partner), [SMEM] + [...  9.21 us
    ppermute x1, waiting for transfers between devices, body(): kv3_near = lax.ppermute(kv3, 'ctx', near)  7.06 us
    ppermute x1, starting transfers between devices, body(): far_b = lax.ppermute(far_b, 'ctx', far)  5.31 us
    unnamed x12, local copies, waits for them, and re-layouts  4.91 us
    pallas_call x2, Pallas kernels, lower(): call(functools.partial(lower_kernel, which), [SMEM] + [VMEM] * 4 + [ANY],...  4.89 us
    ppermute x1, starting transfers between devices, body(): far_a = lax.ppermute(far_a, 'ctx', far)  4.51 us
  transfers between devices with their start and end apart: 17, of which 6 were waited for; matrix products, arithmetic and copies ran while one was open for 0% of the time, Pallas kernels for 32%

profile of v2, /device:TPU:0, one launch (start us, length us, event | category | flops | bytes accessed | tf_op | source)
XLA Modules:
  0.0 93.9 jit_solution(3937846290033011699)
XLA Ops:
  0.7 1.4 %copy-done.1 = bf16[1536,512]{1,0:T(8,128)(2,1)S(1)} copy-done((bf16[1536,512]{1,0:T(8,128)(2,1)S(1)}, bf16[1536,512]{1,0:T(8,128)(2,1)}, u32[]{:S(2)}) %copy-start.1) | copy-done | bytes 1572888
  2.1 1.4 %copy-done.2 = bf16[1536,512]{1,0:T(8,128)(2,1)S(1)} copy-done((bf16[1536,512]{1,0:T(8,128)(2,1)S(1)}, bf16[1536,512]{1,0:T(8,128)(2,1)}, u32[]{:S(2)}) %copy-start.2) | copy-done | bytes 1572888
  3.5 1.4 %copy-done.3 = bf16[1536,512]{1,0:T(8,128)(2,1)S(1)} copy-done((bf16[1536,512]{1,0:T(8,128)(2,1)S(1)}, bf16[1536,512]{1,0:T(8,128)(2,1)}, u32[]{:S(2)}) %copy-start.3) | copy-done | bytes 1572888
  4.9 3.3 %prep.1 = (bf16[4,12,8,16,128]{4,3,2,1,0:T(8,128)(2,1)S(1)}, bf16[4,12,8,16,128]{4,3,2,1,0:T(8,128)(2,1)S(1)}, bf16[4,12,8,16,128]{4,3,2,1,0:T(8,128)(2,1)S(1)},...) custom-call(s32[3,16]{1,0:T(4,128)S(1)} %copy-done, ...), custom_call_target="tpu_custom_call" | custom-call | flops 2147483648 | bytes 4194304 | tf_op jit(solution)/shard_map/prep/pallas_call | solution.py:477
  8.2 3.1 %collective-permute-start = (bf16[4,2,192,128]{3,2,1,0:T(8,128)(2,1)S(1)}, bf16[4,2,192,128]{3,2,1,0:T(8,128)(2,1)S(1)}, u32[]{:S(2)}, u32[]{:S(2)}) collective-permute-start(bf16[4,2,192,128]{3,2,1,0:T(8,128)(2,1)S(1)} %get-tuple-element.45.token), channel_id=1, source_target_pairs={{0,8},{4,12},{8,0},{12,4},{16,24},{20,28},{24,16},{28,20},{1,9},{5... | collective-permute-start | bytes 1179656 | tf_op jit(solution)/shard_map/ppermute | solution.py:549
  11.3 1.5 %collective-permute-start.2 = (bf16[8,192,128]{2,1,0:T(8,128)(2,1)S(1)}, bf16[8,192,128]{2,1,0:T(8,128)(2,1)S(1)}, u32[]{:S(2)}, u32[]{:S(2)}) collective-permute-start(bf16[8,192,128]{2,1,0:T(8,128)(2,1)S(1)} %get-tuple-element.52), channel_id=1, source_target_pairs={{0,4},{4,0},{8,12},{12,8},{16,20},{20,16},{24,28},{28,24},{1,5},{5... | collective-permute-start | bytes 1179656 | tf_op jit(solution)/shard_map/ppermute | solution.py:550
  13.4 7.1 %collective-permute-done.rest_2_ = bf16[4,2,192,128]{3,2,1,0:T(8,128)(2,1)S(1)} collective-permute-done((bf16[4,2,192,128]{3,2,1,0:T(8,128)(2,1)S(1)}, bf16[4,2,192,128]{3,2,1,0:T(8,128)(2,1)S(1)}, u32[]{:S(2)}, u32[]{:S(2)}) %collective-permute-start) | collective-permute-done | bytes 393248 | tf_op jit(solution)/shard_map/ppermute | solution.py:549
  20.5 3.7 %collective-permute-start.4 = (bf16[2,2,2,192,128]{4,3,2,1,0:T(8,128)(2,1)S(1)}, bf16[2,2,2,192,128]{4,3,2,1,0:T(8,128)(2,1)S(1)}, u32[]{:S(2)}, u32[]{:S(2)}) collective-permute-start(bf16[2,2,2,192,128]{4,3,2,1,0:T(8,128)(2,1)S(1)} %get-tuple-element.55), channel_id=1, source_target_pairs={{0,8},{4,12},{16,24},{20,28},{1,9},{5,13},{17,25},{21,29},{2,10},{... | collective-permute-start | bytes 1179656 | tf_op jit(solution)/shard_map/ppermute | solution.py:557
  24.2 4.5 %collective-permute-start.5 = (bf16[2,2,2,192,128]{4,3,2,1,0:T(8,128)(2,1)S(1)}, bf16[2,2,2,192,128]{4,3,2,1,0:T(8,128)(2,1)S(1)}, u32[]{:S(2)}, u32[]{:S(2)}) collective-permute-start(bf16[2,2,2,192,128]{4,3,2,1,0:T(8,128)(2,1)S(1)} %pad_maximum_fusion.token), channel_id=1, source_target_pairs={{0,16},{4,20},{8,24},{12,28},{1,17},{5,21},{9,25},{13,29},{2,18},{... | collective-permute-start | bytes 1179656 | tf_op jit(solution)/shard_map/ppermute | solution.py:556
  28.7 5.6 %own1.1 = (f32[2,12,8,16,128]{4,3,2,1,0:T(8,128)S(1)}, f32[2,12,8,16,128]{4,3,2,1,0:T(8,128)S(1)}) custom-call(s32[3,16]{1,0:T(4,128)S(1)} %copy-done, bf16[4,12,8,16,128]{4,3,2,1,0:T(8,128)(2,1)S(1)} %get-tuple-element.41.qt, bf16[4,12,8,16,128]{4,3,2,1,0:T(8,128)(2,1)S(1)} %get-tuple-element.42.kt, bf16[4,12,8,16,128]{4,3,2,1,0:T(8,128)(2,1)S(1)} %get-tuple-element.43.vt, ...), custom_call_target="tpu_custom_call" | custom-call | flops 10737418240 | bytes 4194304 | tf_op jit(solution)/shard_map/own1/pallas_call | solution.py:497
  34.4 3.0 %lower0.1 = (bf16[9,192,128]{2,1,0:T(8,128)(2,1)S(1)}, f32[4,192,128]{2,1,0:T(8,128)S(1)}, f32[4,192,128]{2,1,0:T(8,128)S(1)}) custom-call(s32[3,16]{1,0:T(4,128)S(1)} %copy-done, bf16[8,192,128]{2,1,0:T(8,128)(2,1)S(1)} %collective-permute-done.2.got, bf16[4,12,8,16,128]{4,3,2,1,0:T(8,128)(2,1)S(1)} %get-tuple-element.41.qt, ...), custom_call_target="tpu_custom_call" | custom-call | flops 3221225472 | bytes 4194304 | tf_op jit(solution)/shard_map/lower0/pallas_call | solution.py:509
  37.9 5.6 %own0.1 = (f32[2,12,8,16,128]{4,3,2,1,0:T(8,128)S(1)}, f32[2,12,8,16,128]{4,3,2,1,0:T(8,128)S(1)}) custom-call(s32[3,16]{1,0:T(4,128)S(1)} %copy-done, bf16[4,12,8,16,128]{4,3,2,1,0:T(8,128)(2,1)S(1)} %get-tuple-element.41.qt, bf16[4,12,8,16,128]{4,3,2,1,0:T(8,128)(2,1)S(1)} %get-tuple-element.42.kt, bf16[4,12,8,16,128]{4,3,2,1,0:T(8,128)(2,1)S(1)} %get-tuple-element.43.vt, ...), custom_call_target="tpu_custom_call" | custom-call | flops 10737418240 | bytes 4194304 | tf_op jit(solution)/shard_map/own0/pallas_call | solution.py:497
  43.6 2.4 %partner0.1.token = bf16[7,192,128]{2,1,0:T(8,128)(2,1)S(1)} custom-call(s32[3,16]{1,0:T(4,128)S(1)} %copy-done, bf16[4,12,8,16,128]{4,3,2,1,0:T(8,128)(2,1)S(1)} %get-tuple-element.41.qt, bf16[4,12,8,16,128]{4,3,2,1,0:T(8,128)(2,1)S(1)} %get-tuple-element.42.kt, bf16[4,12,8,16,128]{4,3,2,1,0:T(8,128)(2,1)S(1)} %get-tuple-element.43.vt, ...), custom_call_target="tpu_custom_call" | custom-call | flops 3221225472 | bytes 4194304 | tf_op jit(solution)/shard_map/partner0/pallas_call | solution.py:522
  46.0 1.6 %collective-permute-start.6 = (bf16[7,192,128]{2,1,0:T(8,128)(2,1)S(1)}, bf16[7,192,128]{2,1,0:T(8,128)(2,1)S(1)}, u32[]{:S(2)}, u32[]{:S(2)}) collective-permute-start(bf16[7,192,128]{2,1,0:T(8,128)(2,1)S(1)} %partner0.1.token), channel_id=1, source_target_pairs={{0,4},{4,0},{8,12},{12,8},{16,20},{20,16},{24,28},{28,24},{1,5},{5... | collective-permute-start | bytes 1032200 | tf_op jit(solution)/shard_map/ppermute | solution.py:562
  47.6 2.3 %collective-permute-start.7 = (bf16[2,2,2,192,128]{4,3,2,1,0:T(8,128)(2,1)S(1)}, bf16[2,2,2,192,128]{4,3,2,1,0:T(8,128)(2,1)S(1)}, u32[]{:S(2)}, u32[]{:S(2)}) collective-permute-start(bf16[2,2,2,192,128]{4,3,2,1,0:T(8,128)(2,1)S(1)} %get-tuple-element.62), channel_id=1, source_target_pairs={{0,8},{4,12},{16,24},{20,28},{1,9},{5,13},{17,25},{21,29},{2,10},{... | collective-permute-start | bytes 1179656 | tf_op jit(solution)/shard_map/ppermute | solution.py:565
  49.9 5.3 %collective-permute-start.8 = (bf16[2,2,2,192,128]{4,3,2,1,0:T(8,128)(2,1)S(1)}, bf16[2,2,2,192,128]{4,3,2,1,0:T(8,128)(2,1)S(1)}, u32[]{:S(2)}, u32[]{:S(2)}) collective-permute-start(bf16[2,2,2,192,128]{4,3,2,1,0:T(8,128)(2,1)S(1)} %pad_maximum_fusion.1), channel_id=1, source_target_pairs={{0,16},{4,20},{8,24},{12,28},{1,17},{5,21},{9,25},{13,29},{2,18},{... | collective-permute-start | bytes 1179656 | tf_op jit(solution)/shard_map/ppermute | solution.py:564
  55.2 1.9 %lower2.1.rest_0_ = bf16[5,192,128]{2,1,0:T(8,128)(2,1)S(1)} custom-call(s32[3,16]{1,0:T(4,128)S(1)} %copy-done, bf16[9,192,128]{2,1,0:T(8,128)(2,1)S(1)} %collective-permute-done.3.got.m1, bf16[4,12,8,16,128]{4,3,2,1,0:T(8,128)(2,1)S(1)} %get-tuple-element.41.qt, bf16[4,12,8,16,128]{4,3,2,1,0:T(8,128)(2,1)S(1)} %get-tuple-element.42.kt, ...), custom_call_target="tpu_custom_call" | custom-call | flops 3221225472 | bytes 4194304 | tf_op jit(solution)/shard_map/lower2/pallas_call | solution.py:509
  57.1 1.5 %collective-permute-start.9 = (bf16[5,192,128]{2,1,0:T(8,128)(2,1)S(1)}, bf16[5,192,128]{2,1,0:T(8,128)(2,1)S(1)}, u32[]{:S(2)}, u32[]{:S(2)}) collective-permute-start(bf16[5,192,128]{2,1,0:T(8,128)(2,1)S(1)} %lower2.1.rest_0_), channel_id=1, source_target_pairs={{0,4},{8,12},{16,20},{24,28},{1,5},{9,13},{17,21},{25,29},{2,6},{1... | collective-permute-start | bytes 737288 | tf_op jit(solution)/shard_map/ppermute | solution.py:567
  58.6 2.3 %mine0.1 = (f32[2,2,192,128]{3,2,1,0:T(8,128)S(1)}, f32[2,2,192,128]{3,2,1,0:T(8,128)S(1)}, f32[2,1,192,128]{3,2,1,0:T(8,128)S(1)}, f32[2,1,192,128]{3,2,1,0:T(8,128)S(1)}) custom-call(s32[3,16]{1,0:T(4,128)S(1)} %copy-done, bf16[4,12,8,16,128]{4,3,2,1,0:T(8,128)(2,1)S(1)} %get-tuple-element.41.qt, bf16[4,12,8,16,128]{4,3,2,1,0:T(8,128)(2,1)S(1)} %get-tuple-element.42.kt, ...), custom_call_target="tpu_custom_call" | custom-call | flops 3221225472 | bytes 4194304 | tf_op jit(solution)/shard_map/mine0/pallas_call | solution.py:522
  60.9 1.7 %merge0.1 = (bf16[384,256]{1,0:T(8,128)(2,1)S(1)}, bf16[384,256]{1,0:T(8,128)(2,1)S(1)}, bf16[384,256]{1,0:T(8,128)(2,1)S(1)}, bf16[384,256]{1,0:T(8,128)(2,1)S(...) custom-call(s32[3,16]{1,0:T(4,128)S(1)} %copy-done, ...), custom_call_target="tpu_custom_call", output_to_operand_aliasing={{4}: (1, {}), {5}: (2, {})} | custom-call | flops 1073741824 | bytes 4194304 | tf_op jit(solution)/shard_map/merge0/pallas_call | solution.py:533
  62.6 1.5 %collective-permute-start.12 = (bf16[384,256]{1,0:T(8,128)(2,1)S(1)}, bf16[384,256]{1,0:T(8,128)(2,1)S(1)}, u32[]{:S(2)}, u32[]{:S(2)}) collective-permute-start(bf16[384,256]{1,0:T(8,128)(2,1)S(1)} %get-tuple-element.71), channel_id=1, source_target_pairs={{0,2},{1,3},{2,0},{3,1},{4,6},{5,7},{6,4},{7,5},{8,10},{9,11},{10,... | collective-permute-start | bytes 589832 | tf_op jit(solution)/shard_map/ppermute | solution.py:543
  64.5 2.3 %partner1.1.rest_0_ = bf16[7,192,128]{2,1,0:T(8,128)(2,1)S(1)} custom-call(s32[3,16]{1,0:T(4,128)S(1)} %copy-done, bf16[4,12,8,16,128]{4,3,2,1,0:T(8,128)(2,1)S(1)} %get-tuple-element.41.qt, bf16[4,12,8,16,128]{4,3,2,1,0:T(8,128)(2,1)S(1)} %get-tuple-element.42.kt, bf16[4,12,8,16,128]{4,3,2,1,0:T(8,128)(2,1)S(1)} %get-tuple-element.43.vt, ...), custom_call_target="tpu_custom_call" | custom-call | flops 3221225472 | bytes 4194304 | tf_op jit(solution)/shard_map/partner1/pallas_call | solution.py:522
  67.0 2.3 %mine1.1 = (f32[2,2,192,128]{3,2,1,0:T(8,128)S(1)}, f32[2,2,192,128]{3,2,1,0:T(8,128)S(1)}, f32[2,1,192,128]{3,2,1,0:T(8,128)S(1)}, f32[2,1,192,128]{3,2,1,0:T(8,128)S(1)}) custom-call(s32[3,16]{1,0:T(4,128)S(1)} %copy-done, bf16[4,12,8,16,128]{4,3,2,1,0:T(8,128)(2,1)S(1)} %get-tuple-element.41.qt, bf16[4,12,8,16,128]{4,3,2,1,0:T(8,128)(2,1)S(1)} %get-tuple-element.42.kt, ...), custom_call_target="tpu_custom_call" | custom-call | flops 3221225472 | bytes 4194304 | tf_op jit(solution)/shard_map/mine1/pallas_call | solution.py:522
  69.2 1.2 %collective-permute-done.12.a2 = bf16[384,256]{1,0:T(8,128)(2,1)S(1)} collective-permute-done((bf16[384,256]{1,0:T(8,128)(2,1)S(1)}, bf16[384,256]{1,0:T(8,128)(2,1)S(1)}, u32[]{:S(2)}, u32[]{:S(2)}) %collective-permute-start.12) | collective-permute-done | bytes 196640 | tf_op jit(solution)/shard_map/ppermute | solution.py:543
  70.4 3.3 %collective-permute-done.13.a3 = bf16[384,256]{1,0:T(8,128)(2,1)S(1)} collective-permute-done((bf16[384,256]{1,0:T(8,128)(2,1)S(1)}, bf16[384,256]{1,0:T(8,128)(2,1)S(1)}, u32[]{:S(2)}, u32[]{:S(2)}) %collective-permute-start.13) | collective-permute-done | bytes 196640 | tf_op jit(solution)/shard_map/ppermute | solution.py:543
  73.7 2.7 %project0.1.rest_2_.rest_0_ = f32[384,2048]{1,0:T(8,128)S(1)} custom-call(bf16[384,256]{1,0:T(8,128)(2,1)S(1)} %get-tuple-element.61.rest_0_.a0, bf16[384,256]{1,0:T(8,128)(2,1)S(1)} %collective-permute-done.11.a1, bf16[384,256]{1,0:T(8,128)(2,1)S(1)} %collective-permute-done.12.a2, bf16[384,256]{1,0:T(8,128)(2,1)S(1)} %collective-permute-done.13.a3, ...), custom_call_target="tpu_custom_call" | custom-call | flops 2147483648 | bytes 4194304 | tf_op jit(solution)/shard_map/project0/pallas_call | solution.py:577
  76.4 0.8 collective-permute-done.10.m23
  77.3 1.7 %merge1.1 = (bf16[384,256]{1,0:T(8,128)(2,1)S(1)}, bf16[384,256]{1,0:T(8,128)(2,1)S(1)}, bf16[384,256]{1,0:T(8,128)(2,1)S(1)}, bf16[384,256]{1,0:T(8,128)(2,1)S(...) custom-call(s32[3,16]{1,0:T(4,128)S(1)} %copy-done, ...), custom_call_target="tpu_custom_call", output_to_operand_aliasing={{4}: (1, {}), {5}: (2, {})} | custom-call | flops 1073741824 | bytes 4194304 | tf_op jit(solution)/shard_map/merge1/pallas_call | solution.py:533
  79.0 1.5 %collective-permute-start.15 = (bf16[384,256]{1,0:T(8,128)(2,1)S(1)}, bf16[384,256]{1,0:T(8,128)(2,1)S(1)}, u32[]{:S(2)}, u32[]{:S(2)}) collective-permute-start(bf16[384,256]{1,0:T(8,128)(2,1)S(1)} %get-tuple-element.75), channel_id=1, source_target_pairs={{0,2},{1,3},{2,0},{3,1},{4,6},{5,7},{6,4},{7,5},{8,10},{9,11},{10,... | collective-permute-start | bytes 589832 | tf_op jit(solution)/shard_map/ppermute | solution.py:543
  80.9 5.9 %collective-permute-done.15.a2 = bf16[384,256]{1,0:T(8,128)(2,1)S(1)} collective-permute-done((bf16[384,256]{1,0:T(8,128)(2,1)S(1)}, bf16[384,256]{1,0:T(8,128)(2,1)S(1)}, u32[]{:S(2)}, u32[]{:S(2)}) %collective-permute-start.15) | collective-permute-done | bytes 196640 | tf_op jit(solution)/shard_map/ppermute | solution.py:543
  86.8 3.3 %collective-permute-done.16.a3 = bf16[384,256]{1,0:T(8,128)(2,1)S(1)} collective-permute-done((bf16[384,256]{1,0:T(8,128)(2,1)S(1)}, bf16[384,256]{1,0:T(8,128)(2,1)S(1)}, u32[]{:S(2)}, u32[]{:S(2)}) %collective-permute-start.16) | collective-permute-done | bytes 196640 | tf_op jit(solution)/shard_map/ppermute | solution.py:543
  90.1 3.8 %project1.1 = bf16[384,2048]{1,0:T(8,128)(2,1)} custom-call(bf16[384,256]{1,0:T(8,128)(2,1)S(1)} %get-tuple-element.73.a0, bf16[384,256]{1,0:T(8,128)(2,1)S(1)} %collective-permute-done.14.a1, bf16[384,256]{1,0:T(8,128)(2,1)S(1)} %collective-permute-done.15.a2, bf16[384,256]{1,0:T(8,128)(2,1)S(1)} %collective-permute-done.16.a3, ...), custom_call_target="tpu_custom_call" | custom-call | flops 2147483648 | bytes 4194304 | tf_op jit(solution)/shard_map/project1/pallas_call | solution.py:587
  (32 shorter events, 2.7 us)
Async XLA Ops:
  0.0 0.7 copy-start
  0.7 1.4 %copy-start.1 = (bf16[1536,512]{1,0:T(8,128)(2,1)S(1)}, bf16[1536,512]{1,0:T(8,128)(2,1)}, u32[]{:S(2)}) copy-start(bf16[1536,512]{1,0:T(8,128)(2,1)} %q_hbm.1) | copy-start | bytes 4718596
  2.1 1.4 %copy-start.2 = (bf16[1536,512]{1,0:T(8,128)(2,1)S(1)}, bf16[1536,512]{1,0:T(8,128)(2,1)}, u32[]{:S(2)}) copy-start(bf16[1536,512]{1,0:T(8,128)(2,1)} %k_hbm.1) | copy-start | bytes 4718596
  3.5 1.4 %copy-start.3 = (bf16[1536,512]{1,0:T(8,128)(2,1)S(1)}, bf16[1536,512]{1,0:T(8,128)(2,1)}, u32[]{:S(2)}) copy-start(bf16[1536,512]{1,0:T(8,128)(2,1)} %v_hbm.1) | copy-start | bytes 4718596
  8.2 12.2 %collective-permute-start = (bf16[4,2,192,128]{3,2,1,0:T(8,128)(2,1)S(1)}, bf16[4,2,192,128]{3,2,1,0:T(8,128)(2,1)S(1)}, u32[]{:S(2)}, u32[]{:S(2)}) collective-permute-start(bf16[4,2,192,128]{3,2,1,0:T(8,128)(2,1)S(1)} %get-tuple-element.45.token), channel_id=1, source_target_pairs={{0,8},{4,12},{8,0},{12,4},{16,24},{20,28},{24,16},{28,20},{1,9},{5... | collective-permute-start | bytes 1179656 | tf_op jit(solution)/shard_map/ppermute | solution.py:549
  11.3 23.0 %collective-permute-start.2 = (bf16[8,192,128]{2,1,0:T(8,128)(2,1)S(1)}, bf16[8,192,128]{2,1,0:T(8,128)(2,1)S(1)}, u32[]{:S(2)}, u32[]{:S(2)}) collective-permute-start(bf16[8,192,128]{2,1,0:T(8,128)(2,1)S(1)} %get-tuple-element.52), channel_id=1, source_target_pairs={{0,4},{4,0},{8,12},{12,8},{16,20},{20,16},{24,28},{28,24},{1,5},{5... | collective-permute-start | bytes 1179656 | tf_op jit(solution)/shard_map/ppermute | solution.py:550
  12.9 30.7 %collective-permute-start.1 = (bf16[4,3,192,128]{3,2,1,0:T(8,128)(2,1)S(1)}, bf16[4,3,192,128]{3,2,1,0:T(8,128)(2,1)S(1)}, u32[]{:S(2)}, u32[]{:S(2)}) collective-permute-start(bf16[4,3,192,128]{3,2,1,0:T(8,128)(2,1)S(1)} %get-tuple-element.49), channel_id=1, source_target_pairs={{0,4},{4,0},{8,12},{12,8},{16,20},{20,16},{24,28},{28,24},{1,5},{5... | collective-permute-start | bytes 1769480 | tf_op jit(solution)/shard_map/ppermute | solution.py:551
  20.5 23.1 %collective-permute-start.4 = (bf16[2,2,2,192,128]{4,3,2,1,0:T(8,128)(2,1)S(1)}, bf16[2,2,2,192,128]{4,3,2,1,0:T(8,128)(2,1)S(1)}, u32[]{:S(2)}, u32[]{:S(2)}) collective-permute-start(bf16[2,2,2,192,128]{4,3,2,1,0:T(8,128)(2,1)S(1)} %get-tuple-element.55), channel_id=1, source_target_pairs={{0,8},{4,12},{16,24},{20,28},{1,9},{5,13},{17,25},{21,29},{2,10},{... | collective-permute-start | bytes 1179656 | tf_op jit(solution)/shard_map/ppermute | solution.py:557
  24.2 19.4 %collective-permute-start.5 = (bf16[2,2,2,192,128]{4,3,2,1,0:T(8,128)(2,1)S(1)}, bf16[2,2,2,192,128]{4,3,2,1,0:T(8,128)(2,1)S(1)}, u32[]{:S(2)}, u32[]{:S(2)}) collective-permute-start(bf16[2,2,2,192,128]{4,3,2,1,0:T(8,128)(2,1)S(1)} %pad_maximum_fusion.token), channel_id=1, source_target_pairs={{0,16},{4,20},{8,24},{12,28},{1,17},{5,21},{9,25},{13,29},{2,18},{... | collective-permute-start | bytes 1179656 | tf_op jit(solution)/shard_map/ppermute | solution.py:556
  37.4 17.8 %collective-permute-start.3 = (bf16[9,192,128]{2,1,0:T(8,128)(2,1)S(1)}, bf16[9,192,128]{2,1,0:T(8,128)(2,1)S(1)}, u32[]{:S(2)}, u32[]{:S(2)}) collective-permute-start(bf16[9,192,128]{2,1,0:T(8,128)(2,1)S(1)} %get-tuple-element.53.rest_0_), channel_id=1, source_target_pairs={{0,4},{4,0},{8,12},{12,8},{16,20},{20,16},{24,28},{28,24},{1,5},{5... | collective-permute-start | bytes 1327112 | tf_op jit(solution)/shard_map/ppermute | solution.py:559
  46.0 14.9 %collective-permute-start.6 = (bf16[7,192,128]{2,1,0:T(8,128)(2,1)S(1)}, bf16[7,192,128]{2,1,0:T(8,128)(2,1)S(1)}, u32[]{:S(2)}, u32[]{:S(2)}) collective-permute-start(bf16[7,192,128]{2,1,0:T(8,128)(2,1)S(1)} %partner0.1.token), channel_id=1, source_target_pairs={{0,4},{4,0},{8,12},{12,8},{16,20},{20,16},{24,28},{28,24},{1,5},{5... | collective-permute-start | bytes 1032200 | tf_op jit(solution)/shard_map/ppermute | solution.py:562
  47.6 16.6 %collective-permute-start.7 = (bf16[2,2,2,192,128]{4,3,2,1,0:T(8,128)(2,1)S(1)}, bf16[2,2,2,192,128]{4,3,2,1,0:T(8,128)(2,1)S(1)}, u32[]{:S(2)}, u32[]{:S(2)}) collective-permute-start(bf16[2,2,2,192,128]{4,3,2,1,0:T(8,128)(2,1)S(1)} %get-tuple-element.62), channel_id=1, source_target_pairs={{0,8},{4,12},{16,24},{20,28},{1,9},{5,13},{17,25},{21,29},{2,10},{... | collective-permute-start | bytes 1179656 | tf_op jit(solution)/shard_map/ppermute | solution.py:565
  49.9 14.6 %collective-permute-start.8 = (bf16[2,2,2,192,128]{4,3,2,1,0:T(8,128)(2,1)S(1)}, bf16[2,2,2,192,128]{4,3,2,1,0:T(8,128)(2,1)S(1)}, u32[]{:S(2)}, u32[]{:S(2)}) collective-permute-start(bf16[2,2,2,192,128]{4,3,2,1,0:T(8,128)(2,1)S(1)} %pad_maximum_fusion.1), channel_id=1, source_target_pairs={{0,16},{4,20},{8,24},{12,28},{1,17},{5,21},{9,25},{13,29},{2,18},{... | collective-permute-start | bytes 1179656 | tf_op jit(solution)/shard_map/ppermute | solution.py:564
  57.1 19.3 %collective-permute-start.9 = (bf16[5,192,128]{2,1,0:T(8,128)(2,1)S(1)}, bf16[5,192,128]{2,1,0:T(8,128)(2,1)S(1)}, u32[]{:S(2)}, u32[]{:S(2)}) collective-permute-start(bf16[5,192,128]{2,1,0:T(8,128)(2,1)S(1)} %lower2.1.rest_0_), channel_id=1, source_target_pairs={{0,4},{8,12},{16,20},{24,28},{1,5},{9,13},{17,21},{25,29},{2,6},{1... | collective-permute-start | bytes 737288 | tf_op jit(solution)/shard_map/ppermute | solution.py:567
  62.6 6.7 %collective-permute-start.11 = (bf16[384,256]{1,0:T(8,128)(2,1)S(1)}, bf16[384,256]{1,0:T(8,128)(2,1)S(1)}, u32[]{:S(2)}, u32[]{:S(2)}) collective-permute-start(bf16[384,256]{1,0:T(8,128)(2,1)S(1)} %get-tuple-element.70), channel_id=1, source_target_pairs={{0,1},{1,0},{2,3},{3,2},{4,5},{5,4},{6,7},{7,6},{8,9},{9,8},{10,11... | collective-permute-start | bytes 589832 | tf_op jit(solution)/shard_map/ppermute | solution.py:543
  62.6 7.8 %collective-permute-start.12 = (bf16[384,256]{1,0:T(8,128)(2,1)S(1)}, bf16[384,256]{1,0:T(8,128)(2,1)S(1)}, u32[]{:S(2)}, u32[]{:S(2)}) collective-permute-start(bf16[384,256]{1,0:T(8,128)(2,1)S(1)} %get-tuple-element.71), channel_id=1, source_target_pairs={{0,2},{1,3},{2,0},{3,1},{4,6},{5,7},{6,4},{7,5},{8,10},{9,11},{10,... | collective-permute-start | bytes 589832 | tf_op jit(solution)/shard_map/ppermute | solution.py:543
  64.2 9.5 %collective-permute-start.13 = (bf16[384,256]{1,0:T(8,128)(2,1)S(1)}, bf16[384,256]{1,0:T(8,128)(2,1)S(1)}, u32[]{:S(2)}, u32[]{:S(2)}) collective-permute-start(bf16[384,256]{1,0:T(8,128)(2,1)S(1)} %get-tuple-element.72), channel_id=1, source_target_pairs={{0,3},{1,2},{2,1},{3,0},{4,7},{5,6},{6,5},{7,4},{8,11},{9,10},{10,... | collective-permute-start | bytes 589832 | tf_op jit(solution)/shard_map/ppermute | solution.py:543
  64.5 9.2 %slice-start = ((s8[8388608]{0:T(1024)(128)(4,1)}), s8[4194304]{0:T(1024)(128)(4,1)S(1)}, s32[]{:S(2)}) async-start(s8[8388608]{0:T(1024)(128)(4,1)} %bitcast.8), calls=%async_computation | async-start | bytes 8388608
  66.9 6.9 %slice-start.1 = ((s8[8388608]{0:T(1024)(128)(4,1)}), s8[4194304]{0:T(1024)(128)(4,1)S(1)}, s32[]{:S(2)}) async-start(s8[8388608]{0:T(1024)(128)(4,1)} %bitcast.8), calls=%async_computation.1 | async-start | bytes 8388608
  66.9 10.4 %collective-permute-start.10 = (bf16[7,192,128]{2,1,0:T(8,128)(2,1)S(1)}, bf16[7,192,128]{2,1,0:T(8,128)(2,1)S(1)}, u32[]{:S(2)}, u32[]{:S(2)}) collective-permute-start(bf16[7,192,128]{2,1,0:T(8,128)(2,1)S(1)} %partner1.1.rest_0_), channel_id=1, source_target_pairs={{0,4},{4,0},{8,12},{12,8},{16,20},{20,16},{24,28},{28,24},{1,5},{5... | collective-permute-start | bytes 1032200 | tf_op jit(solution)/shard_map/ppermute | solution.py:573
  78.9 1.9 %collective-permute-start.14 = (bf16[384,256]{1,0:T(8,128)(2,1)S(1)}, bf16[384,256]{1,0:T(8,128)(2,1)S(1)}, u32[]{:S(2)}, u32[]{:S(2)}) collective-permute-start(bf16[384,256]{1,0:T(8,128)(2,1)S(1)} %get-tuple-element.74), channel_id=1, source_target_pairs={{0,1},{1,0},{2,3},{3,2},{4,5},{5,4},{6,7},{7,6},{8,9},{9,8},{10,11... | collective-permute-start | bytes 589832 | tf_op jit(solution)/shard_map/ppermute | solution.py:543
  79.0 7.8 %collective-permute-start.15 = (bf16[384,256]{1,0:T(8,128)(2,1)S(1)}, bf16[384,256]{1,0:T(8,128)(2,1)S(1)}, u32[]{:S(2)}, u32[]{:S(2)}) collective-permute-start(bf16[384,256]{1,0:T(8,128)(2,1)S(1)} %get-tuple-element.75), channel_id=1, source_target_pairs={{0,2},{1,3},{2,0},{3,1},{4,6},{5,7},{6,4},{7,5},{8,10},{9,11},{10,... | collective-permute-start | bytes 589832 | tf_op jit(solution)/shard_map/ppermute | solution.py:543
  80.5 9.5 %collective-permute-start.16 = (bf16[384,256]{1,0:T(8,128)(2,1)S(1)}, bf16[384,256]{1,0:T(8,128)(2,1)S(1)}, u32[]{:S(2)}, u32[]{:S(2)}) collective-permute-start(bf16[384,256]{1,0:T(8,128)(2,1)S(1)} %get-tuple-element.76), channel_id=1, source_target_pairs={{0,3},{1,2},{2,1},{3,0},{4,7},{5,6},{6,5},{7,4},{8,11},{9,10},{10,... | collective-permute-start | bytes 589832 | tf_op jit(solution)/shard_map/ppermute | solution.py:543

commit v3 on v2

v3 whole, which is shorter than its diff:
```python
import functools
import math

import jax
import jax.numpy as jnp
from jax import lax
from jax.experimental import pallas as pl
from jax.experimental.pallas import tpu as pltpu
from jax.sharding import PartitionSpec as P

DH = 128
HEADS_HERE = 4
GROUPS = ((0, 1), (2,), (3,))
RES = 8
SUB = 16
BLK = RES * SUB
NEG = -1e30
RATE = math.log2(math.e) / math.sqrt(DH)
BF16 = jnp.bfloat16
F32 = jnp.float32
VMEM_LIMIT = 20 * 1024 * 1024


COST = {'mine0': 10**10}


def iota(shape, dim):
    return lax.broadcasted_iota(jnp.int32, shape, dim)


def regroup_matrix(inverse):
    row, col = iota((BLK, BLK), 0), iota((BLK, BLK), 1)
    if inverse:
        hit = col == (row % RES) * SUB + row // RES
    else:
        hit = col == (row % SUB) * RES + row // SUB
    return jnp.where(hit, 1.0, 0.0).astype(BF16)


def causal_bias(position, size):
    rows = position(iota((size, size), 0))
    cols = position(iota((size, size), 1))
    return jnp.where(cols <= rows, 0.0, NEG)


def scores_of(q, blocks):
    scores = []
    for k, _, bias in blocks:
        s = lax.dot_general(q, k, (((1,), (1,)), ((), ())), preferred_element_type=F32)
        scores.append(s if bias is None else s + bias)
    return scores


def finish(scores, blocks):
    wide = scores[0]
    for s in scores[1:]:
        wide = jnp.maximum(wide, s)
    top = jnp.max(wide, axis=1, keepdims=True)
    total = None
    for s, (_, v, _) in zip(scores, blocks):
        p = jnp.exp2((s - top) * RATE).astype(BF16)
        with_ones = jnp.concatenate([v, jnp.ones(v.shape, BF16)], axis=1)
        part = jnp.dot(p, with_ones, preferred_element_type=F32)
        total = part if total is None else total + part
    row_sum = total[:, DH:]
    return total[:, :DH] / row_sum, top * RATE + jnp.log2(row_sum)


def attend_all(tasks):
    held = None
    for load, blocks, put in tasks:
        blocks = blocks()
        scores = scores_of(load(), blocks)
        if held is not None:
            held[2](*finish(held[0], held[1]))
        held = (scores, blocks, put)
    held[2](*finish(held[0], held[1]))


def merge(parts):
    top = parts[0][1]
    for _, lse in parts[1:]:
        top = jnp.maximum(top, lse)
    out, weight = 0.0, 0.0
    for o, lse in parts:
        w = jnp.exp2(lse - top)
        out += o * w
        weight += w
    return out / weight, top + jnp.log2(weight)


def add_rows(out, lse, at, part):
    held = out[at].shape
    was = (out[at].reshape(part[0].shape), lse[at].reshape(part[0].shape))
    o, s = merge([was, part])
    out[at] = o.reshape(held)
    lse[at] = s.reshape(held)


def rows_of(ref, level, shift, first=0, count=None):
    count = ref.shape[0] - first if count is None else count
    return [
        ref[pl.ds(first, count), shift + j * 2**level].reshape(count * SUB, DH)
        for j in range(RES // 2**level)
    ]


def shift_of(off_ref, level, head):
    return off_ref[level - 1, lax.axis_index("head") * HEADS_HERE + head]


def regroup(sources, targets):
    turn = regroup_matrix(False)
    heads, blocks = targets[0].shape[:2]
    for src, dst in zip(sources, targets):
        for b in range(blocks):
            x = src[b * BLK : (b + 1) * BLK, :]
            x = jnp.dot(turn, x, preferred_element_type=F32).astype(BF16)
            for h in range(heads):
                dst[h, b] = x[:, h * DH : (h + 1) * DH].reshape(RES, SUB, DH)


def prep_kv_kernel(off_ref, k_ref, v_ref, kt, vt, kv3, *kv2):
    regroup((k_ref, v_ref), (kt, vt))
    for h in range(kt.shape[0]):
        o2, o3 = (shift_of(off_ref, level, h) for level in (2, 3))
        (g,) = [g for g, members in enumerate(GROUPS) if h in members]
        n = GROUPS[g].index(h)
        for i, src in enumerate((kt, vt)):
            for j, x in enumerate(rows_of(src.at[h], 2, o2)):
                kv2[g][n, i, j] = x
            kv3[h, i] = rows_of(src.at[h], 3, o3)[0]


def prep_q_kernel(off_ref, q_ref, kt, vt, qt, first, q23):
    regroup((q_ref,), (qt,))
    for h in range(qt.shape[0]):
        o2, o3 = (shift_of(off_ref, level, h) for level in (2, 3))
        for j, x in enumerate(rows_of(qt.at[h], 2, o2) + rows_of(qt.at[h], 3, o3)):
            q23[h, j] = x

    @pl.when(lax.axis_index("ctx") % 2 == 1)
    def _():
        for h in range(2):
            for j, x in enumerate(rows_of(qt.at[h], 1, shift_of(off_ref, 1, h))):
                first[4 * h + j] = x

    @pl.when(lax.axis_index("ctx") % 2 == 0)
    def _():
        for i, src in enumerate((kt, vt)):
            for j, x in enumerate(rows_of(src.at[3], 1, shift_of(off_ref, 1, 3))):
                first[4 * i + j] = x


def own_kernel(heads, off_ref, qt, kt, vt, token, *outs):
    blocks = qt.shape[1]
    tasks = []

    def level0(h, n, step):
        head, out, lse = heads[h], outs[2 * h], outs[2 * h + 1]
        size = step * BLK
        bias = causal_bias(lambda r: r // BLK * BLK + r % SUB * RES + r % BLK // SUB, size)
        load = lambda ref, n: ref[head, n * step : (n + 1) * step].reshape(size, DH)

        def put(o, s):
            out[n * step : (n + 1) * step] = o.reshape(step, RES, SUB, DH)
            lse[n * step : (n + 1) * step] = s.reshape(step, RES, SUB, DH)

        tasks.append(
            (
                lambda: load(qt, n),
                lambda: [
                    (load(kt, i), load(vt, i), bias if i == n else None) for i in range(n + 1)
                ],
                put,
            )
        )

    def level1(h, n, step):
        head, out, lse = heads[h], outs[2 * h], outs[2 * h + 1]
        shift = shift_of(off_ref, 1, head)
        rows = step * SUB
        slices = RES // 2
        size = rows * slices
        bias = causal_bias(lambda r: r % rows * slices + r // rows, size)

        def load(ref, n):
            return jnp.concatenate(rows_of(ref.at[head], 1, shift, n * step, step), axis=0)

        def put(o, s):
            for j in range(slices):
                at = (pl.ds(n * step, step), shift + 2 * j)
                fresh = (o[j * rows : (j + 1) * rows], s[j * rows : (j + 1) * rows])
                add_rows(out, lse, at, fresh)

        tasks.append(
            (
                lambda: load(qt, n),
                lambda: [
                    (load(kt, i), load(vt, i), bias if i == n else None) for i in range(n + 1)
                ],
                put,
            )
        )

    for n in range(blocks // 2):
        for h in range(len(heads)):
            level0(h, n, 2)
    for n in range(blocks // 4):
        for h in range(len(heads)):
            level1(h, n, 4)
    attend_all(tasks)


def put_stat(slab, stat, place):
    lane = iota(stat.shape, 1)
    rest = stat
    now = slab[...]
    for i in range(3):
        piece = rest.astype(BF16)
        rest = rest - piece.astype(F32)
        now = jnp.where(lane == place + 32 * i, piece, now)
    slab[...] = now


def get_stat(slab, place):
    lane = iota(slab.shape, 1)
    hit = (lane == place) | (lane == place + 32) | (lane == place + 64)
    return jnp.sum(jnp.where(hit, slab[...].astype(F32), 0.0), axis=1, keepdims=True)


def put_message(msg, place, o, s, count):
    rows = msg.shape[1]
    for j in range(count):
        at = slice(j * rows, (j + 1) * rows)
        msg[place + j] = o[at].astype(BF16)
        put_stat(msg.at[msg.shape[0] - 1], s[at], place + j)


def pair_tasks(load, keys, values, put):
    count = RES // 2

    def blocks():
        k, v = keys(), values()
        return [
            (jnp.concatenate(k[i : i + 2], axis=0), jnp.concatenate(v[i : i + 2], axis=0), None)
            for i in range(0, count, 2)
        ]

    return [
        (
            lambda j=j: jnp.concatenate(load()[j : j + 2], axis=0),
            blocks,
            lambda o, s, j=j: put(j, o, s),
        )
        for j in range(0, count, 2)
    ]


def lower_kernel(heads, off_ref, got, qt, kt, vt, token, msg, *local):
    last = msg.shape[0] - 1
    count = RES // 2
    rows = msg.shape[1]
    later = lax.axis_index("ctx") % 2 == 1
    msg[...] = jnp.zeros(msg.shape, BF16)

    @pl.when(jnp.logical_not(later))
    def _():
        tasks = []
        for n, head in enumerate(heads):
            shift = shift_of(off_ref, 1, head)
            tasks += pair_tasks(
                lambda n=n: [got[n * count + j] for j in range(count)],
                lambda head=head, shift=shift: rows_of(kt.at[head], 1, shift),
                lambda head=head, shift=shift: rows_of(vt.at[head], 1, shift),
                lambda j, o, s, n=n: put_message(msg, n * count + j, o, s, 2),
            )
        attend_all(tasks)
        for ref, fill in zip(local, (0.0, NEG)):
            ref[...] = jnp.full(ref.shape, fill, F32)

    @pl.when(later)
    def _():
        for j, x in enumerate(rows_of(qt.at[2], 1, shift_of(off_ref, 1, 2))):
            msg[j] = x
        shift = shift_of(off_ref, 1, 3)

        def put(j, o, s):
            for i in range(2):
                local[0][j + i] = o[i * rows : (i + 1) * rows]
                local[1][j + i] = s[i * rows : (i + 1) * rows]

        attend_all(
            pair_tasks(
                lambda: rows_of(qt.at[3], 1, shift),
                lambda: [got[j] for j in range(count)],
                lambda: [got[count + j] for j in range(count)],
                put,
            )
        )


def level_blocks(off_ref, level, head, n, q23, kt, vt, kv2, near, far):
    ctx = lax.axis_index("ctx")
    z = ctx // 2
    shift = shift_of(off_ref, level, head)
    count = RES // 2**level
    rows = q23.shape[2]
    size = count * rows
    odd = jnp.where(z % 2 == 1, 0.0, NEG)
    high = jnp.where(z % 4 >= 2, 0.0, NEG)

    def whole(ref):
        return jnp.concatenate(rows_of(ref.at[head], level, shift), axis=0)

    def blocks(bias):
        if level == 2:
            past = [(kv2[n, 0].reshape(size, DH), kv2[n, 1].reshape(size, DH), odd)]
        else:
            past = [
                (near[head, 0], near[head, 1], odd),
                (far[0, n, 0], far[0, n, 1], high),
                (far[1, n, 0], far[1, n, 1], high),
            ]
        return past + [(whole(kt), whole(vt), bias)]

    return whole, blocks, shift, count, rows


def partner_kernel(heads, extra, off_ref, kt, vt, q23, kv2, near, far, token, *refs):
    *turn, msg = refs
    later = jnp.where(lax.axis_index("ctx") % 2 == 0, 0.0, NEG)
    msg[msg.shape[0] - 1] = jnp.zeros(msg.shape[1:], BF16)
    tasks, place = [], 0
    for level in (2, 3):
        for n, head in enumerate(heads):
            _, blocks, _, count, rows = level_blocks(
                off_ref, level, head, n, q23, kt, vt, kv2, near, far
            )
            first = 0 if level == 2 else 2
            tasks.append(
                (
                    lambda h=head, f=first, c=count, r=rows: q23[h, f : f + c].reshape(c * r, DH),
                    lambda blocks=blocks: blocks(later),
                    lambda o, s, p=place, c=count: put_message(msg, p, o, s, c),
                )
            )
            place += count
    for head in extra:
        shift = shift_of(off_ref, 1, head)
        tasks += pair_tasks(
            lambda: [turn[0][j] for j in range(RES // 2)],
            lambda shift=shift, head=head: rows_of(kt.at[head], 1, shift),
            lambda shift=shift, head=head: rows_of(vt.at[head], 1, shift),
            lambda j, o, s, p=place: put_message(msg, p + j, o, s, 2),
        )
    attend_all(tasks)


def add_lower(off_ref, head, msg, first, out, lse):
    later = lax.axis_index("ctx") % 2 == 1
    for j in range(RES // 2):
        at = (slice(None), shift_of(off_ref, 1, head) + 2 * j)
        stat = jnp.where(later, get_stat(msg.at[msg.shape[0] - 1], first + j), NEG)
        part = msg[first + j].astype(F32)
        add_rows(out, lse, at, (part, jnp.broadcast_to(stat, part.shape)))


def mine_kernel(heads, off_ref, *refs):
    number = len(heads)
    refs = refs[2 * number :]
    (qt, kt, vt, q23, kv2, near, far, token), refs = refs[:8], refs[8:]
    lower, state = refs[: -2 * number], refs[-2 * number :]
    tasks = []
    for level in (2, 3):
        for n, head in enumerate(heads):
            out, lse = state[2 * n : 2 * n + 2]
            whole, blocks, shift, count, rows = level_blocks(
                off_ref, level, head, n, q23, kt, vt, kv2, near, far
            )
            triangle = causal_bias(lambda r, c=count, m=rows: r % m * c + r // m, count * rows)

            def put(o, s, out=out, lse=lse, shift=shift, level=level, count=count, rows=rows):
                for j in range(count):
                    at = slice(j * rows, (j + 1) * rows)
                    add_rows(out, lse, (slice(None), shift + j * 2**level), (o[at], s[at]))

            tasks.append(
                (
                    lambda whole=whole: whole(qt),
                    lambda blocks=blocks, t=triangle: blocks(t),
                    put,
                )
            )
    attend_all(tasks)
    for n, head in enumerate(heads):
        if len(lower) == 1:
            add_lower(off_ref, head, lower[0], n * (RES // 2), state[2 * n], state[2 * n + 1])
        elif lower:
            for j in range(RES // 2):
                at = (slice(None), shift_of(off_ref, 1, head) + 2 * j)
                add_rows(state[2 * n], state[2 * n + 1], at, (lower[0][j], lower[1][j]))


def finish_kernel(heads, off_ref, *refs):
    number = len(heads)
    refs = refs[2 * number :]
    msg, token, *extra = refs[: -4 - 2 * number]
    dests, state = refs[-4 - 2 * number : -2 * number], refs[-2 * number :]
    if extra:
        add_lower(off_ref, heads[0], extra[0], 6, *state)
    place = 0
    for level in (2, 3):
        for n, head in enumerate(heads):
            shift = shift_of(off_ref, level, head)
            for j in range(RES // 2**level):
                part = msg[place].astype(F32)
                stat = get_stat(msg.at[msg.shape[0] - 1], place)
                add_rows(
                    state[2 * n],
                    state[2 * n + 1],
                    (slice(None), shift + j * 2**level),
                    (part, jnp.broadcast_to(stat, part.shape)),
                )
                place += 1
    mine = lax.axis_index("head")
    per = state[0].shape[0] // 4
    for t, dest in enumerate(dests):
        for n in range(number):
            x = state[2 * n][pl.ds((mine ^ t) * per, per)].reshape(per * BLK, DH)
            dest[:, n * DH : (n + 1) * DH] = x.astype(BF16)


def weights_kernel(w_ref, token, out):
    mine = lax.axis_index("head")
    at = 0
    for members in GROUPS:
        width = len(members) * DH
        for t in range(4):
            first = (mine ^ t) * (HEADS_HERE * DH) + members[0] * DH
            out[at : at + width, :] = w_ref[pl.ds(pl.multiple_of(first, DH), width), :]
            at += width


def project_kernel(first, added, final, *refs):
    if final:
        *pieces, w_ref, token, out_hbm, plain, out, sems = refs
    else:
        *pieces, w_ref, token, out, plain = refs
    if added:
        *pieces, before = pieces
    back = regroup_matrix(True)
    depth = plain.shape[1]
    for b in range(plain.shape[0] // BLK):
        rows = slice(b * BLK, (b + 1) * BLK)
        x = jnp.concatenate([src[rows, :] for src in pieces], axis=1)
        plain[rows, :] = jnp.dot(back, x, preferred_element_type=F32).astype(BF16)
    tile = 512
    steps = out.shape[1] // tile

    def copy(step):
        cols = pl.ds(pl.multiple_of(step * tile, tile), tile)
        return pltpu.make_async_copy(out.at[:, cols], out_hbm.at[:, cols], sems.at[step])

    @pl.loop(0, steps)
    def _(step):
        cols = pl.ds(pl.multiple_of(step * tile, tile), tile)
        total = jnp.dot(
            plain[...], w_ref[first : first + depth, cols], preferred_element_type=F32
        )
        if added:
            total = total + before[:, cols]
        out[:, cols] = total.astype(out.dtype)
        if final:
            copy(step).start()

    if final:

        @pl.loop(0, steps)
        def _(step):
            copy(step).wait()


SMEM = pl.BlockSpec(memory_space=pltpu.SMEM)
VMEM = pl.BlockSpec(memory_space=pltpu.VMEM)
ANY = pl.BlockSpec(memory_space=pl.ANY)


def shape(*dims, dtype=BF16):
    return jax.ShapeDtypeStruct(dims, dtype)


def call(kernel, specs, outs, name, scratch=(), aliases={}, out_spec=VMEM):
    return pl.pallas_call(
        kernel,
        in_specs=specs,
        out_specs=jax.tree.map(lambda _: out_spec, outs),
        out_shape=outs,
        scratch_shapes=scratch,
        input_output_aliases=aliases,
        compiler_params=pltpu.CompilerParams(vmem_limit_bytes=VMEM_LIMIT),
        cost_estimate=pl.CostEstimate(flops=COST.get(name, 10**9), bytes_accessed=1, transcendentals=0),
        name=name,
    )


def body(queries, keys, values, offsets, out_weight):
    rows_here, width = queries.shape
    blocks = rows_here // BLK
    heads = width // DH
    slots = rows_here // RES
    piece = (slots, DH)
    regrouped = shape(heads, blocks, RES, SUB, DH)
    ctx_size = lax.axis_size("ctx")
    swap = [(i, i ^ 1) for i in range(ctx_size)]
    near = [(i, i ^ 2) for i in range(ctx_size)]
    far = [(i, i ^ 4) for i in range(ctx_size)]
    over = [[(i, i ^ t) for i in range(4)] for t in range(4)]

    kt, vt, kv3, *kv2 = call(
        prep_kv_kernel,
        [SMEM, VMEM, VMEM],
        [regrouped, regrouped, shape(heads, 2, *piece)]
        + [shape(len(members), 2, 2, *piece) for members in GROUPS],
        "prep_kv",
    )(offsets, keys, values)
    kv3_near = lax.ppermute(kv3, "ctx", near)
    qt, first, q23 = call(
        prep_q_kernel,
        [SMEM, VMEM, VMEM, VMEM],
        [regrouped, shape(8, *piece), shape(heads, 3, *piece)],
        "prep_q",
    )(offsets, queries, kt, vt)
    first = lax.ppermute(first, "ctx", swap)
    q23 = lax.ppermute(q23, "ctx", swap)

    state = shape(blocks, RES, SUB, DH, dtype=F32)

    def own(members, token):
        return call(
            functools.partial(own_kernel, members),
            [SMEM, VMEM, VMEM, VMEM, ANY],
            [state] * (2 * len(members)),
            "own%d" % members[0],
        )(offsets, qt, kt, vt, token)

    def lower(members, got, token):
        return call(
            functools.partial(lower_kernel, members),
            [SMEM] + [VMEM] * 4 + [ANY],
            [shape(len(members) * 4 + 1, *piece)] + [shape(4, *piece, dtype=F32)] * 2,
            "lower",
        )(offsets, got, qt, kt, vt, token)

    def partner(members, column, token, extra=(), turn=()):
        return call(
            functools.partial(partner_kernel, members, extra),
            [SMEM] + [VMEM] * 6 + [ANY] + [VMEM] * len(turn),
            shape(len(members) * 3 + len(extra) * 4 + 1, *piece),
            "partner%d" % members[0],
        )(offsets, kt, vt, q23, *column, token, *turn)

    def mine(members, rows, column, below, token):
        return call(
            functools.partial(mine_kernel, members),
            [SMEM] + [VMEM] * (len(rows) + 7) + [ANY] + [VMEM] * len(below),
            [state] * len(rows),
            "mine%d" % members[0],
            aliases={1 + i: i for i in range(len(rows))},
        )(offsets, *rows, qt, kt, vt, q23, *column, token, *below)

    def finished(members, rows, message, token, extra=()):
        dest = shape(rows_here // 4, len(members) * DH)
        return call(
            functools.partial(finish_kernel, members),
            [SMEM] + [VMEM] * (len(rows) + 1) + [ANY] + [VMEM] * len(extra),
            [dest] * 4 + [state] * len(rows),
            "finish%d" % members[0],
            aliases={1 + i: 4 + i for i in range(len(rows))},
        )(offsets, *rows, message, token, *extra)[:4]

    def project(first, pieces, before, token, final=False):
        model = out_weight.shape[1]
        total = shape(rows_here // 4, model, dtype=BF16 if final else F32)
        scratch = [pltpu.VMEM((rows_here // 4, sum(x.shape[1] for x in pieces)), BF16)]
        if final:
            scratch += [
                pltpu.VMEM((rows_here // 4, model), BF16),
                pltpu.SemaphoreType.DMA((model // 512,)),
            ]
        return call(
            functools.partial(project_kernel, first, len(before), final),
            [VMEM] * (len(pieces) + 1 + len(before)) + [ANY],
            total,
            "project%d" % first,
            scratch=scratch,
            out_spec=ANY if final else VMEM,
        )(*pieces, *before, weights, token)

    def both(members):
        cut = slice(members[0], members[-1] + 1)
        return jnp.stack([kv3[cut], kv3_near[cut]])

    def send(value, axis, pairs):
        return lax.ppermute(value, axis, pairs)

    group_a, group_b, group_c = GROUPS
    *rows_a, = own((0, 1), kv3)
    kv3_near, rows_a[1] = lax.optimization_barrier((kv3_near, rows_a[1]))
    far_a, kv2_a = lax.optimization_barrier((both(group_a), kv2[0]))
    rows_bc = own((2, 3), far_a)
    far_a, kv2_a = send(far_a, "ctx", far), send(kv2_a, "ctx", near)
    msg1, o1, s1 = lower((0, 1), first, rows_bc[0])
    turn = send(msg1, "ctx", swap)
    weights = call(weights_kernel, [VMEM, ANY], shape(*out_weight.shape), "weights")(
        out_weight, msg1
    )

    far_a, kv2_a, far_b, kv2_b, weights = lax.optimization_barrier(
        (far_a, kv2_a, both(group_b), kv2[1], weights)
    )
    far_b_now = far_b
    far_b, kv2_b = send(far_b, "ctx", far), send(kv2_b, "ctx", near)
    column_a = [kv2_a, kv3_near, far_a]
    msg_a = partner(group_a, column_a, far_b_now, (2,), (turn,))
    got_a = send(msg_a, "ctx", swap)
    rows_a = list(mine(group_a, rows_a, column_a, [turn], msg_a))

    far_b, kv2_b, far_c, kv2_c, rows_a[0] = lax.optimization_barrier(
        (far_b, kv2_b, both(group_c), kv2[2], rows_a[0])
    )
    column_b = [kv2_b, kv3_near, far_b]
    msg_b = partner(group_b, column_b, far_c)
    far_c, kv2_c = send(far_c, "ctx", far), send(kv2_c, "ctx", near)
    got_b = send(msg_b, "ctx", swap)
    rows_b = mine(group_b, rows_bc[:2], column_b, [], msg_b)
    rows_a = finished(group_a, rows_a, got_a, rows_b[0])
    a1, a2, a3 = (send(rows_a[t], "head", over[t]) for t in (1, 2, 3))

    column_c = [kv2_c, kv3_near, far_c]
    msg_c = partner(group_c, column_c, rows_a[0])
    got_c = send(msg_c, "ctx", swap)
    rows_b = finished(group_b, rows_b, got_b, msg_c, (got_a,))
    b1, b2, b3 = (send(rows_b[t], "head", over[t]) for t in (1, 2, 3))
    rows_c = mine(group_c, rows_bc[2:], column_c, [o1, s1], rows_b[0])
    half = project(0, [rows_a[0], a1, a2, a3], [], rows_c[0])
    rows_c = finished(group_c, rows_c, got_c, half)
    c1, c2, c3 = (send(rows_c[t], "head", over[t]) for t in (1, 2, 3))
    half = project(8 * DH, [rows_b[0], b1, b2, b3], [half], rows_c[0])
    return project(12 * DH, [rows_c[0], c1, c2, c3], [half], half, final=True)


def solution(mesh):
    placed = (P("ctx", "head"), P("ctx", "head"), P("ctx", "head"), P(), P())
    return jax.shard_map(
        body, mesh=mesh, in_specs=placed, out_specs=P(("ctx", "head"), None), check_vma=False
    )
```

time: 94.5 us -> 86 us (0.910)
  waiting for transfers between devices: 21.6 us -> 14.6 us
  Pallas kernels: 38.5 us -> 41.2 us
  starting transfers between devices: 28.5 us -> 25.9 us
  local copies, waits for them, and re-layouts: 4.97 us -> 3.69 us
    ppermute x1, waiting for transfers between devices: 7.06 us -> 0.01 us  [body(): kv3_near = lax.ppermute(kv3, 'ctx', near)]
    pallas_call x13 -> x18, Pallas kernels: 38.5 us -> 41.2 us  [the longest x2 11.5 us: own(): call(functools.partial(own_kernel, members), [SMEM, VMEM, VMEM, VMEM, ANY...]
    ppermute x14 -> x19, starting transfers between devices: 23.4 us -> 20.7 us  [send(): return lax.ppermute(value, axis, pairs)]
    unnamed x12, local copies, waits for them, and re-layouts: 4.91 us -> 3.63 us
    ppermute x14 -> x19, waiting for transfers between devices: 14.6 us -> 14.6 us  [send(): return lax.ppermute(value, axis, pairs)]
  transfers between devices with their start and end apart: 17 -> 22, of which waited for: 6 -> 7; matrix products, arithmetic and copies ran while one was open for 0% -> 0% of each run, Pallas kernels for 32% -> 43%
where the time goes in v3:
time: 86 us; the launch traced here: 85.8 us
  Pallas kernels  41.2 us (48%)
  starting transfers between devices  25.9 us (30%)
  waiting for transfers between devices  14.6 us (17%)
  local copies, waits for them, and re-layouts  3.69 us (4%)
    ppermute x19, starting transfers between devices, send(): return lax.ppermute(value, axis, pairs)  20.7 us
    ppermute x19, waiting for transfers between devices, send(): return lax.ppermute(value, axis, pairs)  14.6 us
    pallas_call x2, Pallas kernels, own(): call(functools.partial(own_kernel, members), [SMEM, VMEM, VMEM, VMEM, ANY...  11.5 us
    pallas_call x3, Pallas kernels, project(): call(functools.partial(project_kernel, first, len(before), final), [VMEM]...  6.93 us
    pallas_call x3, Pallas kernels, mine(): call(functools.partial(mine_kernel, members), [SMEM] + [VMEM] * (len(rows...  6.73 us
    pallas_call x3, Pallas kernels, partner(): call(functools.partial(partner_kernel, members, extra), [SMEM] + [VMEM] *...  6.44 us
    unnamed x12, local copies, waits for them, and re-layouts  3.63 us
    ppermute x1, starting transfers between devices, body(): kv3_near = lax.ppermute(kv3, 'ctx', near)  3.09 us
  transfers between devices with their start and end apart: 22, of which 7 were waited for; matrix products, arithmetic and copies ran while one was open for 0% of the time, Pallas kernels for 43%

profile of v3, /device:TPU:0, one launch (start us, length us, event | category | flops | bytes accessed | tf_op | source)
XLA Modules:
  0.0 85.8 jit_solution(4802900464507754215)
XLA Ops:
  0.8 1.4 %copy-done.2 = bf16[1536,512]{1,0:T(8,128)(2,1)S(1)} copy-done((bf16[1536,512]{1,0:T(8,128)(2,1)S(1)}, bf16[1536,512]{1,0:T(8,128)(2,1)}, u32[]{:S(2)}) %copy-start.2) | copy-done | bytes 1572888
  2.2 1.4 %copy-done.3 = bf16[1536,512]{1,0:T(8,128)(2,1)S(1)} copy-done((bf16[1536,512]{1,0:T(8,128)(2,1)S(1)}, bf16[1536,512]{1,0:T(8,128)(2,1)}, u32[]{:S(2)}) %copy-start.3) | copy-done | bytes 1572888
  3.6 1.7 %prep_kv.1 = (bf16[4,12,8,16,128]{4,3,2,1,0:T(8,128)(2,1)S(1)}, bf16[4,12,8,16,128]{4,3,2,1,0:T(8,128)(2,1)S(1)}, bf16[4,2,192,128]{3,2,1,0:T(8,128)(2,1)S(1)}, ...) custom-call(s32[3,16]{1,0:T(4,128)S(1)} %copy-done.1, ...), custom_call_target="tpu_custom_call" | custom-call | flops 1000000000 | bytes 1 | tf_op jit(solution)/shard_map/prep_kv/pallas_call | solution.py:520
  5.3 3.1 %collective-permute-start = (bf16[4,2,192,128]{3,2,1,0:T(8,128)(2,1)S(1)}, bf16[4,2,192,128]{3,2,1,0:T(8,128)(2,1)S(1)}, u32[]{:S(2)}, u32[]{:S(2)}) collective-permute-start(bf16[4,2,192,128]{3,2,1,0:T(8,128)(2,1)S(1)} %get-tuple-element.62.token), channel_id=1, source_target_pairs={{0,8},{4,12},{8,0},{12,4},{16,24},{20,28},{24,16},{28,20},{1,9},{5... | collective-permute-start | bytes 1179656 | tf_op jit(solution)/shard_map/ppermute | solution.py:527
  8.4 1.2 %prep_q.1 = (bf16[4,12,8,16,128]{4,3,2,1,0:T(8,128)(2,1)S(1)}, bf16[8,192,128]{2,1,0:T(8,128)(2,1)S(1)}, bf16[4,3,192,128]{3,2,1,0:T(8,128)(2,1)S(1)}) custom-call(s32[3,16]{1,0:T(4,128)S(1)} %copy-done.1, bf16[1536,512]{1,0:T(8,128)(2,1)S(1)} %copy-done, bf16[4,12,8,16,128]{4,3,2,1,0:T(8,128)(2,1)S(1)} %get-tuple-element.59.kt.refs_5_.refs_3_, ...), custom_call_target="tpu_custom_call" | custom-call | flops 1000000000 | bytes 1 | tf_op jit(solution)/shard_map/prep_q/pallas_call | solution.py:528
  9.6 1.6 %collective-permute-start.4 = (bf16[8,192,128]{2,1,0:T(8,128)(2,1)S(1)}, bf16[8,192,128]{2,1,0:T(8,128)(2,1)S(1)}, u32[]{:S(2)}, u32[]{:S(2)}) collective-permute-start(bf16[8,192,128]{2,1,0:T(8,128)(2,1)S(1)} %get-tuple-element.72), channel_id=1, source_target_pairs={{0,4},{4,0},{8,12},{12,8},{16,20},{20,16},{24,28},{28,24},{1,5},{5... | collective-permute-start | bytes 1179656 | tf_op jit(solution)/shard_map/ppermute | solution.py:534
  11.7 5.8 %own0.1 = (f32[12,8,16,128]{3,2,1,0:T(8,128)S(1)}, f32[12,8,16,128]{3,2,1,0:T(8,128)S(1)}, f32[12,8,16,128]{3,2,1,0:T(8,128)S(1)}, f32[12,8,16,128]{3,2,1,0:T(8,128)S(1)}) custom-call(s32[3,16]{1,0:T(4,128)S(1)} %copy-done.1, bf16[4,12,8,16,128]{4,3,2,1,0:T(8,128)(2,1)S(1)} %get-tuple-element.61.qt.refs_4_.refs_2_, ...), custom_call_target="tpu_custom_call" | custom-call | flops 1000000000 | bytes 1 | tf_op jit(solution)/shard_map/own0/pallas_call | solution.py:540
  17.6 1.7 %collective-permute-start.3 = (bf16[2,2,2,192,128]{4,3,2,1,0:T(8,128)(2,1)S(1)}, bf16[2,2,2,192,128]{4,3,2,1,0:T(8,128)(2,1)S(1)}, u32[]{:S(2)}, u32[]{:S(2)}) collective-permute-start(bf16[2,2,2,192,128]{4,3,2,1,0:T(8,128)(2,1)S(1)} %get-tuple-element.70), channel_id=1, source_target_pairs={{0,8},{4,12},{8,0},{12,4},{16,24},{20,28},{24,16},{28,20},{1,9},{5... | collective-permute-start | bytes 1179656 | tf_op jit(solution)/shard_map/ppermute | solution.py:605
  19.4 2.6 %collective-permute-start.2 = (bf16[2,2,2,192,128]{4,3,2,1,0:T(8,128)(2,1)S(1)}, bf16[2,2,2,192,128]{4,3,2,1,0:T(8,128)(2,1)S(1)}, u32[]{:S(2)}, u32[]{:S(2)}) collective-permute-start(bf16[2,2,2,192,128]{4,3,2,1,0:T(8,128)(2,1)S(1)} %pad_maximum_fusion.token), channel_id=1, source_target_pairs={{0,16},{4,20},{8,24},{12,28},{16,0},{20,4},{24,8},{28,12},{1,17},{... | collective-permute-start | bytes 1179656 | tf_op jit(solution)/shard_map/ppermute | solution.py:605
  22.0 5.7 %own2.1 = (f32[12,8,16,128]{3,2,1,0:T(8,128)S(1)}, f32[12,8,16,128]{3,2,1,0:T(8,128)S(1)}, f32[12,8,16,128]{3,2,1,0:T(8,128)S(1)}, f32[12,8,16,128]{3,2,1,0:T(8,128)S(1)}) custom-call(s32[3,16]{1,0:T(4,128)S(1)} %copy-done.1, bf16[4,12,8,16,128]{4,3,2,1,0:T(8,128)(2,1)S(1)} %get-tuple-element.61.qt.refs_4_.refs_2_, ...), custom_call_target="tpu_custom_call" | custom-call | flops 1000000000 | bytes 1 | tf_op jit(solution)/shard_map/own2/pallas_call | solution.py:540
  27.7 3.1 %lower.1 = (bf16[9,192,128]{2,1,0:T(8,128)(2,1)S(1)}, f32[4,192,128]{2,1,0:T(8,128)S(1)}, f32[4,192,128]{2,1,0:T(8,128)S(1)}) custom-call(s32[3,16]{1,0:T(4,128)S(1)} %copy-done.1, bf16[8,192,128]{2,1,0:T(8,128)(2,1)S(1)} %collective-permute-done.4.got, bf16[4,12,8,16,128]{4,3,2,1,0:T(8,128)(2,1)S(1)} %get-tuple-element.61.qt.refs_4_.refs_2_, ...), custom_call_target="tpu_custom_call" | custom-call | flops 1000000000 | bytes 1 | tf_op jit(solution)/shard_map/lower/pallas_call | solution.py:548
  32.0 4.3 %collective-permute-done.3.kv2.refs_8_ = bf16[2,2,2,192,128]{4,3,2,1,0:T(8,128)(2,1)S(1)} collective-permute-done((bf16[2,2,2,192,128]{4,3,2,1,0:T(8,128)(2,1)S(1)}, bf16[2,2,2,192,128]{4,3,2,1,0:T(8,128)(2,1)S(1)}, u32[]{:S(2)}, u32[]{:S(2)}) %collective-permute-start.3) | collective-permute-done | bytes 393248 | tf_op jit(solution)/shard_map/ppermute | solution.py:605
  36.3 2.3 %collective-permute-done.2.far.refs_10_ = bf16[2,2,2,192,128]{4,3,2,1,0:T(8,128)(2,1)S(1)} collective-permute-done((bf16[2,2,2,192,128]{4,3,2,1,0:T(8,128)(2,1)S(1)}, bf16[2,2,2,192,128]{4,3,2,1,0:T(8,128)(2,1)S(1)}, u32[]{:S(2)}, u32[]{:S(2)}) %collective-permute-start.2) | collective-permute-done | bytes 393248 | tf_op jit(solution)/shard_map/ppermute | solution.py:605
  38.9 2.7 %collective-permute-start.5 = (bf16[2,1,2,192,128]{4,3,2,1,0:T(8,128)(2,1)S(1)}, bf16[2,1,2,192,128]{4,3,2,1,0:T(8,128)(2,1)S(1)}, u32[]{:S(2)}, u32[]{:S(2)}) collective-permute-start(bf16[2,1,2,192,128]{4,3,2,1,0:T(8,128)(2,1)S(1)} %pad_maximum_fusion.1.token), channel_id=1, source_target_pairs={{0,16},{4,20},{8,24},{12,28},{16,0},{20,4},{24,8},{28,12},{1,17},{... | collective-permute-start | bytes 589832 | tf_op jit(solution)/shard_map/ppermute | solution.py:605
  42.4 3.3 %partner0.1.refs_11_ = bf16[11,192,128]{2,1,0:T(8,128)(2,1)S(1)} custom-call(s32[3,16]{1,0:T(4,128)S(1)} %copy-done.1, bf16[4,12,8,16,128]{4,3,2,1,0:T(8,128)(2,1)S(1)} %get-tuple-element.59.kt.refs_5_.refs_3_, bf16[4,12,8,16,128]{4,3,2,1,0:T(8,128)(2,1)S(1)} %get-tuple-element.60.vt.refs_6_.refs_4_, ...), custom_call_target="tpu_custom_call" | custom-call | flops 1000000000 | bytes 1 | tf_op jit(solution)/shard_map/partner0/pallas_call | solution.py:556
  45.6 1.6 %collective-permute-start.11 = (bf16[11,192,128]{2,1,0:T(8,128)(2,1)S(1)}, bf16[11,192,128]{2,1,0:T(8,128)(2,1)S(1)}, u32[]{:S(2)}, u32[]{:S(2)}) collective-permute-start(bf16[11,192,128]{2,1,0:T(8,128)(2,1)S(1)} %partner0.1.refs_11_), channel_id=1, source_target_pairs={{0,4},{4,0},{8,12},{12,8},{16,20},{20,16},{24,28},{28,24},{1,5},{5... | collective-permute-start | bytes 1622024 | tf_op jit(solution)/shard_map/ppermute | solution.py:605
  47.2 3.0 %mine0.1 = (f32[12,8,16,128]{3,2,1,0:T(8,128)S(1)}, f32[12,8,16,128]{3,2,1,0:T(8,128)S(1)}, f32[12,8,16,128]{3,2,1,0:T(8,128)S(1)}, f32[12,8,16,128]{3,2,1,0:T(8,128)S(1)}) custom-call(s32[3,16]{1,0:T(4,128)S(1)} %copy-done.1, ...), custom_call_target="tpu_custom_call", output_to_operand_aliasing={{0}: (1, {}), {1}: (2, {}), {2}: (3, {}), {3}: (4, {})} | custom-call | flops 10000000000 | bytes 1 | tf_op jit(solution)/shard_map/mine0/pallas_call | solution.py:564
  50.8 2.6 %collective-permute-start.9 = (bf16[2,1,2,192,128]{4,3,2,1,0:T(8,128)(2,1)S(1)}, bf16[2,1,2,192,128]{4,3,2,1,0:T(8,128)(2,1)S(1)}, u32[]{:S(2)}, u32[]{:S(2)}) collective-permute-start(bf16[2,1,2,192,128]{4,3,2,1,0:T(8,128)(2,1)S(1)} %pad_maximum_fusion.2.token), channel_id=1, source_target_pairs={{0,16},{4,20},{8,24},{12,28},{16,0},{20,4},{24,8},{28,12},{1,17},{... | collective-permute-start | bytes 589832 | tf_op jit(solution)/shard_map/ppermute | solution.py:605
  53.4 1.6 %partner2.1.refs_9_ = bf16[4,192,128]{2,1,0:T(8,128)(2,1)S(1)} custom-call(s32[3,16]{1,0:T(4,128)S(1)} %copy-done.1, bf16[4,12,8,16,128]{4,3,2,1,0:T(8,128)(2,1)S(1)} %get-tuple-element.59.kt.refs_5_.refs_3_, bf16[4,12,8,16,128]{4,3,2,1,0:T(8,128)(2,1)S(1)} %get-tuple-element.60.vt.refs_6_.refs_4_, ...), custom_call_target="tpu_custom_call" | custom-call | flops 1000000000 | bytes 1 | tf_op jit(solution)/shard_map/partner2/pallas_call | solution.py:556
  55.6 1.7 %mine2.1 = (f32[12,8,16,128]{3,2,1,0:T(8,128)S(1)}, f32[12,8,16,128]{3,2,1,0:T(8,128)S(1)}) custom-call(s32[3,16]{1,0:T(4,128)S(1)} %copy-done.1, f32[12,8,16,128]{3,2,1,0:T(8,128)S(1)} %get-tuple-element.73.token.refs_0_, f32[12,8,16,128]{3,2,1,0:T(8,128)S(1)} %get-tuple-element.87.refs_1_, ...), custom_call_target="tpu_custom_call", output_to_operand_aliasing={{0}: (1, {}), {1}: (2, {})} | custom-call | flops 1000000000 | bytes 1 | tf_op jit(solution)/shard_map/mine2/pallas_call | solution.py:564
  57.3 3.2 %collective-permute-done.11.refs_4_ = bf16[11,192,128]{2,1,0:T(8,128)(2,1)S(1)} collective-permute-done((bf16[11,192,128]{2,1,0:T(8,128)(2,1)S(1)}, bf16[11,192,128]{2,1,0:T(8,128)(2,1)S(1)}, u32[]{:S(2)}, u32[]{:S(2)}) %collective-permute-start.11) | collective-permute-done | bytes 540704 | tf_op jit(solution)/shard_map/ppermute | solution.py:605
  61.7 1.5 %collective-permute-start.14 = (bf16[384,256]{1,0:T(8,128)(2,1)S(1)}, bf16[384,256]{1,0:T(8,128)(2,1)S(1)}, u32[]{:S(2)}, u32[]{:S(2)}) collective-permute-start(bf16[384,256]{1,0:T(8,128)(2,1)S(1)} %get-tuple-element.103), channel_id=1, source_target_pairs={{0,2},{1,3},{2,0},{3,1},{4,6},{5,7},{6,4},{7,5},{8,10},{9,11},{10,... | collective-permute-start | bytes 589832 | tf_op jit(solution)/shard_map/ppermute | solution.py:605
  63.5 1.6 %partner3.1.refs_3_ = bf16[4,192,128]{2,1,0:T(8,128)(2,1)S(1)} custom-call(s32[3,16]{1,0:T(4,128)S(1)} %copy-done.1, bf16[4,12,8,16,128]{4,3,2,1,0:T(8,128)(2,1)S(1)} %get-tuple-element.59.kt.refs_5_.refs_3_, bf16[4,12,8,16,128]{4,3,2,1,0:T(8,128)(2,1)S(1)} %get-tuple-element.60.vt.refs_6_.refs_4_, ...), custom_call_target="tpu_custom_call" | custom-call | flops 1000000000 | bytes 1 | tf_op jit(solution)/shard_map/partner3/pallas_call | solution.py:556
  65.1 1.7 %collective-permute-start.12 = (bf16[4,192,128]{2,1,0:T(8,128)(2,1)S(1)}, bf16[4,192,128]{2,1,0:T(8,128)(2,1)S(1)}, u32[]{:S(2)}, u32[]{:S(2)}) collective-permute-start(bf16[4,192,128]{2,1,0:T(8,128)(2,1)S(1)} %partner3.1.refs_3_), channel_id=1, source_target_pairs={{0,4},{4,0},{8,12},{12,8},{16,20},{20,16},{24,28},{28,24},{1,5},{5... | collective-permute-start | bytes 589832 | tf_op jit(solution)/shard_map/ppermute | solution.py:605
  66.8 1.1 %finish2.1 = (bf16[384,128]{1,0:T(8,128)(2,1)S(1)}, bf16[384,128]{1,0:T(8,128)(2,1)S(1)}, bf16[384,128]{1,0:T(8,128)(2,1)S(1)}, bf16[384,128]{1,0:T(8,128)(2,1)S...) custom-call(s32[3,16]{1,0:T(4,128)S(1)} %copy-done.1, ...), custom_call_target="tpu_custom_call", output_to_operand_aliasing={{4}: (1, {}), {5}: (2, {})} | custom-call | flops 1000000000 | bytes 1 | tf_op jit(solution)/shard_map/finish2/pallas_call | solution.py:574
  68.1 2.0 %mine3.1 = (f32[12,8,16,128]{3,2,1,0:T(8,128)S(1)}, f32[12,8,16,128]{3,2,1,0:T(8,128)S(1)}) custom-call(s32[3,16]{1,0:T(4,128)S(1)} %copy-done.1, f32[12,8,16,128]{3,2,1,0:T(8,128)S(1)} %get-tuple-element.67.refs_0_, f32[12,8,16,128]{3,2,1,0:T(8,128)S(1)} %get-tuple-element.68.refs_1_, ...), custom_call_target="tpu_custom_call", output_to_operand_aliasing={{0}: (1, {}), {1}: (2, {})} | custom-call | flops 1000000000 | bytes 1 | tf_op jit(solution)/shard_map/mine3/pallas_call | solution.py:564
  70.1 1.6 %collective-permute-start.20 = (bf16[384,128]{1,0:T(8,128)(2,1)S(1)}, bf16[384,128]{1,0:T(8,128)(2,1)S(1)}, u32[]{:S(2)}, u32[]{:S(2)}) collective-permute-start(bf16[384,128]{1,0:T(8,128)(2,1)S(1)} %get-tuple-element.111), channel_id=1, source_target_pairs={{0,2},{1,3},{2,0},{3,1},{4,6},{5,7},{6,4},{7,5},{8,10},{9,11},{10,... | collective-permute-start | bytes 294920 | tf_op jit(solution)/shard_map/ppermute | solution.py:605
  72.7 2.7 %project0.1.refs_3_.refs_4_ = f32[384,2048]{1,0:T(8,128)S(1)} custom-call(bf16[384,256]{1,0:T(8,128)(2,1)S(1)} %get-tuple-element.96.token.refs_0_, bf16[384,256]{1,0:T(8,128)(2,1)S(1)} %collective-permute-done.13.refs_1_, bf16[384,256]{1,0:T(8,128)(2,1)S(1)} %collective-permute-done.14.refs_2_, bf16[384,256]{1,0:T(8,128)(2,1)S(1)} %collective-permute-done.15.refs_3_, ...), custom_call_target="tpu_custom_call" | custom-call | flops 1000000000 | bytes 1 | tf_op jit(solution)/shard_map/project0/pallas_call | solution.py:591
  76.6 1.4 %collective-permute-start.17 = (bf16[384,128]{1,0:T(8,128)(2,1)S(1)}, bf16[384,128]{1,0:T(8,128)(2,1)S(1)}, u32[]{:S(2)}, u32[]{:S(2)}) collective-permute-start(bf16[384,128]{1,0:T(8,128)(2,1)S(1)} %get-tuple-element.108), channel_id=1, source_target_pairs={{0,2},{1,3},{2,0},{3,1},{4,6},{5,7},{6,4},{7,5},{8,10},{9,11},{10,... | collective-permute-start | bytes 294920 | tf_op jit(solution)/shard_map/ppermute | solution.py:605
  78.2 1.7 %project1024.1.refs_4_.refs_6_ = f32[384,2048]{1,0:T(8,128)S(1)} custom-call(bf16[384,128]{1,0:T(8,128)(2,1)S(1)} %get-tuple-element.97.refs_9_.refs_0_, bf16[384,128]{1,0:T(8,128)(2,1)S(1)} %collective-permute-done.19.refs_1_, bf16[384,128]{1,0:T(8,128)(2,1)S(1)} %collective-permute-done.20.refs_2_, bf16[384,128]{1,0:T(8,128)(2,1)S(1)} %collective-permute-done.21.refs_3_, ...), custom_call_target="tpu_custom_call" | custom-call | flops 1000000000 | bytes 1 | tf_op jit(solution)/shard_map/project1024/pallas_call | solution.py:591
  80.0 2.1 %collective-permute-done.17.refs_2_ = bf16[384,128]{1,0:T(8,128)(2,1)S(1)} collective-permute-done((bf16[384,128]{1,0:T(8,128)(2,1)S(1)}, bf16[384,128]{1,0:T(8,128)(2,1)S(1)}, u32[]{:S(2)}, u32[]{:S(2)}) %collective-permute-start.17) | collective-permute-done | bytes 98336 | tf_op jit(solution)/shard_map/ppermute | solution.py:605
  83.2 2.5 %project1536.1 = bf16[384,2048]{1,0:T(8,128)(2,1)} custom-call(bf16[384,128]{1,0:T(8,128)(2,1)S(1)} %get-tuple-element.106.refs_6_.refs_0_, bf16[384,128]{1,0:T(8,128)(2,1)S(1)} %collective-permute-done.16.refs_1_, bf16[384,128]{1,0:T(8,128)(2,1)S(1)} %collective-permute-done.17.refs_2_, bf16[384,128]{1,0:T(8,128)(2,1)S(1)} %collective-permute-done.18.refs_3_, ...), custom_call_target="tpu_custom_call" | custom-call | flops 1000000000 | bytes 1 | tf_op jit(solution)/shard_map/project1536/pallas_call | solution.py:591
  (50 shorter events, 9.8 us)
Async XLA Ops:
  0.0 8.4 %copy-start = (bf16[1536,512]{1,0:T(8,128)(2,1)S(1)}, bf16[1536,512]{1,0:T(8,128)(2,1)}, u32[]{:S(2)}) copy-start(bf16[1536,512]{1,0:T(8,128)(2,1)} %q_ref.1) | copy-start | bytes 4718596
  0.0 0.8 copy-start.1
  0.8 1.4 %copy-start.2 = (bf16[1536,512]{1,0:T(8,128)(2,1)S(1)}, bf16[1536,512]{1,0:T(8,128)(2,1)}, u32[]{:S(2)}) copy-start(bf16[1536,512]{1,0:T(8,128)(2,1)} %k_ref.1) | copy-start | bytes 4718596
  2.2 1.4 %copy-start.3 = (bf16[1536,512]{1,0:T(8,128)(2,1)S(1)}, bf16[1536,512]{1,0:T(8,128)(2,1)}, u32[]{:S(2)}) copy-start(bf16[1536,512]{1,0:T(8,128)(2,1)} %v_ref.1) | copy-start | bytes 4718596
  5.3 12.2 %collective-permute-start = (bf16[4,2,192,128]{3,2,1,0:T(8,128)(2,1)S(1)}, bf16[4,2,192,128]{3,2,1,0:T(8,128)(2,1)S(1)}, u32[]{:S(2)}, u32[]{:S(2)}) collective-permute-start(bf16[4,2,192,128]{3,2,1,0:T(8,128)(2,1)S(1)} %get-tuple-element.62.token), channel_id=1, source_target_pairs={{0,8},{4,12},{8,0},{12,4},{16,24},{20,28},{24,16},{28,20},{1,9},{5... | collective-permute-start | bytes 1179656 | tf_op jit(solution)/shard_map/ppermute | solution.py:527
  9.6 18.1 %collective-permute-start.4 = (bf16[8,192,128]{2,1,0:T(8,128)(2,1)S(1)}, bf16[8,192,128]{2,1,0:T(8,128)(2,1)S(1)}, u32[]{:S(2)}, u32[]{:S(2)}) collective-permute-start(bf16[8,192,128]{2,1,0:T(8,128)(2,1)S(1)} %get-tuple-element.72), channel_id=1, source_target_pairs={{0,4},{4,0},{8,12},{12,8},{16,20},{20,16},{24,28},{28,24},{1,5},{5... | collective-permute-start | bytes 1179656 | tf_op jit(solution)/shard_map/ppermute | solution.py:534
  11.2 30.4 %collective-permute-start.1 = (bf16[4,3,192,128]{3,2,1,0:T(8,128)(2,1)S(1)}, bf16[4,3,192,128]{3,2,1,0:T(8,128)(2,1)S(1)}, u32[]{:S(2)}, u32[]{:S(2)}) collective-permute-start(bf16[4,3,192,128]{3,2,1,0:T(8,128)(2,1)S(1)} %get-tuple-element.69), channel_id=1, source_target_pairs={{0,4},{4,0},{8,12},{12,8},{16,20},{20,16},{24,28},{28,24},{1,5},{5... | collective-permute-start | bytes 1769480 | tf_op jit(solution)/shard_map/ppermute | solution.py:535
  11.7 19.6 %slice-start = ((s8[8388608]{0:T(1024)(128)(4,1)}), s8[4194304]{0:T(1024)(128)(4,1)S(1)}, s32[]{:S(2)}) async-start(s8[8388608]{0:T(1024)(128)(4,1)} %bitcast.12), calls=%async_computation | async-start | bytes 8388608
  17.6 13.7 %slice-start.1 = ((s8[8388608]{0:T(1024)(128)(4,1)}), s8[4194304]{0:T(1024)(128)(4,1)S(1)}, s32[]{:S(2)}) async-start(s8[8388608]{0:T(1024)(128)(4,1)} %bitcast.12), calls=%async_computation.1 | async-start | bytes 8388608
  17.6 18.6 %collective-permute-start.3 = (bf16[2,2,2,192,128]{4,3,2,1,0:T(8,128)(2,1)S(1)}, bf16[2,2,2,192,128]{4,3,2,1,0:T(8,128)(2,1)S(1)}, u32[]{:S(2)}, u32[]{:S(2)}) collective-permute-start(bf16[2,2,2,192,128]{4,3,2,1,0:T(8,128)(2,1)S(1)} %get-tuple-element.70), channel_id=1, source_target_pairs={{0,8},{4,12},{8,0},{12,4},{16,24},{20,28},{24,16},{28,20},{1,9},{5... | collective-permute-start | bytes 1179656 | tf_op jit(solution)/shard_map/ppermute | solution.py:605
  19.4 19.2 %collective-permute-start.2 = (bf16[2,2,2,192,128]{4,3,2,1,0:T(8,128)(2,1)S(1)}, bf16[2,2,2,192,128]{4,3,2,1,0:T(8,128)(2,1)S(1)}, u32[]{:S(2)}, u32[]{:S(2)}) collective-permute-start(bf16[2,2,2,192,128]{4,3,2,1,0:T(8,128)(2,1)S(1)} %pad_maximum_fusion.token), channel_id=1, source_target_pairs={{0,16},{4,20},{8,24},{12,28},{16,0},{20,4},{24,8},{28,12},{1,17},{... | collective-permute-start | bytes 1179656 | tf_op jit(solution)/shard_map/ppermute | solution.py:605
  30.8 11.6 %collective-permute-start.7 = (bf16[9,192,128]{2,1,0:T(8,128)(2,1)S(1)}, bf16[9,192,128]{2,1,0:T(8,128)(2,1)S(1)}, u32[]{:S(2)}, u32[]{:S(2)}) collective-permute-start(bf16[9,192,128]{2,1,0:T(8,128)(2,1)S(1)} %get-tuple-element.74.token), channel_id=1, source_target_pairs={{0,4},{4,0},{8,12},{12,8},{16,20},{20,16},{24,28},{28,24},{1,5},{5... | collective-permute-start | bytes 1327112 | tf_op jit(solution)/shard_map/ppermute | solution.py:605
  38.6 11.7 %collective-permute-start.6 = (bf16[1,2,2,192,128]{4,3,2,1,0:T(8,128)(2,1)S(1)}, bf16[1,2,2,192,128]{4,3,2,1,0:T(8,128)(2,1)S(1)}, u32[]{:S(2)}, u32[]{:S(2)}) collective-permute-start(bf16[1,2,2,192,128]{4,3,2,1,0:T(8,128)(2,1)S(1)} %get-tuple-element.76), channel_id=1, source_target_pairs={{0,8},{4,12},{8,0},{12,4},{16,24},{20,28},{24,16},{28,20},{1,9},{5... | collective-permute-start | bytes 589832 | tf_op jit(solution)/shard_map/ppermute | solution.py:605
  38.9 11.4 %collective-permute-start.5 = (bf16[2,1,2,192,128]{4,3,2,1,0:T(8,128)(2,1)S(1)}, bf16[2,1,2,192,128]{4,3,2,1,0:T(8,128)(2,1)S(1)}, u32[]{:S(2)}, u32[]{:S(2)}) collective-permute-start(bf16[2,1,2,192,128]{4,3,2,1,0:T(8,128)(2,1)S(1)} %pad_maximum_fusion.1.token), channel_id=1, source_target_pairs={{0,16},{4,20},{8,24},{12,28},{16,0},{20,4},{24,8},{28,12},{1,17},{... | collective-permute-start | bytes 589832 | tf_op jit(solution)/shard_map/ppermute | solution.py:605
  45.6 14.9 %collective-permute-start.11 = (bf16[11,192,128]{2,1,0:T(8,128)(2,1)S(1)}, bf16[11,192,128]{2,1,0:T(8,128)(2,1)S(1)}, u32[]{:S(2)}, u32[]{:S(2)}) collective-permute-start(bf16[11,192,128]{2,1,0:T(8,128)(2,1)S(1)} %partner0.1.refs_11_), channel_id=1, source_target_pairs={{0,4},{4,0},{8,12},{12,8},{16,20},{20,16},{24,28},{28,24},{1,5},{5... | collective-permute-start | bytes 1622024 | tf_op jit(solution)/shard_map/ppermute | solution.py:605
  50.3 12.9 %collective-permute-start.8 = (bf16[1,2,2,192,128]{4,3,2,1,0:T(8,128)(2,1)S(1)}, bf16[1,2,2,192,128]{4,3,2,1,0:T(8,128)(2,1)S(1)}, u32[]{:S(2)}, u32[]{:S(2)}) collective-permute-start(bf16[1,2,2,192,128]{4,3,2,1,0:T(8,128)(2,1)S(1)} %get-tuple-element.85), channel_id=1, source_target_pairs={{0,8},{4,12},{8,0},{12,4},{16,24},{20,28},{24,16},{28,20},{1,9},{5... | collective-permute-start | bytes 589832 | tf_op jit(solution)/shard_map/ppermute | solution.py:605
  50.8 12.7 %collective-permute-start.9 = (bf16[2,1,2,192,128]{4,3,2,1,0:T(8,128)(2,1)S(1)}, bf16[2,1,2,192,128]{4,3,2,1,0:T(8,128)(2,1)S(1)}, u32[]{:S(2)}, u32[]{:S(2)}) collective-permute-start(bf16[2,1,2,192,128]{4,3,2,1,0:T(8,128)(2,1)S(1)} %pad_maximum_fusion.2.token), channel_id=1, source_target_pairs={{0,16},{4,20},{8,24},{12,28},{16,0},{20,4},{24,8},{28,12},{1,17},{... | collective-permute-start | bytes 589832 | tf_op jit(solution)/shard_map/ppermute | solution.py:605
  55.0 11.8 %collective-permute-start.10 = (bf16[4,192,128]{2,1,0:T(8,128)(2,1)S(1)}, bf16[4,192,128]{2,1,0:T(8,128)(2,1)S(1)}, u32[]{:S(2)}, u32[]{:S(2)}) collective-permute-start(bf16[4,192,128]{2,1,0:T(8,128)(2,1)S(1)} %partner2.1.refs_9_), channel_id=1, source_target_pairs={{0,4},{4,0},{8,12},{12,8},{16,20},{20,16},{24,28},{28,24},{1,5},{5... | collective-permute-start | bytes 589832 | tf_op jit(solution)/shard_map/ppermute | solution.py:605
  61.6 8.5 %collective-permute-start.13 = (bf16[384,256]{1,0:T(8,128)(2,1)S(1)}, bf16[384,256]{1,0:T(8,128)(2,1)S(1)}, u32[]{:S(2)}, u32[]{:S(2)}) collective-permute-start(bf16[384,256]{1,0:T(8,128)(2,1)S(1)} %get-tuple-element.102), channel_id=1, source_target_pairs={{0,1},{1,0},{2,3},{3,2},{4,5},{5,4},{6,7},{7,6},{8,9},{9,8},{10,11... | collective-permute-start | bytes 589832 | tf_op jit(solution)/shard_map/ppermute | solution.py:605
  61.7 10.0 %collective-permute-start.14 = (bf16[384,256]{1,0:T(8,128)(2,1)S(1)}, bf16[384,256]{1,0:T(8,128)(2,1)S(1)}, u32[]{:S(2)}, u32[]{:S(2)}) collective-permute-start(bf16[384,256]{1,0:T(8,128)(2,1)S(1)} %get-tuple-element.103), channel_id=1, source_target_pairs={{0,2},{1,3},{2,0},{3,1},{4,6},{5,7},{6,4},{7,5},{8,10},{9,11},{10,... | collective-permute-start | bytes 589832 | tf_op jit(solution)/shard_map/ppermute | solution.py:605
  63.2 9.6 %collective-permute-start.15 = (bf16[384,256]{1,0:T(8,128)(2,1)S(1)}, bf16[384,256]{1,0:T(8,128)(2,1)S(1)}, u32[]{:S(2)}, u32[]{:S(2)}) collective-permute-start(bf16[384,256]{1,0:T(8,128)(2,1)S(1)} %get-tuple-element.104), channel_id=1, source_target_pairs={{0,3},{1,2},{2,1},{3,0},{4,7},{5,6},{6,5},{7,4},{8,11},{9,10},{10,... | collective-permute-start | bytes 589832 | tf_op jit(solution)/shard_map/ppermute | solution.py:605
  65.1 10.3 %collective-permute-start.12 = (bf16[4,192,128]{2,1,0:T(8,128)(2,1)S(1)}, bf16[4,192,128]{2,1,0:T(8,128)(2,1)S(1)}, u32[]{:S(2)}, u32[]{:S(2)}) collective-permute-start(bf16[4,192,128]{2,1,0:T(8,128)(2,1)S(1)} %partner3.1.refs_3_), channel_id=1, source_target_pairs={{0,4},{4,0},{8,12},{12,8},{16,20},{20,16},{24,28},{28,24},{1,5},{5... | collective-permute-start | bytes 589832 | tf_op jit(solution)/shard_map/ppermute | solution.py:605
  68.0 10.1 %collective-permute-start.19 = (bf16[384,128]{1,0:T(8,128)(2,1)S(1)}, bf16[384,128]{1,0:T(8,128)(2,1)S(1)}, u32[]{:S(2)}, u32[]{:S(2)}) collective-permute-start(bf16[384,128]{1,0:T(8,128)(2,1)S(1)} %get-tuple-element.110), channel_id=1, source_target_pairs={{0,1},{1,0},{2,3},{3,2},{4,5},{5,4},{6,7},{7,6},{8,9},{9,8},{10,11... | collective-permute-start | bytes 294920 | tf_op jit(solution)/shard_map/ppermute | solution.py:605
  70.1 8.1 %collective-permute-start.20 = (bf16[384,128]{1,0:T(8,128)(2,1)S(1)}, bf16[384,128]{1,0:T(8,128)(2,1)S(1)}, u32[]{:S(2)}, u32[]{:S(2)}) collective-permute-start(bf16[384,128]{1,0:T(8,128)(2,1)S(1)} %get-tuple-element.111), channel_id=1, source_target_pairs={{0,2},{1,3},{2,0},{3,1},{4,6},{5,7},{6,4},{7,5},{8,10},{9,11},{10,... | collective-permute-start | bytes 294920 | tf_op jit(solution)/shard_map/ppermute | solution.py:605
  71.7 6.5 %collective-permute-start.21 = (bf16[384,128]{1,0:T(8,128)(2,1)S(1)}, bf16[384,128]{1,0:T(8,128)(2,1)S(1)}, u32[]{:S(2)}, u32[]{:S(2)}) collective-permute-start(bf16[384,128]{1,0:T(8,128)(2,1)S(1)} %get-tuple-element.112), channel_id=1, source_target_pairs={{0,3},{1,2},{2,1},{3,0},{4,7},{5,6},{6,5},{7,4},{8,11},{9,10},{10,... | collective-permute-start | bytes 294920 | tf_op jit(solution)/shard_map/ppermute | solution.py:605
  76.3 3.7 %collective-permute-start.16 = (bf16[384,128]{1,0:T(8,128)(2,1)S(1)}, bf16[384,128]{1,0:T(8,128)(2,1)S(1)}, u32[]{:S(2)}, u32[]{:S(2)}) collective-permute-start(bf16[384,128]{1,0:T(8,128)(2,1)S(1)} %get-tuple-element.107), channel_id=1, source_target_pairs={{0,1},{1,0},{2,3},{3,2},{4,5},{5,4},{6,7},{7,6},{8,9},{9,8},{10,11... | collective-permute-start | bytes 294920 | tf_op jit(solution)/shard_map/ppermute | solution.py:605
  76.6 5.5 %collective-permute-start.17 = (bf16[384,128]{1,0:T(8,128)(2,1)S(1)}, bf16[384,128]{1,0:T(8,128)(2,1)S(1)}, u32[]{:S(2)}, u32[]{:S(2)}) collective-permute-start(bf16[384,128]{1,0:T(8,128)(2,1)S(1)} %get-tuple-element.108), channel_id=1, source_target_pairs={{0,2},{1,3},{2,0},{3,1},{4,6},{5,7},{6,4},{7,5},{8,10},{9,11},{10,... | collective-permute-start | bytes 294920 | tf_op jit(solution)/shard_map/ppermute | solution.py:605
  78.1 5.1 %collective-permute-start.18 = (bf16[384,128]{1,0:T(8,128)(2,1)S(1)}, bf16[384,128]{1,0:T(8,128)(2,1)S(1)}, u32[]{:S(2)}, u32[]{:S(2)}) collective-permute-start(bf16[384,128]{1,0:T(8,128)(2,1)S(1)} %get-tuple-element.109), channel_id=1, source_target_pairs={{0,3},{1,2},{2,1},{3,0},{4,7},{5,6},{6,5},{7,4},{8,11},{9,10},{10,... | collective-permute-start | bytes 294920 | tf_op jit(solution)/shard_map/ppermute | solution.py:605

commit v4 on v3

--- a/solution.py
+++ b/solution.py
@@ -10,7 +10,8 @@
 
 DH = 128
 HEADS_HERE = 4
-GROUPS = ((0, 1), (2,), (3,))
+GROUPS = ((0, 1), (2, 3))
+PIECES = ((0, 1), (2,), (3,))
 RES = 8
 SUB = 16
 BLK = RES * SUB
@@ -21,7 +22,7 @@
 VMEM_LIMIT = 20 * 1024 * 1024
 
 
-COST = {'mine0': 10**10}
+COST = {'mine0': 10**10, 'partner2': 10**10, 'lower': 3 * 10**9}
 
 
 def iota(shape, dim):
@@ -300,6 +301,22 @@
         )
 
 
+def last_kernel(off_ref, turn, kt, vt, token, msg):
+    msg[...] = jnp.zeros(msg.shape, BF16)
+
+    @pl.when(lax.axis_index("ctx") % 2 == 0)
+    def _():
+        shift = shift_of(off_ref, 1, 2)
+        attend_all(
+            pair_tasks(
+                lambda: [turn[j] for j in range(RES // 2)],
+                lambda: rows_of(kt.at[2], 1, shift),
+                lambda: rows_of(vt.at[2], 1, shift),
+                lambda j, o, s: put_message(msg, j, o, s, 2),
+            )
+        )
+
+
 def level_blocks(off_ref, level, head, n, q23, kt, vt, kv2, near, far):
     ctx = lax.axis_index("ctx")
     z = ctx // 2
@@ -327,33 +344,29 @@
     return whole, blocks, shift, count, rows
 
 
-def partner_kernel(heads, extra, off_ref, kt, vt, q23, kv2, near, far, token, *refs):
-    *turn, msg = refs
+def partner_kernel(heads, off_ref, kt, vt, q23, kv2, near, far, token, *msgs):
     later = jnp.where(lax.axis_index("ctx") % 2 == 0, 0.0, NEG)
-    msg[msg.shape[0] - 1] = jnp.zeros(msg.shape[1:], BF16)
-    tasks, place = [], 0
-    for level in (2, 3):
-        for n, head in enumerate(heads):
-            _, blocks, _, count, rows = level_blocks(
-                off_ref, level, head, n, q23, kt, vt, kv2, near, far
-            )
-            first = 0 if level == 2 else 2
-            tasks.append(
-                (
-                    lambda h=head, f=first, c=count, r=rows: q23[h, f : f + c].reshape(c * r, DH),
-                    lambda blocks=blocks: blocks(later),
-                    lambda o, s, p=place, c=count: put_message(msg, p, o, s, c),
-                )
-            )
-            place += count
-    for head in extra:
-        shift = shift_of(off_ref, 1, head)
-        tasks += pair_tasks(
-            lambda: [turn[0][j] for j in range(RES // 2)],
-            lambda shift=shift, head=head: rows_of(kt.at[head], 1, shift),
-            lambda shift=shift, head=head: rows_of(vt.at[head], 1, shift),
-            lambda j, o, s, p=place: put_message(msg, p + j, o, s, 2),
-        )
+    tasks = []
+    for msg in msgs:
+        msg[msg.shape[0] - 1] = jnp.zeros(msg.shape[1:], BF16)
+    places = [0] * len(msgs)
+    order = [(level, n) for level in (2, 3) for n in range(len(heads))]
+    if len(msgs) > 1:
+        order.sort(key=lambda item: item[1])
+    for level, n in order:
+        head, which = heads[n], n % len(msgs)
+        _, blocks, _, count, rows = level_blocks(
+            off_ref, level, head, n, q23, kt, vt, kv2, near, far
+        )
+        first = 0 if level == 2 else 2
+        tasks.append(
+            (
+                lambda h=head, f=first, c=count, r=rows: q23[h, f : f + c].reshape(c * r, DH),
+                lambda blocks=blocks: blocks(later),
+                lambda o, s, m=msgs[which], p=places[which], c=count: put_message(m, p, o, s, c),
+            )
+        )
+        places[which] += count
     attend_all(tasks)
 
 
@@ -366,7 +379,7 @@
         add_rows(out, lse, at, (part, jnp.broadcast_to(stat, part.shape)))
 
 
-def mine_kernel(heads, off_ref, *refs):
+def mine_kernel(heads, which, off_ref, *refs):
     number = len(heads)
     refs = refs[2 * number :]
     (qt, kt, vt, q23, kv2, near, far, token), refs = refs[:8], refs[8:]
@@ -388,27 +401,26 @@
             tasks.append(
                 (
                     lambda whole=whole: whole(qt),
-                    lambda blocks=blocks, t=triangle: blocks(t),
+                    lambda blocks=blocks, t=triangle: blocks(t)[which],
                     put,
                 )
             )
     attend_all(tasks)
     for n, head in enumerate(heads):
-        if len(lower) == 1:
-            add_lower(off_ref, head, lower[0], n * (RES // 2), state[2 * n], state[2 * n + 1])
-        elif lower:
+        if lower and head == 3:
             for j in range(RES // 2):
                 at = (slice(None), shift_of(off_ref, 1, head) + 2 * j)
                 add_rows(state[2 * n], state[2 * n + 1], at, (lower[0][j], lower[1][j]))
 
 
-def finish_kernel(heads, off_ref, *refs):
+def finish_kernel(heads, stacked, off_ref, *refs):
     number = len(heads)
     refs = refs[2 * number :]
-    msg, token, *extra = refs[: -4 - 2 * number]
+    msg, token, *below = refs[: -4 - 2 * number]
     dests, state = refs[-4 - 2 * number : -2 * number], refs[-2 * number :]
-    if extra:
-        add_lower(off_ref, heads[0], extra[0], 6, *state)
+    for n, head in enumerate(heads):
+        if below:
+            add_lower(off_ref, head, below[0], n * (RES // 2), state[2 * n], state[2 * n + 1])
     place = 0
     for level in (2, 3):
         for n, head in enumerate(heads):
@@ -425,6 +437,8 @@
                 place += 1
     mine = lax.axis_index("head")
     per = state[0].shape[0] // 4
+    if stacked:
+        dests = (dests[0], dests[1], dests[2].at[0], dests[2].at[1])
     for t, dest in enumerate(dests):
         for n in range(number):
             x = state[2 * n][pl.ds((mine ^ t) * per, per)].reshape(per * BLK, DH)
@@ -434,7 +448,7 @@
 def weights_kernel(w_ref, token, out):
     mine = lax.axis_index("head")
     at = 0
-    for members in GROUPS:
+    for members in PIECES:
         width = len(members) * DH
         for t in range(4):
             first = (mine ^ t) * (HEADS_HERE * DH) + members[0] * DH
@@ -453,7 +467,9 @@
     depth = plain.shape[1]
     for b in range(plain.shape[0] // BLK):
         rows = slice(b * BLK, (b + 1) * BLK)
-        x = jnp.concatenate([src[rows, :] for src in pieces], axis=1)
+        x = jnp.concatenate(
+            [src[0, rows, :] if len(src.shape) == 3 else src[rows, :] for src in pieces], axis=1
+        )
         plain[rows, :] = jnp.dot(back, x, preferred_element_type=F32).astype(BF16)
     tile = 512
     steps = out.shape[1] // tile
@@ -532,7 +548,6 @@
         "prep_q",
     )(offsets, queries, kt, vt)
     first = lax.ppermute(first, "ctx", swap)
-    q23 = lax.ppermute(q23, "ctx", swap)
 
     state = shape(blocks, RES, SUB, DH, dtype=F32)
 
@@ -552,37 +567,39 @@
             "lower",
         )(offsets, got, qt, kt, vt, token)
 
-    def partner(members, column, token, extra=(), turn=()):
+    def partner(members, column, token, messages):
         return call(
-            functools.partial(partner_kernel, members, extra),
-            [SMEM] + [VMEM] * 6 + [ANY] + [VMEM] * len(turn),
-            shape(len(members) * 3 + len(extra) * 4 + 1, *piece),
+            functools.partial(partner_kernel, members),
+            [SMEM] + [VMEM] * 6 + [ANY],
+            [shape(len(members) // messages * 3 + 1, *piece)] * messages,
             "partner%d" % members[0],
-        )(offsets, kt, vt, q23, *column, token, *turn)
-
-    def mine(members, rows, column, below, token):
+        )(offsets, kt, vt, q23, *column, token)
+
+    def mine(members, rows, column, below, token, which=slice(None), name="mine"):
         return call(
-            functools.partial(mine_kernel, members),
+            functools.partial(mine_kernel, members, which),
             [SMEM] + [VMEM] * (len(rows) + 7) + [ANY] + [VMEM] * len(below),
             [state] * len(rows),
-            "mine%d" % members[0],
+            name + "%d" % members[0],
             aliases={1 + i: i for i in range(len(rows))},
         )(offsets, *rows, qt, kt, vt, q23, *column, token, *below)
 
-    def finished(members, rows, message, token, extra=()):
+    def finished(members, rows, message, token, *below):
         dest = shape(rows_here // 4, len(members) * DH)
+        stacked = members != PIECES[-1]
+        dests = [dest, dest, shape(2, *dest.shape), shape(8, DH)] if stacked else [dest] * 4
         return call(
-            functools.partial(finish_kernel, members),
-            [SMEM] + [VMEM] * (len(rows) + 1) + [ANY] + [VMEM] * len(extra),
-            [dest] * 4 + [state] * len(rows),
+            functools.partial(finish_kernel, members, stacked),
+            [SMEM] + [VMEM] * (len(rows) + 1) + [ANY] + [VMEM] * len(below),
+            dests + [state] * len(rows),
             "finish%d" % members[0],
             aliases={1 + i: 4 + i for i in range(len(rows))},
-        )(offsets, *rows, message, token, *extra)[:4]
+        )(offsets, *rows, message, token, *below)[:4]
 
     def project(first, pieces, before, token, final=False):
         model = out_weight.shape[1]
         total = shape(rows_here // 4, model, dtype=BF16 if final else F32)
-        scratch = [pltpu.VMEM((rows_here // 4, sum(x.shape[1] for x in pieces)), BF16)]
+        scratch = [pltpu.VMEM((rows_here // 4, sum(x.shape[-1] for x in pieces)), BF16)]
         if final:
             scratch += [
                 pltpu.VMEM((rows_here // 4, model), BF16),
@@ -604,13 +621,14 @@
     def send(value, axis, pairs):
         return lax.ppermute(value, axis, pairs)
 
-    group_a, group_b, group_c = GROUPS
+    group_a, group_b = GROUPS
     *rows_a, = own((0, 1), kv3)
     kv3_near, rows_a[1] = lax.optimization_barrier((kv3_near, rows_a[1]))
-    far_a, kv2_a = lax.optimization_barrier((both(group_a), kv2[0]))
-    rows_bc = own((2, 3), far_a)
+    far_a, kv2_a, q23 = lax.optimization_barrier((both(group_a), kv2[0], q23))
+    rows_b = own((2, 3), far_a)
     far_a, kv2_a = send(far_a, "ctx", far), send(kv2_a, "ctx", near)
-    msg1, o1, s1 = lower((0, 1), first, rows_bc[0])
+    q23 = send(q23, "ctx", swap)
+    msg1, o1, s1 = lower((0, 1), first, rows_b[0])
     turn = send(msg1, "ctx", swap)
     weights = call(weights_kernel, [VMEM, ANY], shape(*out_weight.shape), "weights")(
         out_weight, msg1
@@ -619,35 +637,35 @@
     far_a, kv2_a, far_b, kv2_b, weights = lax.optimization_barrier(
         (far_a, kv2_a, both(group_b), kv2[1], weights)
     )
-    far_b_now = far_b
+    ready = far_b
     far_b, kv2_b = send(far_b, "ctx", far), send(kv2_b, "ctx", near)
     column_a = [kv2_a, kv3_near, far_a]
-    msg_a = partner(group_a, column_a, far_b_now, (2,), (turn,))
+    (msg_a,) = partner(group_a, column_a, ready, 1)
     got_a = send(msg_a, "ctx", swap)
-    rows_a = list(mine(group_a, rows_a, column_a, [turn], msg_a))
-
-    far_b, kv2_b, far_c, kv2_c, rows_a[0] = lax.optimization_barrier(
-        (far_b, kv2_b, both(group_c), kv2[2], rows_a[0])
-    )
+    rows_a = list(mine(group_a, rows_a, column_a, [], msg_a))
+    msg1c = call(
+        last_kernel, [SMEM] + [VMEM] * 3 + [ANY], shape(RES // 2 + 1, *piece), "last"
+    )(offsets, turn, kt, vt, rows_a[0])
+    got1c = send(msg1c, "ctx", swap)
+    rows_a = finished(group_a, rows_a, got_a, msg1c, turn)
+    a1, a23 = send(rows_a[1], "head", over[1]), send(rows_a[2], "head", over[2])
+
     column_b = [kv2_b, kv3_near, far_b]
-    msg_b = partner(group_b, column_b, far_c)
-    far_c, kv2_c = send(far_c, "ctx", far), send(kv2_c, "ctx", near)
-    got_b = send(msg_b, "ctx", swap)
-    rows_b = mine(group_b, rows_bc[:2], column_b, [], msg_b)
-    rows_a = finished(group_a, rows_a, got_a, rows_b[0])
-    a1, a2, a3 = (send(rows_a[t], "head", over[t]) for t in (1, 2, 3))
-
-    column_c = [kv2_c, kv3_near, far_c]
-    msg_c = partner(group_c, column_c, rows_a[0])
-    got_c = send(msg_c, "ctx", swap)
-    rows_b = finished(group_b, rows_b, got_b, msg_c, (got_a,))
-    b1, b2, b3 = (send(rows_b[t], "head", over[t]) for t in (1, 2, 3))
-    rows_c = mine(group_c, rows_bc[2:], column_c, [o1, s1], rows_b[0])
-    half = project(0, [rows_a[0], a1, a2, a3], [], rows_c[0])
-    rows_c = finished(group_c, rows_c, got_c, half)
-    c1, c2, c3 = (send(rows_c[t], "head", over[t]) for t in (1, 2, 3))
-    half = project(8 * DH, [rows_b[0], b1, b2, b3], [half], rows_c[0])
-    return project(12 * DH, [rows_c[0], c1, c2, c3], [half], half, final=True)
+    msg_b, msg_c = partner(group_b, column_b, rows_a[0], 2)
+    got_b, got_c = send(msg_b, "ctx", swap), send(msg_c, "ctx", swap)
+    rows_b = mine(group_b, rows_b, column_b, [o1, s1], msg_c)
+    a23, *rows_b = lax.optimization_barrier((a23, *rows_b))
+    a3 = send(a23[1], "head", over[1])
+    rows_b, rows_c = rows_b[:2], rows_b[2:]
+    rows_b = finished((2,), rows_b, got_b, rows_c[0], got1c)
+    b1, b23 = send(rows_b[1], "head", over[1]), send(rows_b[2], "head", over[2])
+    rows_c = finished((3,), rows_c, got_c, rows_b[0])
+    c2, c3, c1 = (send(rows_c[t], "head", over[t]) for t in (2, 3, 1))
+    half = project(0, [rows_a[0], a1, a23, a3], [], rows_c[0])
+    b23, half = lax.optimization_barrier((b23, half))
+    b3 = send(b23[1], "head", over[1])
+    half = project(8 * DH, [rows_b[0], b1, b23, b3, rows_c[0], c1], [half], half)
+    return project(14 * DH, [c2, c3], [half], half, final=True)
 
 
 def solution(mesh):

time: 86 us -> 83.9 us (0.976)
  starting transfers between devices: 25.9 us -> 24.1 us
    ppermute x19, starting transfers between devices: 20.7 us -> 19.4 us  [send(): return lax.ppermute(value, axis, pairs)]
    pallas_call x9 -> x8, Pallas kernels: 16.2 us -> 16.1 us  [the longest x2 5.26 us: mine(): call(functools.partial(mine_kernel, members, which), [SMEM] + [VMEM] * (l...]
  transfers between devices with their start and end apart: 22 -> 21, of which waited for: 7 -> 9; matrix products, arithmetic and copies ran while one was open for 0% -> 0% of each run, Pallas kernels for 43% -> 45%
where the time goes in v4:
time: 83.9 us; the launch traced here: 83.7 us
  Pallas kernels  41.1 us (49%)
  starting transfers between devices  24.1 us (29%)
  waiting for transfers between devices  14.3 us (17%)
  local copies, waits for them, and re-layouts  3.71 us (4%)
    ppermute x19, starting transfers between devices, send(): return lax.ppermute(value, axis, pairs)  19.4 us
    ppermute x19, waiting for transfers between devices, send(): return lax.ppermute(value, axis, pairs)  13.8 us
    pallas_call x2, Pallas kernels, own(): call(functools.partial(own_kernel, members), [SMEM, VMEM, VMEM, VMEM, ANY...  11.6 us
    pallas_call x3, Pallas kernels, project(): call(functools.partial(project_kernel, first, len(before), final), [VMEM]...  6.94 us
    pallas_call x2, Pallas kernels, mine(): call(functools.partial(mine_kernel, members, which), [SMEM] + [VMEM] * (l...  5.26 us
    pallas_call x2, Pallas kernels, partner(): call(functools.partial(partner_kernel, members), [SMEM] + [VMEM] * 6 + [A...  4.68 us
    pallas_call x3, Pallas kernels, finished(): call(functools.partial(finish_kernel, members, stacked), [SMEM] + [VMEM]...  4.07 us
    unnamed x12, local copies, waits for them, and re-layouts  3.63 us
  transfers between devices with their start and end apart: 21, of which 9 were waited for; matrix products, arithmetic and copies ran while one was open for 0% of the time, Pallas kernels for 45%

profile of v4, /device:TPU:0, one launch (start us, length us, event | category | flops | bytes accessed | tf_op | source)
XLA Modules:
  0.0 83.7 jit_solution(778352712011902037)
XLA Ops:
  0.8 1.4 %copy-done.2 = bf16[1536,512]{1,0:T(8,128)(2,1)S(1)} copy-done((bf16[1536,512]{1,0:T(8,128)(2,1)S(1)}, bf16[1536,512]{1,0:T(8,128)(2,1)}, u32[]{:S(2)}) %copy-start.2) | copy-done | bytes 1572888
  2.2 1.4 %copy-done.3 = bf16[1536,512]{1,0:T(8,128)(2,1)S(1)} copy-done((bf16[1536,512]{1,0:T(8,128)(2,1)S(1)}, bf16[1536,512]{1,0:T(8,128)(2,1)}, u32[]{:S(2)}) %copy-start.3) | copy-done | bytes 1572888
  3.6 1.7 %prep_kv.1 = (bf16[4,12,8,16,128]{4,3,2,1,0:T(8,128)(2,1)S(1)}, bf16[4,12,8,16,128]{4,3,2,1,0:T(8,128)(2,1)S(1)}, bf16[4,2,192,128]{3,2,1,0:T(8,128)(2,1)S(1)}, ...) custom-call(s32[3,16]{1,0:T(4,128)S(1)} %copy-done.1, bf16[1536,512]{1,0:T(8,128)(2,1)S(1)} %copy-done.2, ...), custom_call_target="tpu_custom_call" | custom-call | flops 1000000000 | bytes 1 | tf_op jit(solution)/shard_map/prep_kv/pallas_call | solution.py:536
  5.3 3.1 %collective-permute-start = (bf16[4,2,192,128]{3,2,1,0:T(8,128)(2,1)S(1)}, bf16[4,2,192,128]{3,2,1,0:T(8,128)(2,1)S(1)}, u32[]{:S(2)}, u32[]{:S(2)}) collective-permute-start(bf16[4,2,192,128]{3,2,1,0:T(8,128)(2,1)S(1)} %get-tuple-element.64.token), channel_id=1, source_target_pairs={{0,8},{4,12},{8,0},{12,4},{16,24},{20,28},{24,16},{28,20},{1,9},{5... | collective-permute-start | bytes 1179656 | tf_op jit(solution)/shard_map/ppermute | solution.py:543
  8.4 1.2 %prep_q.1 = (bf16[4,12,8,16,128]{4,3,2,1,0:T(8,128)(2,1)S(1)}, bf16[8,192,128]{2,1,0:T(8,128)(2,1)S(1)}, bf16[4,3,192,128]{3,2,1,0:T(8,128)(2,1)S(1)}) custom-call(s32[3,16]{1,0:T(4,128)S(1)} %copy-done.1, bf16[1536,512]{1,0:T(8,128)(2,1)S(1)} %copy-done, bf16[4,12,8,16,128]{4,3,2,1,0:T(8,128)(2,1)S(1)} %get-tuple-element.61.kt.refs_5_, ...), custom_call_target="tpu_custom_call" | custom-call | flops 1000000000 | bytes 1 | tf_op jit(solution)/shard_map/prep_q/pallas_call | solution.py:544
  9.6 1.6 %collective-permute-start.4 = (bf16[8,192,128]{2,1,0:T(8,128)(2,1)S(1)}, bf16[8,192,128]{2,1,0:T(8,128)(2,1)S(1)}, u32[]{:S(2)}, u32[]{:S(2)}) collective-permute-start(bf16[8,192,128]{2,1,0:T(8,128)(2,1)S(1)} %get-tuple-element.77), channel_id=1, source_target_pairs={{0,4},{4,0},{8,12},{12,8},{16,20},{20,16},{24,28},{28,24},{1,5},{5... | collective-permute-start | bytes 1179656 | tf_op jit(solution)/shard_map/ppermute | solution.py:550
  11.2 5.8 %own0.1 = (f32[12,8,16,128]{3,2,1,0:T(8,128)S(1)}, f32[12,8,16,128]{3,2,1,0:T(8,128)S(1)}, f32[12,8,16,128]{3,2,1,0:T(8,128)S(1)}, f32[12,8,16,128]{3,2,1,0:T(8,128)S(1)}) custom-call(s32[3,16]{1,0:T(4,128)S(1)} %copy-done.1, bf16[4,12,8,16,128]{4,3,2,1,0:T(8,128)(2,1)S(1)} %get-tuple-element.63.qt.refs_4_, ...), custom_call_target="tpu_custom_call" | custom-call | flops 1000000000 | bytes 1 | tf_op jit(solution)/shard_map/own0/pallas_call | solution.py:555
  17.6 2.8 %collective-permute-start.2 = (bf16[2,2,2,192,128]{4,3,2,1,0:T(8,128)(2,1)S(1)}, bf16[2,2,2,192,128]{4,3,2,1,0:T(8,128)(2,1)S(1)}, u32[]{:S(2)}, u32[]{:S(2)}) collective-permute-start(bf16[2,2,2,192,128]{4,3,2,1,0:T(8,128)(2,1)S(1)} %pad_maximum_fusion.token), channel_id=1, source_target_pairs={{0,16},{4,20},{8,24},{12,28},{16,0},{20,4},{24,8},{28,12},{1,17},{... | collective-permute-start | bytes 1179656 | tf_op jit(solution)/shard_map/ppermute | solution.py:622
  20.4 1.6 %collective-permute-start.3 = (bf16[2,2,2,192,128]{4,3,2,1,0:T(8,128)(2,1)S(1)}, bf16[2,2,2,192,128]{4,3,2,1,0:T(8,128)(2,1)S(1)}, u32[]{:S(2)}, u32[]{:S(2)}) collective-permute-start(bf16[2,2,2,192,128]{4,3,2,1,0:T(8,128)(2,1)S(1)} %get-tuple-element.75), channel_id=1, source_target_pairs={{0,8},{4,12},{8,0},{12,4},{16,24},{20,28},{24,16},{28,20},{1,9},{5... | collective-permute-start | bytes 1179656 | tf_op jit(solution)/shard_map/ppermute | solution.py:622
  22.0 1.5 %collective-permute-start.1 = (bf16[4,3,192,128]{3,2,1,0:T(8,128)(2,1)S(1)}, bf16[4,3,192,128]{3,2,1,0:T(8,128)(2,1)S(1)}, u32[]{:S(2)}, u32[]{:S(2)}) collective-permute-start(bf16[4,3,192,128]{3,2,1,0:T(8,128)(2,1)S(1)} %get-tuple-element.73), channel_id=1, source_target_pairs={{0,4},{4,0},{8,12},{12,8},{16,20},{20,16},{24,28},{28,24},{1,5},{5... | collective-permute-start | bytes 1769480 | tf_op jit(solution)/shard_map/ppermute | solution.py:622
  23.5 5.8 %own2.1 = (f32[12,8,16,128]{3,2,1,0:T(8,128)S(1)}, f32[12,8,16,128]{3,2,1,0:T(8,128)S(1)}, f32[12,8,16,128]{3,2,1,0:T(8,128)S(1)}, f32[12,8,16,128]{3,2,1,0:T(8,128)S(1)}) custom-call(s32[3,16]{1,0:T(4,128)S(1)} %copy-done.1, bf16[4,12,8,16,128]{4,3,2,1,0:T(8,128)(2,1)S(1)} %get-tuple-element.63.qt.refs_4_, ...), custom_call_target="tpu_custom_call" | custom-call | flops 1000000000 | bytes 1 | tf_op jit(solution)/shard_map/own2/pallas_call | solution.py:555
  29.3 3.0 %lower.1 = (bf16[9,192,128]{2,1,0:T(8,128)(2,1)S(1)}, f32[4,192,128]{2,1,0:T(8,128)S(1)}, f32[4,192,128]{2,1,0:T(8,128)S(1)}) custom-call(s32[3,16]{1,0:T(4,128)S(1)} %copy-done.1, bf16[8,192,128]{2,1,0:T(8,128)(2,1)S(1)} %collective-permute-done.4.got, bf16[4,12,8,16,128]{4,3,2,1,0:T(8,128)(2,1)S(1)} %get-tuple-element.63.qt.refs_4_, ...), custom_call_target="tpu_custom_call" | custom-call | flops 3000000000 | bytes 1 | tf_op jit(solution)/shard_map/lower/pallas_call | solution.py:563
  33.1 4.3 %collective-permute-done.2.far.refs_10_ = bf16[2,2,2,192,128]{4,3,2,1,0:T(8,128)(2,1)S(1)} collective-permute-done((bf16[2,2,2,192,128]{4,3,2,1,0:T(8,128)(2,1)S(1)}, bf16[2,2,2,192,128]{4,3,2,1,0:T(8,128)(2,1)S(1)}, u32[]{:S(2)}, u32[]{:S(2)}) %collective-permute-start.2) | collective-permute-done | bytes 393248 | tf_op jit(solution)/shard_map/ppermute | solution.py:622
  37.6 1.3 %collective-permute-start.8 = (bf16[2,2,2,192,128]{4,3,2,1,0:T(8,128)(2,1)S(1)}, bf16[2,2,2,192,128]{4,3,2,1,0:T(8,128)(2,1)S(1)}, u32[]{:S(2)}, u32[]{:S(2)}) collective-permute-start(bf16[2,2,2,192,128]{4,3,2,1,0:T(8,128)(2,1)S(1)} %get-tuple-element.91), channel_id=1, source_target_pairs={{0,8},{4,12},{8,0},{12,4},{16,24},{20,28},{24,16},{28,20},{1,9},{5... | collective-permute-start | bytes 1179656 | tf_op jit(solution)/shard_map/ppermute | solution.py:622
  38.9 2.3 %collective-permute-start.9 = (bf16[2,2,2,192,128]{4,3,2,1,0:T(8,128)(2,1)S(1)}, bf16[2,2,2,192,128]{4,3,2,1,0:T(8,128)(2,1)S(1)}, u32[]{:S(2)}, u32[]{:S(2)}) collective-permute-start(bf16[2,2,2,192,128]{4,3,2,1,0:T(8,128)(2,1)S(1)} %pad_maximum_fusion.1.token), channel_id=1, source_target_pairs={{0,16},{4,20},{8,24},{12,28},{16,0},{20,4},{24,8},{28,12},{1,17},{... | collective-permute-start | bytes 1179656 | tf_op jit(solution)/shard_map/ppermute | solution.py:622
  41.2 2.4 %partner0.1.refs_11_ = bf16[7,192,128]{2,1,0:T(8,128)(2,1)S(1)} custom-call(s32[3,16]{1,0:T(4,128)S(1)} %copy-done.1, bf16[4,12,8,16,128]{4,3,2,1,0:T(8,128)(2,1)S(1)} %get-tuple-element.61.kt.refs_5_, bf16[4,12,8,16,128]{4,3,2,1,0:T(8,128)(2,1)S(1)} %get-tuple-element.62.vt.refs_6_, bf16[4,3,192,128]{3,2,1,0:T(8,128)(2,1)S(1)} %collective-permute-done.1.q23.refs_7_, ...), custom_call_target="tpu_custom_call" | custom-call | flops 1000000000 | bytes 1 | tf_op jit(solution)/shard_map/partner0/pallas_call | solution.py:571
  43.5 1.6 %collective-permute-start.5 = (bf16[7,192,128]{2,1,0:T(8,128)(2,1)S(1)}, bf16[7,192,128]{2,1,0:T(8,128)(2,1)S(1)}, u32[]{:S(2)}, u32[]{:S(2)}) collective-permute-start(bf16[7,192,128]{2,1,0:T(8,128)(2,1)S(1)} %partner0.1.refs_11_), channel_id=1, source_target_pairs={{0,4},{4,0},{8,12},{12,8},{16,20},{20,16},{24,28},{28,24},{1,5},{5... | collective-permute-start | bytes 1032200 | tf_op jit(solution)/shard_map/ppermute | solution.py:622
  45.1 2.5 %mine0.1 = (f32[12,8,16,128]{3,2,1,0:T(8,128)S(1)}, f32[12,8,16,128]{3,2,1,0:T(8,128)S(1)}, f32[12,8,16,128]{3,2,1,0:T(8,128)S(1)}, f32[12,8,16,128]{3,2,1,0:T(8,128)S(1)}) custom-call(s32[3,16]{1,0:T(4,128)S(1)} %copy-done.1, ...), custom_call_target="tpu_custom_call", output_to_operand_aliasing={{0}: (1, {}), {1}: (2, {}), {2}: (3, {}), {3}: (4, {})} | custom-call | flops 10000000000 | bytes 1 | tf_op jit(solution)/shard_map/mine0/pallas_call | solution.py:579
  47.6 2.1 %last.1.refs_5_ = bf16[5,192,128]{2,1,0:T(8,128)(2,1)S(1)} custom-call(s32[3,16]{1,0:T(4,128)S(1)} %copy-done.1, bf16[9,192,128]{2,1,0:T(8,128)(2,1)S(1)} %collective-permute-done.6.turn.refs_6_, bf16[4,12,8,16,128]{4,3,2,1,0:T(8,128)(2,1)S(1)} %get-tuple-element.61.kt.refs_5_, bf16[4,12,8,16,128]{4,3,2,1,0:T(8,128)(2,1)S(1)} %get-tuple-element.62.vt.refs_6_, ...), custom_call_target="tpu_custom_call" | custom-call | flops 1000000000 | bytes 1 | tf_op jit(solution)/shard_map/last/pallas_call | solution.py:646
  49.8 4.6 %collective-permute-done.5.refs_4_ = bf16[7,192,128]{2,1,0:T(8,128)(2,1)S(1)} collective-permute-done((bf16[7,192,128]{2,1,0:T(8,128)(2,1)S(1)}, bf16[7,192,128]{2,1,0:T(8,128)(2,1)S(1)}, u32[]{:S(2)}, u32[]{:S(2)}) %collective-permute-start.5) | collective-permute-done | bytes 344096 | tf_op jit(solution)/shard_map/ppermute | solution.py:622
  54.4 2.1 %finish0.1 = (bf16[384,256]{1,0:T(8,128)(2,1)S(1)}, bf16[384,256]{1,0:T(8,128)(2,1)S(1)}, bf16[2,384,256]{2,1,0:T(8,128)(2,1)S(1)}, bf16[8,128]{1,0:T(8,128)(2,1...) custom-call(s32[3,16]{1,0:T(4,128)S(1)} %copy-done.1, ...), custom_call_target="tpu_custom_call", output_to_operand_aliasing={{4}: (1, {}), {5}: (2, {}), {6}: (3, {}), {7}: (4, {})} | custom-call | flops 1000000000 | bytes 1 | tf_op jit(solution)/shard_map/finish0/pallas_call | solution.py:591
  56.5 1.4 %collective-permute-start.7 = (bf16[2,384,256]{2,1,0:T(8,128)(2,1)S(1)}, bf16[2,384,256]{2,1,0:T(8,128)(2,1)S(1)}, u32[]{:S(2)}, u32[]{:S(2)}) collective-permute-start(bf16[2,384,256]{2,1,0:T(8,128)(2,1)S(1)} %get-tuple-element.87), channel_id=1, source_target_pairs={{0,2},{1,3},{2,0},{3,1},{4,6},{5,7},{6,4},{7,5},{8,10},{9,11},{10,... | collective-permute-start | bytes 1179656 | tf_op jit(solution)/shard_map/ppermute | solution.py:622
  58.7 2.3 %partner2.1 = (bf16[4,192,128]{2,1,0:T(8,128)(2,1)S(1)}, bf16[4,192,128]{2,1,0:T(8,128)(2,1)S(1)}) custom-call(s32[3,16]{1,0:T(4,128)S(1)} %copy-done.1, bf16[4,12,8,16,128]{4,3,2,1,0:T(8,128)(2,1)S(1)} %get-tuple-element.61.kt.refs_5_, bf16[4,12,8,16,128]{4,3,2,1,0:T(8,128)(2,1)S(1)} %get-tuple-element.62.vt.refs_6_, ...), custom_call_target="tpu_custom_call" | custom-call | flops 10000000000 | bytes 1 | tf_op jit(solution)/shard_map/partner2/pallas_call | solution.py:571
  61.0 1.6 %collective-permute-start.11 = (bf16[4,192,128]{2,1,0:T(8,128)(2,1)S(1)}, bf16[4,192,128]{2,1,0:T(8,128)(2,1)S(1)}, u32[]{:S(2)}, u32[]{:S(2)}) collective-permute-start(bf16[4,192,128]{2,1,0:T(8,128)(2,1)S(1)} %get-tuple-element.104), channel_id=1, source_target_pairs={{0,4},{4,0},{8,12},{12,8},{16,20},{20,16},{24,28},{28,24},{1,5},{5... | collective-permute-start | bytes 589832 | tf_op jit(solution)/shard_map/ppermute | solution.py:622
  63.1 2.7 %mine2.1 = (f32[12,8,16,128]{3,2,1,0:T(8,128)S(1)}, f32[12,8,16,128]{3,2,1,0:T(8,128)S(1)}, f32[12,8,16,128]{3,2,1,0:T(8,128)S(1)}, f32[12,8,16,128]{3,2,1,0:T(8,128)S(1)}) custom-call(s32[3,16]{1,0:T(4,128)S(1)} %copy-done.1, ...), custom_call_target="tpu_custom_call", output_to_operand_aliasing={{0}: (1, {}), {1}: (2, {}), {2}: (3, {}), {3}: (4, {})} | custom-call | flops 1000000000 | bytes 1 | tf_op jit(solution)/shard_map/mine2/pallas_call | solution.py:579
  67.9 1.5 %collective-permute-start.16 = (bf16[2,384,128]{2,1,0:T(8,128)(2,1)S(1)}, bf16[2,384,128]{2,1,0:T(8,128)(2,1)S(1)}, u32[]{:S(2)}, u32[]{:S(2)}) collective-permute-start(bf16[2,384,128]{2,1,0:T(8,128)(2,1)S(1)} %get-tuple-element.109), channel_id=1, source_target_pairs={{0,2},{1,3},{2,0},{3,1},{4,6},{5,7},{6,4},{7,5},{8,10},{9,11},{10,... | collective-permute-start | bytes 589832 | tf_op jit(solution)/shard_map/ppermute | solution.py:622
  70.9 2.7 %project0.1.refs_6_.refs_8_ = f32[384,2048]{1,0:T(8,128)S(1)} custom-call(bf16[384,256]{1,0:T(8,128)(2,1)S(1)} %get-tuple-element.92.token.refs_0_, bf16[384,256]{1,0:T(8,128)(2,1)S(1)} %collective-permute-done.17.refs_1_, bf16[2,384,256]{2,1,0:T(8,128)(2,1)S(1)} %collective-permute-done.7.refs_2_, bf16[384,256]{1,0:T(8,128)(2,1)S(1)} %collective-permute-done.18.refs_3_, ...), custom_call_target="tpu_custom_call" | custom-call | flops 1000000000 | bytes 1 | tf_op jit(solution)/shard_map/project0/pallas_call | solution.py:608
  74.6 1.6 %collective-permute-start.13 = (bf16[384,128]{1,0:T(8,128)(2,1)S(1)}, bf16[384,128]{1,0:T(8,128)(2,1)S(1)}, u32[]{:S(2)}, u32[]{:S(2)}) collective-permute-start(bf16[384,128]{1,0:T(8,128)(2,1)S(1)} %get-tuple-element.106), channel_id=1, source_target_pairs={{0,2},{1,3},{2,0},{3,1},{4,6},{5,7},{6,4},{7,5},{8,10},{9,11},{10,... | collective-permute-start | bytes 294920 | tf_op jit(solution)/shard_map/ppermute | solution.py:622
  76.5 2.2 %project1024.1.refs_2_.refs_4_ = f32[384,2048]{1,0:T(8,128)S(1)} custom-call(bf16[384,128]{1,0:T(8,128)(2,1)S(1)} %get-tuple-element.105.refs_3_.refs_0_, bf16[384,128]{1,0:T(8,128)(2,1)S(1)} %collective-permute-done.15.refs_1_, bf16[2,384,128]{2,1,0:T(8,128)(2,1)S(1)} %collective-permute-done.16.refs_2_, ...), custom_call_target="tpu_custom_call" | custom-call | flops 1000000000 | bytes 1 | tf_op jit(solution)/shard_map/project1024/pallas_call | solution.py:608
  78.7 1.6 %collective-permute-done.13.refs_0_ = bf16[384,128]{1,0:T(8,128)(2,1)S(1)} collective-permute-done((bf16[384,128]{1,0:T(8,128)(2,1)S(1)}, bf16[384,128]{1,0:T(8,128)(2,1)S(1)}, u32[]{:S(2)}, u32[]{:S(2)}) %collective-permute-start.13) | collective-permute-done | bytes 98336 | tf_op jit(solution)/shard_map/ppermute | solution.py:622
  80.2 1.2 %collective-permute-done.14.refs_1_ = bf16[384,128]{1,0:T(8,128)(2,1)S(1)} collective-permute-done((bf16[384,128]{1,0:T(8,128)(2,1)S(1)}, bf16[384,128]{1,0:T(8,128)(2,1)S(1)}, u32[]{:S(2)}, u32[]{:S(2)}) %collective-permute-start.14) | collective-permute-done | bytes 98336 | tf_op jit(solution)/shard_map/ppermute | solution.py:622
  81.4 2.1 %project1792.1 = bf16[384,2048]{1,0:T(8,128)(2,1)} custom-call(bf16[384,128]{1,0:T(8,128)(2,1)S(1)} %collective-permute-done.13.refs_0_, bf16[384,128]{1,0:T(8,128)(2,1)S(1)} %collective-permute-done.14.refs_1_, f32[384,2048]{1,0:T(8,128)S(1)} %project1024.1.refs_2_.refs_4_, bf16[2048,2048]{1,0:T(8,128)(2,1)S(1)} %weights.1.refs_4_.refs_7_.refs_3_, ...), custom_call_target="tpu_custom_call" | custom-call | flops 1000000000 | bytes 1 | tf_op jit(solution)/shard_map/project1792/pallas_call | solution.py:608
  (46 shorter events, 8.3 us)
Async XLA Ops:
  0.0 8.4 %copy-start = (bf16[1536,512]{1,0:T(8,128)(2,1)S(1)}, bf16[1536,512]{1,0:T(8,128)(2,1)}, u32[]{:S(2)}) copy-start(bf16[1536,512]{1,0:T(8,128)(2,1)} %q_ref.1) | copy-start | bytes 4718596
  0.0 0.8 copy-start.1
  0.8 1.4 %copy-start.2 = (bf16[1536,512]{1,0:T(8,128)(2,1)S(1)}, bf16[1536,512]{1,0:T(8,128)(2,1)}, u32[]{:S(2)}) copy-start(bf16[1536,512]{1,0:T(8,128)(2,1)} %k_ref.1) | copy-start | bytes 4718596
  2.2 1.4 %copy-start.3 = (bf16[1536,512]{1,0:T(8,128)(2,1)S(1)}, bf16[1536,512]{1,0:T(8,128)(2,1)}, u32[]{:S(2)}) copy-start(bf16[1536,512]{1,0:T(8,128)(2,1)} %v_ref.1) | copy-start | bytes 4718596
  5.3 12.2 %collective-permute-start = (bf16[4,2,192,128]{3,2,1,0:T(8,128)(2,1)S(1)}, bf16[4,2,192,128]{3,2,1,0:T(8,128)(2,1)S(1)}, u32[]{:S(2)}, u32[]{:S(2)}) collective-permute-start(bf16[4,2,192,128]{3,2,1,0:T(8,128)(2,1)S(1)} %get-tuple-element.64.token), channel_id=1, source_target_pairs={{0,8},{4,12},{8,0},{12,4},{16,24},{20,28},{24,16},{28,20},{1,9},{5... | collective-permute-start | bytes 1179656 | tf_op jit(solution)/shard_map/ppermute | solution.py:543
  9.6 19.7 %collective-permute-start.4 = (bf16[8,192,128]{2,1,0:T(8,128)(2,1)S(1)}, bf16[8,192,128]{2,1,0:T(8,128)(2,1)S(1)}, u32[]{:S(2)}, u32[]{:S(2)}) collective-permute-start(bf16[8,192,128]{2,1,0:T(8,128)(2,1)S(1)} %get-tuple-element.77), channel_id=1, source_target_pairs={{0,4},{4,0},{8,12},{12,8},{16,20},{20,16},{24,28},{28,24},{1,5},{5... | collective-permute-start | bytes 1179656 | tf_op jit(solution)/shard_map/ppermute | solution.py:550
  17.6 19.8 %collective-permute-start.2 = (bf16[2,2,2,192,128]{4,3,2,1,0:T(8,128)(2,1)S(1)}, bf16[2,2,2,192,128]{4,3,2,1,0:T(8,128)(2,1)S(1)}, u32[]{:S(2)}, u32[]{:S(2)}) collective-permute-start(bf16[2,2,2,192,128]{4,3,2,1,0:T(8,128)(2,1)S(1)} %pad_maximum_fusion.token), channel_id=1, source_target_pairs={{0,16},{4,20},{8,24},{12,28},{16,0},{20,4},{24,8},{28,12},{1,17},{... | collective-permute-start | bytes 1179656 | tf_op jit(solution)/shard_map/ppermute | solution.py:622
  20.4 17.2 %collective-permute-start.3 = (bf16[2,2,2,192,128]{4,3,2,1,0:T(8,128)(2,1)S(1)}, bf16[2,2,2,192,128]{4,3,2,1,0:T(8,128)(2,1)S(1)}, u32[]{:S(2)}, u32[]{:S(2)}) collective-permute-start(bf16[2,2,2,192,128]{4,3,2,1,0:T(8,128)(2,1)S(1)} %get-tuple-element.75), channel_id=1, source_target_pairs={{0,8},{4,12},{8,0},{12,4},{16,24},{20,28},{24,16},{28,20},{1,9},{5... | collective-permute-start | bytes 1179656 | tf_op jit(solution)/shard_map/ppermute | solution.py:622
  22.0 19.2 %collective-permute-start.1 = (bf16[4,3,192,128]{3,2,1,0:T(8,128)(2,1)S(1)}, bf16[4,3,192,128]{3,2,1,0:T(8,128)(2,1)S(1)}, u32[]{:S(2)}, u32[]{:S(2)}) collective-permute-start(bf16[4,3,192,128]{3,2,1,0:T(8,128)(2,1)S(1)} %get-tuple-element.73), channel_id=1, source_target_pairs={{0,4},{4,0},{8,12},{12,8},{16,20},{20,16},{24,28},{28,24},{1,5},{5... | collective-permute-start | bytes 1769480 | tf_op jit(solution)/shard_map/ppermute | solution.py:622
  23.5 9.0 %slice-start = ((s8[8388608]{0:T(1024)(128)(4,1)}), s8[4194304]{0:T(1024)(128)(4,1)S(1)}, s32[]{:S(2)}) async-start(s8[8388608]{0:T(1024)(128)(4,1)} %bitcast.12), calls=%async_computation | async-start | bytes 8388608
  29.3 3.2 %slice-start.1 = ((s8[8388608]{0:T(1024)(128)(4,1)}), s8[4194304]{0:T(1024)(128)(4,1)S(1)}, s32[]{:S(2)}) async-start(s8[8388608]{0:T(1024)(128)(4,1)} %bitcast.12), calls=%async_computation.1 | async-start | bytes 8388608
  32.4 15.2 %collective-permute-start.6 = (bf16[9,192,128]{2,1,0:T(8,128)(2,1)S(1)}, bf16[9,192,128]{2,1,0:T(8,128)(2,1)S(1)}, u32[]{:S(2)}, u32[]{:S(2)}) collective-permute-start(bf16[9,192,128]{2,1,0:T(8,128)(2,1)S(1)} %get-tuple-element.79.token), channel_id=1, source_target_pairs={{0,4},{4,0},{8,12},{12,8},{16,20},{20,16},{24,28},{28,24},{1,5},{5... | collective-permute-start | bytes 1327112 | tf_op jit(solution)/shard_map/ppermute | solution.py:622
  37.6 20.4 %collective-permute-start.8 = (bf16[2,2,2,192,128]{4,3,2,1,0:T(8,128)(2,1)S(1)}, bf16[2,2,2,192,128]{4,3,2,1,0:T(8,128)(2,1)S(1)}, u32[]{:S(2)}, u32[]{:S(2)}) collective-permute-start(bf16[2,2,2,192,128]{4,3,2,1,0:T(8,128)(2,1)S(1)} %get-tuple-element.91), channel_id=1, source_target_pairs={{0,8},{4,12},{8,0},{12,4},{16,24},{20,28},{24,16},{28,20},{1,9},{5... | collective-permute-start | bytes 1179656 | tf_op jit(solution)/shard_map/ppermute | solution.py:622
  38.9 19.8 %collective-permute-start.9 = (bf16[2,2,2,192,128]{4,3,2,1,0:T(8,128)(2,1)S(1)}, bf16[2,2,2,192,128]{4,3,2,1,0:T(8,128)(2,1)S(1)}, u32[]{:S(2)}, u32[]{:S(2)}) collective-permute-start(bf16[2,2,2,192,128]{4,3,2,1,0:T(8,128)(2,1)S(1)} %pad_maximum_fusion.1.token), channel_id=1, source_target_pairs={{0,16},{4,20},{8,24},{12,28},{16,0},{20,4},{24,8},{28,12},{1,17},{... | collective-permute-start | bytes 1179656 | tf_op jit(solution)/shard_map/ppermute | solution.py:622
  43.5 10.9 %collective-permute-start.5 = (bf16[7,192,128]{2,1,0:T(8,128)(2,1)S(1)}, bf16[7,192,128]{2,1,0:T(8,128)(2,1)S(1)}, u32[]{:S(2)}, u32[]{:S(2)}) collective-permute-start(bf16[7,192,128]{2,1,0:T(8,128)(2,1)S(1)} %partner0.1.refs_11_), channel_id=1, source_target_pairs={{0,4},{4,0},{8,12},{12,8},{16,20},{20,16},{24,28},{28,24},{1,5},{5... | collective-permute-start | bytes 1032200 | tf_op jit(solution)/shard_map/ppermute | solution.py:622
  49.7 16.7 %collective-permute-start.12 = (bf16[5,192,128]{2,1,0:T(8,128)(2,1)S(1)}, bf16[5,192,128]{2,1,0:T(8,128)(2,1)S(1)}, u32[]{:S(2)}, u32[]{:S(2)}) collective-permute-start(bf16[5,192,128]{2,1,0:T(8,128)(2,1)S(1)} %last.1.refs_5_), channel_id=1, source_target_pairs={{0,4},{4,0},{8,12},{12,8},{16,20},{20,16},{24,28},{28,24},{1,5},{5... | collective-permute-start | bytes 737288 | tf_op jit(solution)/shard_map/ppermute | solution.py:622
  56.5 9.3 %collective-permute-start.7 = (bf16[2,384,256]{2,1,0:T(8,128)(2,1)S(1)}, bf16[2,384,256]{2,1,0:T(8,128)(2,1)S(1)}, u32[]{:S(2)}, u32[]{:S(2)}) collective-permute-start(bf16[2,384,256]{2,1,0:T(8,128)(2,1)S(1)} %get-tuple-element.87), channel_id=1, source_target_pairs={{0,2},{1,3},{2,0},{3,1},{4,6},{5,7},{6,4},{7,5},{8,10},{9,11},{10,... | collective-permute-start | bytes 1179656 | tf_op jit(solution)/shard_map/ppermute | solution.py:622
  61.0 5.7 %collective-permute-start.11 = (bf16[4,192,128]{2,1,0:T(8,128)(2,1)S(1)}, bf16[4,192,128]{2,1,0:T(8,128)(2,1)S(1)}, u32[]{:S(2)}, u32[]{:S(2)}) collective-permute-start(bf16[4,192,128]{2,1,0:T(8,128)(2,1)S(1)} %get-tuple-element.104), channel_id=1, source_target_pairs={{0,4},{4,0},{8,12},{12,8},{16,20},{20,16},{24,28},{28,24},{1,5},{5... | collective-permute-start | bytes 589832 | tf_op jit(solution)/shard_map/ppermute | solution.py:622
  62.6 6.9 %collective-permute-start.10 = (bf16[4,192,128]{2,1,0:T(8,128)(2,1)S(1)}, bf16[4,192,128]{2,1,0:T(8,128)(2,1)S(1)}, u32[]{:S(2)}, u32[]{:S(2)}) collective-permute-start(bf16[4,192,128]{2,1,0:T(8,128)(2,1)S(1)} %get-tuple-element.93.refs_11_), channel_id=1, source_target_pairs={{0,4},{4,0},{8,12},{12,8},{16,20},{20,16},{24,28},{28,24},{1,5},{5... | collective-permute-start | bytes 589832 | tf_op jit(solution)/shard_map/ppermute | solution.py:622
  63.1 7.8 %collective-permute-start.17 = (bf16[384,256]{1,0:T(8,128)(2,1)S(1)}, bf16[384,256]{1,0:T(8,128)(2,1)S(1)}, u32[]{:S(2)}, u32[]{:S(2)}) collective-permute-start(bf16[384,256]{1,0:T(8,128)(2,1)S(1)} %get-tuple-element.110), channel_id=1, source_target_pairs={{0,1},{1,0},{2,3},{3,2},{4,5},{5,4},{6,7},{7,6},{8,9},{9,8},{10,11... | collective-permute-start | bytes 589832 | tf_op jit(solution)/shard_map/ppermute | solution.py:622
  65.9 5.0 %collective-permute-start.18 = (bf16[384,256]{1,0:T(8,128)(2,1)S(1)}, bf16[384,256]{1,0:T(8,128)(2,1)S(1)}, u32[]{:S(2)}, u32[]{:S(2)}) collective-permute-start(bf16[384,256]{1,0:T(8,128)(2,1)S(1)} %slice_bitcast_fusion), channel_id=1, source_target_pairs={{0,1},{1,0},{2,3},{3,2},{4,5},{5,4},{6,7},{7,6},{8,9},{9,8},{10,11... | collective-permute-start | bytes 589832 | tf_op jit(solution)/shard_map/ppermute | solution.py:622
  67.9 6.6 %collective-permute-start.16 = (bf16[2,384,128]{2,1,0:T(8,128)(2,1)S(1)}, bf16[2,384,128]{2,1,0:T(8,128)(2,1)S(1)}, u32[]{:S(2)}, u32[]{:S(2)}) collective-permute-start(bf16[2,384,128]{2,1,0:T(8,128)(2,1)S(1)} %get-tuple-element.109), channel_id=1, source_target_pairs={{0,2},{1,3},{2,0},{3,1},{4,6},{5,7},{6,4},{7,5},{8,10},{9,11},{10,... | collective-permute-start | bytes 589832 | tf_op jit(solution)/shard_map/ppermute | solution.py:622
  70.3 6.2 %collective-permute-start.20 = (bf16[384,128]{1,0:T(8,128)(2,1)S(1)}, bf16[384,128]{1,0:T(8,128)(2,1)S(1)}, u32[]{:S(2)}, u32[]{:S(2)}) collective-permute-start(bf16[384,128]{1,0:T(8,128)(2,1)S(1)} %get-tuple-element.115), channel_id=1, source_target_pairs={{0,1},{1,0},{2,3},{3,2},{4,5},{5,4},{6,7},{7,6},{8,9},{9,8},{10,11... | collective-permute-start | bytes 294920 | tf_op jit(solution)/shard_map/ppermute | solution.py:622
  70.4 6.1 %collective-permute-start.15 = (bf16[384,128]{1,0:T(8,128)(2,1)S(1)}, bf16[384,128]{1,0:T(8,128)(2,1)S(1)}, u32[]{:S(2)}, u32[]{:S(2)}) collective-permute-start(bf16[384,128]{1,0:T(8,128)(2,1)S(1)} %get-tuple-element.108), channel_id=1, source_target_pairs={{0,1},{1,0},{2,3},{3,2},{4,5},{5,4},{6,7},{7,6},{8,9},{9,8},{10,11... | collective-permute-start | bytes 294920 | tf_op jit(solution)/shard_map/ppermute | solution.py:622
  74.5 2.0 %collective-permute-start.19 = (bf16[384,128]{1,0:T(8,128)(2,1)S(1)}, bf16[384,128]{1,0:T(8,128)(2,1)S(1)}, u32[]{:S(2)}, u32[]{:S(2)}) collective-permute-start(bf16[384,128]{1,0:T(8,128)(2,1)S(1)} %slice_bitcast_fusion.5), channel_id=1, source_target_pairs={{0,1},{1,0},{2,3},{3,2},{4,5},{5,4},{6,7},{7,6},{8,9},{9,8},{10,11... | collective-permute-start | bytes 294920 | tf_op jit(solution)/shard_map/ppermute | solution.py:622
  74.6 5.7 %collective-permute-start.13 = (bf16[384,128]{1,0:T(8,128)(2,1)S(1)}, bf16[384,128]{1,0:T(8,128)(2,1)S(1)}, u32[]{:S(2)}, u32[]{:S(2)}) collective-permute-start(bf16[384,128]{1,0:T(8,128)(2,1)S(1)} %get-tuple-element.106), channel_id=1, source_target_pairs={{0,2},{1,3},{2,0},{3,1},{4,6},{5,7},{6,4},{7,5},{8,10},{9,11},{10,... | collective-permute-start | bytes 294920 | tf_op jit(solution)/shard_map/ppermute | solution.py:622
  76.1 5.3 %collective-permute-start.14 = (bf16[384,128]{1,0:T(8,128)(2,1)S(1)}, bf16[384,128]{1,0:T(8,128)(2,1)S(1)}, u32[]{:S(2)}, u32[]{:S(2)}) collective-permute-start(bf16[384,128]{1,0:T(8,128)(2,1)S(1)} %get-tuple-element.107), channel_id=1, source_target_pairs={{0,3},{1,2},{2,1},{3,0},{4,7},{5,6},{6,5},{7,4},{8,11},{9,10},{10,... | collective-permute-start | bytes 294920 | tf_op jit(solution)/shard_map/ppermute | solution.py:622

commit v5 on v4

--- a/solution.py
+++ b/solution.py
@@ -15,6 +15,7 @@
 RES = 8
 SUB = 16
 BLK = RES * SUB
+TAIL = 64
 NEG = -1e30
 RATE = math.log2(math.e) / math.sqrt(DH)
 BF16 = jnp.bfloat16
@@ -213,29 +214,54 @@
     attend_all(tasks)
 
 
-def put_stat(slab, stat, place):
-    lane = iota(stat.shape, 1)
-    rest = stat
-    now = slab[...]
-    for i in range(3):
-        piece = rest.astype(BF16)
-        rest = rest - piece.astype(F32)
-        now = jnp.where(lane == place + 32 * i, piece, now)
-    slab[...] = now
+def put_message(msg, slab, place, o, s, count):
+    rows = o.shape[0] // count
+    lane = iota((rows, DH), 1)
+    for j in range(count):
+        at = slice(j * rows, (j + 1) * rows)
+        msg[(place + j) * rows : (place + j + 1) * rows, :] = o[at].astype(BF16)
+        rest, now = s[at], slab[:rows, :]
+        for i in range(3):
+            piece = rest.astype(BF16)
+            rest = rest - piece.astype(F32)
+            now = jnp.where(lane == 3 * (place + j) + i, piece, now)
+        slab[:rows, :] = now
+
+
+def unit(rows):
+    hit = iota((rows, DH), 0) == iota((rows, DH), 1)
+    return jnp.where(hit, 1.0, 0.0).astype(BF16)
+
+
+def close_message(msg, slab):
+    first = msg.shape[0] - TAIL
+    half = TAIL // 2
+    turned = lax.dot_general(
+        unit(half), slab[...], (((1,), (1,)), ((), ())), preferred_element_type=F32
+    ).astype(BF16)
+    for i in range(2):
+        msg[first + i * half : first + (i + 1) * half, :] = turned[:, i * DH : (i + 1) * DH]
+
+
+def open_message(msg, rows):
+    first = msg.shape[0] - TAIL
+    half = TAIL // 2
+    parts = [
+        lax.dot_general(
+            msg[first + i * half : first + (i + 1) * half, :],
+            unit(half),
+            (((0,), (0,)), ((), ())),
+            preferred_element_type=F32,
+        )
+        for i in range(2)
+    ]
+    return jnp.concatenate(parts, axis=0)[:rows]
 
 
 def get_stat(slab, place):
     lane = iota(slab.shape, 1)
-    hit = (lane == place) | (lane == place + 32) | (lane == place + 64)
-    return jnp.sum(jnp.where(hit, slab[...].astype(F32), 0.0), axis=1, keepdims=True)
-
-
-def put_message(msg, place, o, s, count):
-    rows = msg.shape[1]
-    for j in range(count):
-        at = slice(j * rows, (j + 1) * rows)
-        msg[place + j] = o[at].astype(BF16)
-        put_stat(msg.at[msg.shape[0] - 1], s[at], place + j)
+    hit = (lane >= 3 * place) & (lane < 3 * place + 3)
+    return jnp.sum(jnp.where(hit, slab, 0.0), axis=1, keepdims=True)
 
 
 def pair_tasks(load, keys, values, put):
@@ -258,12 +284,13 @@
     ]
 
 
-def lower_kernel(heads, off_ref, got, qt, kt, vt, token, msg, *local):
-    last = msg.shape[0] - 1
+def lower_kernel(heads, off_ref, got, qt, kt, vt, token, msg, *refs):
+    *local, slab = refs
     count = RES // 2
-    rows = msg.shape[1]
+    rows = kt.shape[1] * SUB
     later = lax.axis_index("ctx") % 2 == 1
     msg[...] = jnp.zeros(msg.shape, BF16)
+    slab[...] = jnp.zeros(slab.shape, BF16)
 
     @pl.when(jnp.logical_not(later))
     def _():
@@ -274,16 +301,17 @@
                 lambda n=n: [got[n * count + j] for j in range(count)],
                 lambda head=head, shift=shift: rows_of(kt.at[head], 1, shift),
                 lambda head=head, shift=shift: rows_of(vt.at[head], 1, shift),
-                lambda j, o, s, n=n: put_message(msg, n * count + j, o, s, 2),
+                lambda j, o, s, n=n: put_message(msg, slab, n * count + j, o, s, 2),
             )
         attend_all(tasks)
+        close_message(msg, slab)
         for ref, fill in zip(local, (0.0, NEG)):
             ref[...] = jnp.full(ref.shape, fill, F32)
 
     @pl.when(later)
     def _():
         for j, x in enumerate(rows_of(qt.at[2], 1, shift_of(off_ref, 1, 2))):
-            msg[j] = x
+            msg[j * rows : (j + 1) * rows, :] = x
         shift = shift_of(off_ref, 1, 3)
 
         def put(j, o, s):
@@ -301,28 +329,31 @@
         )
 
 
-def last_kernel(off_ref, turn, kt, vt, token, msg):
+def last_kernel(off_ref, turn, kt, vt, token, msg, slab):
     msg[...] = jnp.zeros(msg.shape, BF16)
+    slab[...] = jnp.zeros(slab.shape, BF16)
+    rows = kt.shape[1] * SUB
 
     @pl.when(lax.axis_index("ctx") % 2 == 0)
     def _():
         shift = shift_of(off_ref, 1, 2)
         attend_all(
             pair_tasks(
-                lambda: [turn[j] for j in range(RES // 2)],
+                lambda: [turn[j * rows : (j + 1) * rows, :] for j in range(RES // 2)],
                 lambda: rows_of(kt.at[2], 1, shift),
                 lambda: rows_of(vt.at[2], 1, shift),
-                lambda j, o, s: put_message(msg, j, o, s, 2),
+                lambda j, o, s: put_message(msg, slab, j, o, s, 2),
             )
         )
-
-
-def level_blocks(off_ref, level, head, n, q23, kt, vt, kv2, near, far):
+        close_message(msg, slab)
+
+
+def level_blocks(off_ref, level, head, n, kt, vt, kv2, near, far):
     ctx = lax.axis_index("ctx")
     z = ctx // 2
     shift = shift_of(off_ref, level, head)
     count = RES // 2**level
-    rows = q23.shape[2]
+    rows = kt.shape[1] * SUB
     size = count * rows
     odd = jnp.where(z % 2 == 1, 0.0, NEG)
     high = jnp.where(z % 4 >= 2, 0.0, NEG)
@@ -330,25 +361,27 @@
     def whole(ref):
         return jnp.concatenate(rows_of(ref.at[head], level, shift), axis=0)
 
-    def blocks(bias):
-        if level == 2:
+    def blocks(bias, which="all"):
+        past = []
+        if which != "own" and level == 2:
             past = [(kv2[n, 0].reshape(size, DH), kv2[n, 1].reshape(size, DH), odd)]
-        else:
+        elif which != "own":
             past = [
                 (near[head, 0], near[head, 1], odd),
                 (far[0, n, 0], far[0, n, 1], high),
                 (far[1, n, 0], far[1, n, 1], high),
             ]
-        return past + [(whole(kt), whole(vt), bias)]
+        return past if which == "past" else past + [(whole(kt), whole(vt), bias)]
 
     return whole, blocks, shift, count, rows
 
 
-def partner_kernel(heads, off_ref, kt, vt, q23, kv2, near, far, token, *msgs):
+def partner_kernel(heads, off_ref, kt, vt, q23, kv2, near, far, token, *refs):
     later = jnp.where(lax.axis_index("ctx") % 2 == 0, 0.0, NEG)
     tasks = []
-    for msg in msgs:
-        msg[msg.shape[0] - 1] = jnp.zeros(msg.shape[1:], BF16)
+    msgs, slabs = refs[: len(refs) // 2], refs[len(refs) // 2 :]
+    for slab in slabs:
+        slab[...] = jnp.zeros(slab.shape, BF16)
     places = [0] * len(msgs)
     order = [(level, n) for level in (2, 3) for n in range(len(heads))]
     if len(msgs) > 1:
@@ -356,40 +389,40 @@
     for level, n in order:
         head, which = heads[n], n % len(msgs)
         _, blocks, _, count, rows = level_blocks(
-            off_ref, level, head, n, q23, kt, vt, kv2, near, far
+            off_ref, level, head, n, kt, vt, kv2, near, far
         )
         first = 0 if level == 2 else 2
         tasks.append(
             (
                 lambda h=head, f=first, c=count, r=rows: q23[h, f : f + c].reshape(c * r, DH),
                 lambda blocks=blocks: blocks(later),
-                lambda o, s, m=msgs[which], p=places[which], c=count: put_message(m, p, o, s, c),
+                lambda o, s, w=which, p=places[which], c=count: put_message(
+                    msgs[w], slabs[w], p, o, s, c
+                ),
             )
         )
         places[which] += count
     attend_all(tasks)
-
-
-def add_lower(off_ref, head, msg, first, out, lse):
-    later = lax.axis_index("ctx") % 2 == 1
-    for j in range(RES // 2):
-        at = (slice(None), shift_of(off_ref, 1, head) + 2 * j)
-        stat = jnp.where(later, get_stat(msg.at[msg.shape[0] - 1], first + j), NEG)
-        part = msg[first + j].astype(F32)
-        add_rows(out, lse, at, (part, jnp.broadcast_to(stat, part.shape)))
-
-
-def mine_kernel(heads, which, off_ref, *refs):
-    number = len(heads)
-    refs = refs[2 * number :]
-    (qt, kt, vt, q23, kv2, near, far, token), refs = refs[:8], refs[8:]
-    lower, state = refs[: -2 * number], refs[-2 * number :]
+    for msg, slab in zip(msgs, slabs):
+        close_message(msg, slab)
+
+
+def add_message(msg, slab, place, out, lse, at, valid=None):
+    rows = slab.shape[0]
+    stat = get_stat(slab, place)
+    if valid is not None:
+        stat = jnp.where(valid, stat, NEG)
+    part = msg[place * rows : (place + 1) * rows, :].astype(F32)
+    add_rows(out, lse, at, (part, jnp.broadcast_to(stat, part.shape)))
+
+
+def own_rows(heads, which, off_ref, qt, kt, vt, kv2, near, far, state):
     tasks = []
     for level in (2, 3):
         for n, head in enumerate(heads):
             out, lse = state[2 * n : 2 * n + 2]
             whole, blocks, shift, count, rows = level_blocks(
-                off_ref, level, head, n, q23, kt, vt, kv2, near, far
+                off_ref, level, head, n, kt, vt, kv2, near, far
             )
             triangle = causal_bias(lambda r, c=count, m=rows: r % m * c + r // m, count * rows)
 
@@ -401,16 +434,36 @@
             tasks.append(
                 (
                     lambda whole=whole: whole(qt),
-                    lambda blocks=blocks, t=triangle: blocks(t)[which],
+                    lambda blocks=blocks, t=triangle: blocks(t, which),
                     put,
                 )
             )
     attend_all(tasks)
-    for n, head in enumerate(heads):
-        if lower and head == 3:
-            for j in range(RES // 2):
-                at = (slice(None), shift_of(off_ref, 1, head) + 2 * j)
-                add_rows(state[2 * n], state[2 * n + 1], at, (lower[0][j], lower[1][j]))
+
+
+def mine_kernel(heads, which, off_ref, *refs):
+    number = len(heads)
+    refs = refs[2 * number :]
+    own_rows(heads, which, off_ref, *refs[:6], refs[7:])
+
+
+def weights_kernel(off_ref, *refs):
+    heads = GROUPS[1]
+    number = len(heads)
+    qt, kt, vt, o1, s1, w_ref, token, *refs = refs[2 * number :]
+    state, out = refs[:-1], refs[-1]
+    mine = lax.axis_index("head")
+    at = 0
+    for members in PIECES:
+        width = len(members) * DH
+        for t in range(4):
+            first = (mine ^ t) * (HEADS_HERE * DH) + members[0] * DH
+            out[at : at + width, :] = w_ref[pl.ds(pl.multiple_of(first, DH), width), :]
+            at += width
+    own_rows(heads, "own", off_ref, qt, kt, vt, None, None, None, state)
+    for j in range(RES // 2):
+        at = (slice(None), shift_of(off_ref, 1, 3) + 2 * j)
+        add_rows(state[-2], state[-1], at, (o1[j], s1[j]))
 
 
 def finish_kernel(heads, stacked, off_ref, *refs):
@@ -418,22 +471,23 @@
     refs = refs[2 * number :]
     msg, token, *below = refs[: -4 - 2 * number]
     dests, state = refs[-4 - 2 * number : -2 * number], refs[-2 * number :]
-    for n, head in enumerate(heads):
-        if below:
-            add_lower(off_ref, head, below[0], n * (RES // 2), state[2 * n], state[2 * n + 1])
+    rows = state[0].shape[0] * SUB
+    later = lax.axis_index("ctx") % 2 == 1
+    if below:
+        slab = open_message(below[0], rows)
+        for n, head in enumerate(heads):
+            for j in range(RES // 2):
+                at = (slice(None), shift_of(off_ref, 1, head) + 2 * j)
+                place = n * (RES // 2) + j
+                add_message(below[0], slab, place, state[2 * n], state[2 * n + 1], at, later)
+    slab = open_message(msg, rows)
     place = 0
     for level in (2, 3):
         for n, head in enumerate(heads):
             shift = shift_of(off_ref, level, head)
             for j in range(RES // 2**level):
-                part = msg[place].astype(F32)
-                stat = get_stat(msg.at[msg.shape[0] - 1], place)
-                add_rows(
-                    state[2 * n],
-                    state[2 * n + 1],
-                    (slice(None), shift + j * 2**level),
-                    (part, jnp.broadcast_to(stat, part.shape)),
-                )
+                at = (slice(None), shift + j * 2**level)
+                add_message(msg, slab, place, state[2 * n], state[2 * n + 1], at)
                 place += 1
     mine = lax.axis_index("head")
     per = state[0].shape[0] // 4
@@ -443,17 +497,6 @@
         for n in range(number):
             x = state[2 * n][pl.ds((mine ^ t) * per, per)].reshape(per * BLK, DH)
             dest[:, n * DH : (n + 1) * DH] = x.astype(BF16)
-
-
-def weights_kernel(w_ref, token, out):
-    mine = lax.axis_index("head")
-    at = 0
-    for members in PIECES:
-        width = len(members) * DH
-        for t in range(4):
-            first = (mine ^ t) * (HEADS_HERE * DH) + members[0] * DH
-            out[at : at + width, :] = w_ref[pl.ds(pl.multiple_of(first, DH), width), :]
-            at += width
 
 
 def project_kernel(first, added, final, *refs):
@@ -526,6 +569,8 @@
     heads = width // DH
     slots = rows_here // RES
     piece = (slots, DH)
+    message = lambda count: shape(count * slots + TAIL, DH)
+    slab = pltpu.VMEM((2 * DH, DH), BF16)
     regrouped = shape(heads, blocks, RES, SUB, DH)
     ctx_size = lax.axis_size("ctx")
     swap = [(i, i ^ 1) for i in range(ctx_size)]
@@ -563,26 +608,28 @@
         return call(
             functools.partial(lower_kernel, members),
             [SMEM] + [VMEM] * 4 + [ANY],
-            [shape(len(members) * 4 + 1, *piece)] + [shape(4, *piece, dtype=F32)] * 2,
+            [message(len(members) * 4)] + [shape(4, *piece, dtype=F32)] * 2,
             "lower",
+            scratch=[slab],
         )(offsets, got, qt, kt, vt, token)
 
     def partner(members, column, token, messages):
         return call(
             functools.partial(partner_kernel, members),
             [SMEM] + [VMEM] * 6 + [ANY],
-            [shape(len(members) // messages * 3 + 1, *piece)] * messages,
+            [message(len(members) // messages * 3)] * messages,
             "partner%d" % members[0],
+            scratch=[slab] * messages,
         )(offsets, kt, vt, q23, *column, token)
 
-    def mine(members, rows, column, below, token, which=slice(None), name="mine"):
+    def mine(members, rows, column, token, which="all"):
         return call(
             functools.partial(mine_kernel, members, which),
-            [SMEM] + [VMEM] * (len(rows) + 7) + [ANY] + [VMEM] * len(below),
+            [SMEM] + [VMEM] * (len(rows) + 6) + [ANY],
             [state] * len(rows),
-            name + "%d" % members[0],
+            "mine%d" % members[0],
             aliases={1 + i: i for i in range(len(rows))},
-        )(offsets, *rows, qt, kt, vt, q23, *column, token, *below)
+        )(offsets, *rows, qt, kt, vt, *column, token)
 
     def finished(members, rows, message, token, *below):
         dest = shape(rows_here // 4, len(members) * DH)
@@ -630,9 +677,13 @@
     q23 = send(q23, "ctx", swap)
     msg1, o1, s1 = lower((0, 1), first, rows_b[0])
     turn = send(msg1, "ctx", swap)
-    weights = call(weights_kernel, [VMEM, ANY], shape(*out_weight.shape), "weights")(
-        out_weight, msg1
-    )
+    *rows_b, weights = call(
+        weights_kernel,
+        [SMEM] + [VMEM] * 10 + [ANY],
+        [state] * 4 + [shape(*out_weight.shape)],
+        "weights",
+        aliases={1 + i: i for i in range(4)},
+    )(offsets, *rows_b, qt, kt, vt, o1, s1, out_weight, msg1)
 
     far_a, kv2_a, far_b, kv2_b, weights = lax.optimization_barrier(
         (far_a, kv2_a, both(group_b), kv2[1], weights)
@@ -642,9 +693,13 @@
     column_a = [kv2_a, kv3_near, far_a]
     (msg_a,) = partner(group_a, column_a, ready, 1)
     got_a = send(msg_a, "ctx", swap)
-    rows_a = list(mine(group_a, rows_a, column_a, [], msg_a))
+    rows_a = list(mine(group_a, rows_a, column_a, msg_a))
     msg1c = call(
-        last_kernel, [SMEM] + [VMEM] * 3 + [ANY], shape(RES // 2 + 1, *piece), "last"
+        last_kernel,
+        [SMEM] + [VMEM] * 3 + [ANY],
+        message(RES // 2),
+        "last",
+        scratch=[slab],
     )(offsets, turn, kt, vt, rows_a[0])
     got1c = send(msg1c, "ctx", swap)
     rows_a = finished(group_a, rows_a, got_a, msg1c, turn)
@@ -653,7 +708,7 @@
     column_b = [kv2_b, kv3_near, far_b]
     msg_b, msg_c = partner(group_b, column_b, rows_a[0], 2)
     got_b, got_c = send(msg_b, "ctx", swap), send(msg_c, "ctx", swap)
-    rows_b = mine(group_b, rows_b, column_b, [o1, s1], msg_c)
+    rows_b = mine(group_b, rows_b, column_b, msg_c, "past")
     a23, *rows_b = lax.optimization_barrier((a23, *rows_b))
     a3 = send(a23[1], "head", over[1])
     rows_b, rows_c = rows_b[:2], rows_b[2:]
@@ -661,11 +716,11 @@
     b1, b23 = send(rows_b[1], "head", over[1]), send(rows_b[2], "head", over[2])
     rows_c = finished((3,), rows_c, got_c, rows_b[0])
     c2, c3, c1 = (send(rows_c[t], "head", over[t]) for t in (2, 3, 1))
-    half = project(0, [rows_a[0], a1, a23, a3], [], rows_c[0])
+    half = project(0, [rows_a[0], a1, a23, a3, rows_b[0], b1], [], rows_c[0])
     b23, half = lax.optimization_barrier((b23, half))
     b3 = send(b23[1], "head", over[1])
-    half = project(8 * DH, [rows_b[0], b1, b23, b3, rows_c[0], c1], [half], half)
-    return project(14 * DH, [c2, c3], [half], half, final=True)
+    last = [b23, b3, rows_c[0], c1, c2, c3]
+    return project(10 * DH, last, [half], half, final=True)
 
 
 def solution(mesh):

time: 83.9 us -> 81.5 us (0.971)
  waiting for transfers between devices: 14.3 us -> 10.7 us
  Pallas kernels: 41.1 us -> 42.4 us
    ppermute x19, waiting for transfers between devices: 13.8 us -> 10.3 us  [send(): return lax.ppermute(value, axis, pairs)]
    pallas_call x2, Pallas kernels: 2.63 us -> 4.61 us  [the longest x1 2.51 us: body(): call(weights_kernel, [SMEM] + [VMEM] * 10 + [ANY], [state] * 4 + [shape(*...]
    pallas_call x3 -> x2, Pallas kernels: 6.94 us -> 6.15 us  [project(): call(functools.partial(project_kernel, first, len(before), final), [VMEM]...]
  transfers between devices with their start and end apart: 21 -> 21, of which waited for: 9 -> 9; matrix products, arithmetic and copies ran while one was open for 0% -> 0% of each run, Pallas kernels for 45% -> 46%
where the time goes in v5:
time: 81.5 us; the launch traced here: 81.3 us
  Pallas kernels  42.4 us (52%)
  starting transfers between devices  24 us (29%)
  waiting for transfers between devices  10.7 us (13%)
  local copies, waits for them, and re-layouts  3.71 us (5%)
    ppermute x19, starting transfers between devices, send(): return lax.ppermute(value, axis, pairs)  19.3 us
    pallas_call x2, Pallas kernels, own(): call(functools.partial(own_kernel, members), [SMEM, VMEM, VMEM, VMEM, ANY...  11.6 us
    ppermute x19, waiting for transfers between devices, send(): return lax.ppermute(value, axis, pairs)  10.3 us
    pallas_call x2, Pallas kernels, project(): call(functools.partial(project_kernel, first, len(before), final), [VMEM]...  6.15 us
    pallas_call x2, Pallas kernels, partner(): call(functools.partial(partner_kernel, members), [SMEM] + [VMEM] * 6 + [A...  4.93 us
    pallas_call x3, Pallas kernels, finished(): call(functools.partial(finish_kernel, members, stacked), [SMEM] + [VMEM]...  4.61 us
    pallas_call x2, Pallas kernels, mine(): call(functools.partial(mine_kernel, members, which), [SMEM] + [VMEM] * (l...  4.44 us
    unnamed x12, local copies, waits for them, and re-layouts  3.63 us
  transfers between devices with their start and end apart: 21, of which 9 were waited for; matrix products, arithmetic and copies ran while one was open for 0% of the time, Pallas kernels for 46%

profile of v5, /device:TPU:0, one launch (start us, length us, event | category | flops | bytes accessed | tf_op | source)
XLA Modules:
  0.0 81.3 jit_solution(15090153360168908161)
XLA Ops:
  0.8 1.4 %copy-done.2 = bf16[1536,512]{1,0:T(8,128)(2,1)S(1)} copy-done((bf16[1536,512]{1,0:T(8,128)(2,1)S(1)}, bf16[1536,512]{1,0:T(8,128)(2,1)}, u32[]{:S(2)}) %copy-start.2) | copy-done | bytes 1572888
  2.2 1.4 %copy-done.3 = bf16[1536,512]{1,0:T(8,128)(2,1)S(1)} copy-done((bf16[1536,512]{1,0:T(8,128)(2,1)S(1)}, bf16[1536,512]{1,0:T(8,128)(2,1)}, u32[]{:S(2)}) %copy-start.3) | copy-done | bytes 1572888
  3.6 1.7 %prep_kv.1 = (bf16[4,12,8,16,128]{4,3,2,1,0:T(8,128)(2,1)S(1)}, bf16[4,12,8,16,128]{4,3,2,1,0:T(8,128)(2,1)S(1)}, bf16[4,2,192,128]{3,2,1,0:T(8,128)(2,1)S(1)}, ...) custom-call(s32[3,16]{1,0:T(4,128)S(1)} %copy-done.1, bf16[1536,512]{1,0:T(8,128)(2,1)S(1)} %copy-done.2, ...), custom_call_target="tpu_custom_call" | custom-call | flops 1000000000 | bytes 1 | tf_op jit(solution)/shard_map/prep_kv/pallas_call | solution.py:581
  5.3 3.1 %collective-permute-start = (bf16[4,2,192,128]{3,2,1,0:T(8,128)(2,1)S(1)}, bf16[4,2,192,128]{3,2,1,0:T(8,128)(2,1)S(1)}, u32[]{:S(2)}, u32[]{:S(2)}) collective-permute-start(bf16[4,2,192,128]{3,2,1,0:T(8,128)(2,1)S(1)} %get-tuple-element.69.token), channel_id=1, source_target_pairs={{0,8},{4,12},{8,0},{12,4},{16,24},{20,28},{24,16},{28,20},{1,9},{5... | collective-permute-start | bytes 1179656 | tf_op jit(solution)/shard_map/ppermute | solution.py:588
  8.4 1.2 %prep_q.1 = (bf16[4,12,8,16,128]{4,3,2,1,0:T(8,128)(2,1)S(1)}, bf16[8,192,128]{2,1,0:T(8,128)(2,1)S(1)}, bf16[4,3,192,128]{3,2,1,0:T(8,128)(2,1)S(1)}) custom-call(s32[3,16]{1,0:T(4,128)S(1)} %copy-done.1, bf16[1536,512]{1,0:T(8,128)(2,1)S(1)} %copy-done, bf16[4,12,8,16,128]{4,3,2,1,0:T(8,128)(2,1)S(1)} %get-tuple-element.66.kt.refs_5_, ...), custom_call_target="tpu_custom_call" | custom-call | flops 1000000000 | bytes 1 | tf_op jit(solution)/shard_map/prep_q/pallas_call | solution.py:589
  9.6 1.6 %collective-permute-start.3 = (bf16[8,192,128]{2,1,0:T(8,128)(2,1)S(1)}, bf16[8,192,128]{2,1,0:T(8,128)(2,1)S(1)}, u32[]{:S(2)}, u32[]{:S(2)}) collective-permute-start(bf16[8,192,128]{2,1,0:T(8,128)(2,1)S(1)} %get-tuple-element.85), channel_id=1, source_target_pairs={{0,4},{4,0},{8,12},{12,8},{16,20},{20,16},{24,28},{28,24},{1,5},{5... | collective-permute-start | bytes 1179656 | tf_op jit(solution)/shard_map/ppermute | solution.py:595
  11.2 5.8 %own0.1 = (f32[12,8,16,128]{3,2,1,0:T(8,128)S(1)}, f32[12,8,16,128]{3,2,1,0:T(8,128)S(1)}, f32[12,8,16,128]{3,2,1,0:T(8,128)S(1)}, f32[12,8,16,128]{3,2,1,0:T(8,128)S(1)}) custom-call(s32[3,16]{1,0:T(4,128)S(1)} %copy-done.1, bf16[4,12,8,16,128]{4,3,2,1,0:T(8,128)(2,1)S(1)} %get-tuple-element.68.qt.refs_4_, ...), custom_call_target="tpu_custom_call" | custom-call | flops 1000000000 | bytes 1 | tf_op jit(solution)/shard_map/own0/pallas_call | solution.py:600
  17.6 2.8 %collective-permute-start.1 = (bf16[2,2,2,192,128]{4,3,2,1,0:T(8,128)(2,1)S(1)}, bf16[2,2,2,192,128]{4,3,2,1,0:T(8,128)(2,1)S(1)}, u32[]{:S(2)}, u32[]{:S(2)}) collective-permute-start(bf16[2,2,2,192,128]{4,3,2,1,0:T(8,128)(2,1)S(1)} %pad_maximum_fusion.token), channel_id=1, source_target_pairs={{0,16},{4,20},{8,24},{12,28},{16,0},{20,4},{24,8},{28,12},{1,17},{... | collective-permute-start | bytes 1179656 | tf_op jit(solution)/shard_map/ppermute | solution.py:669
  20.4 1.6 %collective-permute-start.2 = (bf16[2,2,2,192,128]{4,3,2,1,0:T(8,128)(2,1)S(1)}, bf16[2,2,2,192,128]{4,3,2,1,0:T(8,128)(2,1)S(1)}, u32[]{:S(2)}, u32[]{:S(2)}) collective-permute-start(bf16[2,2,2,192,128]{4,3,2,1,0:T(8,128)(2,1)S(1)} %get-tuple-element.79), channel_id=1, source_target_pairs={{0,8},{4,12},{8,0},{12,4},{16,24},{20,28},{24,16},{28,20},{1,9},{5... | collective-permute-start | bytes 1179656 | tf_op jit(solution)/shard_map/ppermute | solution.py:669
  22.0 1.5 %collective-permute-start.4 = (bf16[4,3,192,128]{3,2,1,0:T(8,128)(2,1)S(1)}, bf16[4,3,192,128]{3,2,1,0:T(8,128)(2,1)S(1)}, u32[]{:S(2)}, u32[]{:S(2)}) collective-permute-start(bf16[4,3,192,128]{3,2,1,0:T(8,128)(2,1)S(1)} %get-tuple-element.92), channel_id=1, source_target_pairs={{0,4},{4,0},{8,12},{12,8},{16,20},{20,16},{24,28},{28,24},{1,5},{5... | collective-permute-start | bytes 1769480 | tf_op jit(solution)/shard_map/ppermute | solution.py:669
  23.5 5.8 %own2.1 = (f32[12,8,16,128]{3,2,1,0:T(8,128)S(1)}, f32[12,8,16,128]{3,2,1,0:T(8,128)S(1)}, f32[12,8,16,128]{3,2,1,0:T(8,128)S(1)}, f32[12,8,16,128]{3,2,1,0:T(8,128)S(1)}) custom-call(s32[3,16]{1,0:T(4,128)S(1)} %copy-done.1, bf16[4,12,8,16,128]{4,3,2,1,0:T(8,128)(2,1)S(1)} %get-tuple-element.68.qt.refs_4_, ...), custom_call_target="tpu_custom_call" | custom-call | flops 1000000000 | bytes 1 | tf_op jit(solution)/shard_map/own2/pallas_call | solution.py:600
  29.3 3.1 %lower.1 = (bf16[1600,128]{1,0:T(8,128)(2,1)S(1)}, f32[4,192,128]{2,1,0:T(8,128)S(1)}, f32[4,192,128]{2,1,0:T(8,128)S(1)}) custom-call(s32[3,16]{1,0:T(4,128)S(1)} %copy-done.1, bf16[8,192,128]{2,1,0:T(8,128)(2,1)S(1)} %collective-permute-done.3.got, bf16[4,12,8,16,128]{4,3,2,1,0:T(8,128)(2,1)S(1)} %get-tuple-element.68.qt.refs_4_, ...), custom_call_target="tpu_custom_call" | custom-call | flops 3000000000 | bytes 1 | tf_op jit(solution)/shard_map/lower/pallas_call | solution.py:608
  32.5 2.5 %weights.1 = (f32[12,8,16,128]{3,2,1,0:T(8,128)S(1)}, f32[12,8,16,128]{3,2,1,0:T(8,128)S(1)}, f32[12,8,16,128]{3,2,1,0:T(8,128)S(1)}, f32[12,8,16,128]{3,2,1,0:T(8,128)S(1)}, bf16[2048,2048]{1,0:T(8,128)(2,1)S(1)}) custom-call(s32[3,16]{1,0:T(4,128)S(1)} %copy-done.1, ...), custom_call_target="tpu_custom_call", output_to_operand_aliasing={{0}: (1, {}), {1}: (2, {}), {2}: (3, {}), {3}: (4, {})} | custom-call | flops 1000000000 | bytes 1 | tf_op jit(solution)/shard_map/weights/pallas_call | solution.py:680
  35.1 2.3 %collective-permute-done.1.far.refs_9_ = bf16[2,2,2,192,128]{4,3,2,1,0:T(8,128)(2,1)S(1)} collective-permute-done((bf16[2,2,2,192,128]{4,3,2,1,0:T(8,128)(2,1)S(1)}, bf16[2,2,2,192,128]{4,3,2,1,0:T(8,128)(2,1)S(1)}, u32[]{:S(2)}, u32[]{:S(2)}) %collective-permute-start.1) | collective-permute-done | bytes 393248 | tf_op jit(solution)/shard_map/ppermute | solution.py:669
  37.6 1.3 %collective-permute-start.8 = (bf16[2,2,2,192,128]{4,3,2,1,0:T(8,128)(2,1)S(1)}, bf16[2,2,2,192,128]{4,3,2,1,0:T(8,128)(2,1)S(1)}, u32[]{:S(2)}, u32[]{:S(2)}) collective-permute-start(bf16[2,2,2,192,128]{4,3,2,1,0:T(8,128)(2,1)S(1)} %get-tuple-element.103), channel_id=1, source_target_pairs={{0,8},{4,12},{8,0},{12,4},{16,24},{20,28},{24,16},{28,20},{1,9},{5... | collective-permute-start | bytes 1179656 | tf_op jit(solution)/shard_map/ppermute | solution.py:669
  38.9 2.3 %collective-permute-start.9 = (bf16[2,2,2,192,128]{4,3,2,1,0:T(8,128)(2,1)S(1)}, bf16[2,2,2,192,128]{4,3,2,1,0:T(8,128)(2,1)S(1)}, u32[]{:S(2)}, u32[]{:S(2)}) collective-permute-start(bf16[2,2,2,192,128]{4,3,2,1,0:T(8,128)(2,1)S(1)} %pad_maximum_fusion.1.token), channel_id=1, source_target_pairs={{0,16},{4,20},{8,24},{12,28},{16,0},{20,4},{24,8},{28,12},{1,17},{... | collective-permute-start | bytes 1179656 | tf_op jit(solution)/shard_map/ppermute | solution.py:669
  41.2 2.5 %partner0.1.refs_10_ = bf16[1216,128]{1,0:T(8,128)(2,1)S(1)} custom-call(s32[3,16]{1,0:T(4,128)S(1)} %copy-done.1, bf16[4,12,8,16,128]{4,3,2,1,0:T(8,128)(2,1)S(1)} %get-tuple-element.66.kt.refs_5_, bf16[4,12,8,16,128]{4,3,2,1,0:T(8,128)(2,1)S(1)} %get-tuple-element.67.vt.refs_6_, bf16[4,3,192,128]{3,2,1,0:T(8,128)(2,1)S(1)} %collective-permute-done.4.q23, ...), custom_call_target="tpu_custom_call" | custom-call | flops 1000000000 | bytes 1 | tf_op jit(solution)/shard_map/partner0/pallas_call | solution.py:617
  43.7 1.5 %collective-permute-start.5 = (bf16[1216,128]{1,0:T(8,128)(2,1)S(1)}, bf16[1216,128]{1,0:T(8,128)(2,1)S(1)}, u32[]{:S(2)}, u32[]{:S(2)}) collective-permute-start(bf16[1216,128]{1,0:T(8,128)(2,1)S(1)} %partner0.1.refs_10_), channel_id=1, source_target_pairs={{0,4},{4,0},{8,12},{12,8},{16,20},{20,16},{24,28},{28,24},{1,5},{5... | collective-permute-start | bytes 933896 | tf_op jit(solution)/shard_map/ppermute | solution.py:669
  45.2 2.5 %mine0.1 = (f32[12,8,16,128]{3,2,1,0:T(8,128)S(1)}, f32[12,8,16,128]{3,2,1,0:T(8,128)S(1)}, f32[12,8,16,128]{3,2,1,0:T(8,128)S(1)}, f32[12,8,16,128]{3,2,1,0:T(8,128)S(1)}) custom-call(s32[3,16]{1,0:T(4,128)S(1)} %copy-done.1, ...), custom_call_target="tpu_custom_call", output_to_operand_aliasing={{0}: (1, {}), {1}: (2, {}), {2}: (3, {}), {3}: (4, {})} | custom-call | flops 10000000000 | bytes 1 | tf_op jit(solution)/shard_map/mine0/pallas_call | solution.py:626
  47.7 2.1 %last.1.refs_5_ = bf16[832,128]{1,0:T(8,128)(2,1)S(1)} custom-call(s32[3,16]{1,0:T(4,128)S(1)} %copy-done.1, bf16[1600,128]{1,0:T(8,128)(2,1)S(1)} %collective-permute-done.6.turn.refs_6_, bf16[4,12,8,16,128]{4,3,2,1,0:T(8,128)(2,1)S(1)} %get-tuple-element.66.kt.refs_5_, bf16[4,12,8,16,128]{4,3,2,1,0:T(8,128)(2,1)S(1)} %get-tuple-element.67.vt.refs_6_, ...), custom_call_target="tpu_custom_call" | custom-call | flops 1000000000 | bytes 1 | tf_op jit(solution)/shard_map/last/pallas_call | solution.py:697
  49.9 3.2 %collective-permute-done.5.refs_4_ = bf16[1216,128]{1,0:T(8,128)(2,1)S(1)} collective-permute-done((bf16[1216,128]{1,0:T(8,128)(2,1)S(1)}, bf16[1216,128]{1,0:T(8,128)(2,1)S(1)}, u32[]{:S(2)}, u32[]{:S(2)}) %collective-permute-start.5) | collective-permute-done | bytes 311328 | tf_op jit(solution)/shard_map/ppermute | solution.py:669
  53.1 2.2 %finish0.1 = (bf16[384,256]{1,0:T(8,128)(2,1)S(1)}, bf16[384,256]{1,0:T(8,128)(2,1)S(1)}, bf16[2,384,256]{2,1,0:T(8,128)(2,1)S(1)}, bf16[8,128]{1,0:T(8,128)(2,1...) custom-call(s32[3,16]{1,0:T(4,128)S(1)} %copy-done.1, ...), custom_call_target="tpu_custom_call", output_to_operand_aliasing={{4}: (1, {}), {5}: (2, {}), {6}: (3, {}), {7}: (4, {})} | custom-call | flops 1000000000 | bytes 1 | tf_op jit(solution)/shard_map/finish0/pallas_call | solution.py:638
  55.3 1.5 %collective-permute-start.7 = (bf16[2,384,256]{2,1,0:T(8,128)(2,1)S(1)}, bf16[2,384,256]{2,1,0:T(8,128)(2,1)S(1)}, u32[]{:S(2)}, u32[]{:S(2)}) collective-permute-start(bf16[2,384,256]{2,1,0:T(8,128)(2,1)S(1)} %get-tuple-element.98), channel_id=1, source_target_pairs={{0,2},{1,3},{2,0},{3,1},{4,6},{5,7},{6,4},{7,5},{8,10},{9,11},{10,... | collective-permute-start | bytes 1179656 | tf_op jit(solution)/shard_map/ppermute | solution.py:669
  56.8 1.9 %collective-permute-done.9.far.refs_9_ = bf16[2,2,2,192,128]{4,3,2,1,0:T(8,128)(2,1)S(1)} collective-permute-done((bf16[2,2,2,192,128]{4,3,2,1,0:T(8,128)(2,1)S(1)}, bf16[2,2,2,192,128]{4,3,2,1,0:T(8,128)(2,1)S(1)}, u32[]{:S(2)}, u32[]{:S(2)}) %collective-permute-start.9) | collective-permute-done | bytes 393248 | tf_op jit(solution)/shard_map/ppermute | solution.py:669
  58.7 2.4 %partner2.1 = (bf16[640,128]{1,0:T(8,128)(2,1)S(1)}, bf16[640,128]{1,0:T(8,128)(2,1)S(1)}) custom-call(s32[3,16]{1,0:T(4,128)S(1)} %copy-done.1, bf16[4,12,8,16,128]{4,3,2,1,0:T(8,128)(2,1)S(1)} %get-tuple-element.66.kt.refs_5_, bf16[4,12,8,16,128]{4,3,2,1,0:T(8,128)(2,1)S(1)} %get-tuple-element.67.vt.refs_6_, ...), custom_call_target="tpu_custom_call" | custom-call | flops 10000000000 | bytes 1 | tf_op jit(solution)/shard_map/partner2/pallas_call | solution.py:617
  61.1 1.5 %collective-permute-start.10 = (bf16[640,128]{1,0:T(8,128)(2,1)S(1)}, bf16[640,128]{1,0:T(8,128)(2,1)S(1)}, u32[]{:S(2)}, u32[]{:S(2)}) collective-permute-start(bf16[640,128]{1,0:T(8,128)(2,1)S(1)} %get-tuple-element.112), channel_id=1, source_target_pairs={{0,4},{4,0},{8,12},{12,8},{16,20},{20,16},{24,28},{28,24},{1,5},{5... | collective-permute-start | bytes 491528 | tf_op jit(solution)/shard_map/ppermute | solution.py:669
  63.2 1.9 %mine2.1 = (f32[12,8,16,128]{3,2,1,0:T(8,128)S(1)}, f32[12,8,16,128]{3,2,1,0:T(8,128)S(1)}, f32[12,8,16,128]{3,2,1,0:T(8,128)S(1)}, f32[12,8,16,128]{3,2,1,0:T(8,128)S(1)}) custom-call(s32[3,16]{1,0:T(4,128)S(1)} %copy-done.1, ...), custom_call_target="tpu_custom_call", output_to_operand_aliasing={{0}: (1, {}), {1}: (2, {}), {2}: (3, {}), {3}: (4, {})} | custom-call | flops 1000000000 | bytes 1 | tf_op jit(solution)/shard_map/mine2/pallas_call | solution.py:626
  65.4 1.7 %collective-permute-done.10.refs_2_ = bf16[640,128]{1,0:T(8,128)(2,1)S(1)} collective-permute-done((bf16[640,128]{1,0:T(8,128)(2,1)S(1)}, bf16[640,128]{1,0:T(8,128)(2,1)S(1)}, u32[]{:S(2)}, u32[]{:S(2)}) %collective-permute-start.10) | collective-permute-done | bytes 163872 | tf_op jit(solution)/shard_map/ppermute | solution.py:669
  67.2 1.3 %finish2.1 = (bf16[384,128]{1,0:T(8,128)(2,1)S(1)}, bf16[384,128]{1,0:T(8,128)(2,1)S(1)}, bf16[2,384,128]{2,1,0:T(8,128)(2,1)S(1)}, bf16[8,128]{1,0:T(8,128)(2,1...) custom-call(s32[3,16]{1,0:T(4,128)S(1)} %copy-done.1, ...), custom_call_target="tpu_custom_call", output_to_operand_aliasing={{4}: (1, {}), {5}: (2, {})} | custom-call | flops 1000000000 | bytes 1 | tf_op jit(solution)/shard_map/finish2/pallas_call | solution.py:638
  68.5 1.6 %collective-permute-start.12 = (bf16[2,384,128]{2,1,0:T(8,128)(2,1)S(1)}, bf16[2,384,128]{2,1,0:T(8,128)(2,1)S(1)}, u32[]{:S(2)}, u32[]{:S(2)}) collective-permute-start(bf16[2,384,128]{2,1,0:T(8,128)(2,1)S(1)} %get-tuple-element.114), channel_id=1, source_target_pairs={{0,2},{1,3},{2,0},{3,1},{4,6},{5,7},{6,4},{7,5},{8,10},{9,11},{10,... | collective-permute-start | bytes 589832 | tf_op jit(solution)/shard_map/ppermute | solution.py:669
  73.2 3.1 %project0.1.refs_6_.refs_8_ = f32[384,2048]{1,0:T(8,128)S(1)} custom-call(bf16[384,256]{1,0:T(8,128)(2,1)S(1)} %get-tuple-element.104.token.refs_0_, bf16[384,256]{1,0:T(8,128)(2,1)S(1)} %collective-permute-done.13.refs_1_, bf16[2,384,256]{2,1,0:T(8,128)(2,1)S(1)} %collective-permute-done.7.refs_2_, bf16[384,256]{1,0:T(8,128)(2,1)S(1)} %collective-permute-done.14.refs_3_, ...), custom_call_target="tpu_custom_call" | custom-call | flops 1000000000 | bytes 1 | tf_op jit(solution)/shard_map/project0/pallas_call | solution.py:655
  78.1 3.0 %project1280.1 = bf16[384,2048]{1,0:T(8,128)(2,1)} custom-call(bf16[2,384,128]{2,1,0:T(8,128)(2,1)S(1)} %collective-permute-done.12.refs_0_, bf16[384,128]{1,0:T(8,128)(2,1)S(1)} %collective-permute-done.17.refs_1_, bf16[384,128]{1,0:T(8,128)(2,1)S(1)} %get-tuple-element.121.refs_7_.refs_2_, bf16[384,128]{1,0:T(8,128)(2,1)S(1)} %collective-permute-done.18.refs_3_, ...), custom_call_target="tpu_custom_call" | custom-call | flops 1000000000 | bytes 1 | tf_op jit(solution)/shard_map/project1280/pallas_call | solution.py:655
  (45 shorter events, 7.3 us)
Async XLA Ops:
  0.0 8.4 %copy-start = (bf16[1536,512]{1,0:T(8,128)(2,1)S(1)}, bf16[1536,512]{1,0:T(8,128)(2,1)}, u32[]{:S(2)}) copy-start(bf16[1536,512]{1,0:T(8,128)(2,1)} %q_ref.1) | copy-start | bytes 4718596
  0.0 0.8 copy-start.1
  0.8 1.4 %copy-start.2 = (bf16[1536,512]{1,0:T(8,128)(2,1)S(1)}, bf16[1536,512]{1,0:T(8,128)(2,1)}, u32[]{:S(2)}) copy-start(bf16[1536,512]{1,0:T(8,128)(2,1)} %k_ref.1) | copy-start | bytes 4718596
  2.2 1.4 %copy-start.3 = (bf16[1536,512]{1,0:T(8,128)(2,1)S(1)}, bf16[1536,512]{1,0:T(8,128)(2,1)}, u32[]{:S(2)}) copy-start(bf16[1536,512]{1,0:T(8,128)(2,1)} %v_ref.1) | copy-start | bytes 4718596
  5.3 12.2 %collective-permute-start = (bf16[4,2,192,128]{3,2,1,0:T(8,128)(2,1)S(1)}, bf16[4,2,192,128]{3,2,1,0:T(8,128)(2,1)S(1)}, u32[]{:S(2)}, u32[]{:S(2)}) collective-permute-start(bf16[4,2,192,128]{3,2,1,0:T(8,128)(2,1)S(1)} %get-tuple-element.69.token), channel_id=1, source_target_pairs={{0,8},{4,12},{8,0},{12,4},{16,24},{20,28},{24,16},{28,20},{1,9},{5... | collective-permute-start | bytes 1179656 | tf_op jit(solution)/shard_map/ppermute | solution.py:588
  9.6 19.7 %collective-permute-start.3 = (bf16[8,192,128]{2,1,0:T(8,128)(2,1)S(1)}, bf16[8,192,128]{2,1,0:T(8,128)(2,1)S(1)}, u32[]{:S(2)}, u32[]{:S(2)}) collective-permute-start(bf16[8,192,128]{2,1,0:T(8,128)(2,1)S(1)} %get-tuple-element.85), channel_id=1, source_target_pairs={{0,4},{4,0},{8,12},{12,8},{16,20},{20,16},{24,28},{28,24},{1,5},{5... | collective-permute-start | bytes 1179656 | tf_op jit(solution)/shard_map/ppermute | solution.py:595
  17.6 19.8 %collective-permute-start.1 = (bf16[2,2,2,192,128]{4,3,2,1,0:T(8,128)(2,1)S(1)}, bf16[2,2,2,192,128]{4,3,2,1,0:T(8,128)(2,1)S(1)}, u32[]{:S(2)}, u32[]{:S(2)}) collective-permute-start(bf16[2,2,2,192,128]{4,3,2,1,0:T(8,128)(2,1)S(1)} %pad_maximum_fusion.token), channel_id=1, source_target_pairs={{0,16},{4,20},{8,24},{12,28},{16,0},{20,4},{24,8},{28,12},{1,17},{... | collective-permute-start | bytes 1179656 | tf_op jit(solution)/shard_map/ppermute | solution.py:669
  20.4 17.2 %collective-permute-start.2 = (bf16[2,2,2,192,128]{4,3,2,1,0:T(8,128)(2,1)S(1)}, bf16[2,2,2,192,128]{4,3,2,1,0:T(8,128)(2,1)S(1)}, u32[]{:S(2)}, u32[]{:S(2)}) collective-permute-start(bf16[2,2,2,192,128]{4,3,2,1,0:T(8,128)(2,1)S(1)} %get-tuple-element.79), channel_id=1, source_target_pairs={{0,8},{4,12},{8,0},{12,4},{16,24},{20,28},{24,16},{28,20},{1,9},{5... | collective-permute-start | bytes 1179656 | tf_op jit(solution)/shard_map/ppermute | solution.py:669
  22.0 19.2 %collective-permute-start.4 = (bf16[4,3,192,128]{3,2,1,0:T(8,128)(2,1)S(1)}, bf16[4,3,192,128]{3,2,1,0:T(8,128)(2,1)S(1)}, u32[]{:S(2)}, u32[]{:S(2)}) collective-permute-start(bf16[4,3,192,128]{3,2,1,0:T(8,128)(2,1)S(1)} %get-tuple-element.92), channel_id=1, source_target_pairs={{0,4},{4,0},{8,12},{12,8},{16,20},{20,16},{24,28},{28,24},{1,5},{5... | collective-permute-start | bytes 1769480 | tf_op jit(solution)/shard_map/ppermute | solution.py:669
  23.5 9.0 %slice-start = ((s8[8388608]{0:T(1024)(128)(4,1)}), s8[4194304]{0:T(1024)(128)(4,1)S(1)}, s32[]{:S(2)}) async-start(s8[8388608]{0:T(1024)(128)(4,1)} %bitcast.12), calls=%async_computation | async-start | bytes 8388608
  29.3 3.2 %slice-start.1 = ((s8[8388608]{0:T(1024)(128)(4,1)}), s8[4194304]{0:T(1024)(128)(4,1)S(1)}, s32[]{:S(2)}) async-start(s8[8388608]{0:T(1024)(128)(4,1)} %bitcast.12), calls=%async_computation.1 | async-start | bytes 8388608
  32.5 15.2 %collective-permute-start.6 = (bf16[1600,128]{1,0:T(8,128)(2,1)S(1)}, bf16[1600,128]{1,0:T(8,128)(2,1)S(1)}, u32[]{:S(2)}, u32[]{:S(2)}) collective-permute-start(bf16[1600,128]{1,0:T(8,128)(2,1)S(1)} %get-tuple-element.88.refs_10_), channel_id=1, source_target_pairs={{0,4},{4,0},{8,12},{12,8},{16,20},{20,16},{24,28},{28,24},{1,5},{5... | collective-permute-start | bytes 1228808 | tf_op jit(solution)/shard_map/ppermute | solution.py:669
  37.6 19.2 %collective-permute-start.8 = (bf16[2,2,2,192,128]{4,3,2,1,0:T(8,128)(2,1)S(1)}, bf16[2,2,2,192,128]{4,3,2,1,0:T(8,128)(2,1)S(1)}, u32[]{:S(2)}, u32[]{:S(2)}) collective-permute-start(bf16[2,2,2,192,128]{4,3,2,1,0:T(8,128)(2,1)S(1)} %get-tuple-element.103), channel_id=1, source_target_pairs={{0,8},{4,12},{8,0},{12,4},{16,24},{20,28},{24,16},{28,20},{1,9},{5... | collective-permute-start | bytes 1179656 | tf_op jit(solution)/shard_map/ppermute | solution.py:669
  38.9 19.8 %collective-permute-start.9 = (bf16[2,2,2,192,128]{4,3,2,1,0:T(8,128)(2,1)S(1)}, bf16[2,2,2,192,128]{4,3,2,1,0:T(8,128)(2,1)S(1)}, u32[]{:S(2)}, u32[]{:S(2)}) collective-permute-start(bf16[2,2,2,192,128]{4,3,2,1,0:T(8,128)(2,1)S(1)} %pad_maximum_fusion.1.token), channel_id=1, source_target_pairs={{0,16},{4,20},{8,24},{12,28},{16,0},{20,4},{24,8},{28,12},{1,17},{... | collective-permute-start | bytes 1179656 | tf_op jit(solution)/shard_map/ppermute | solution.py:669
  43.7 9.4 %collective-permute-start.5 = (bf16[1216,128]{1,0:T(8,128)(2,1)S(1)}, bf16[1216,128]{1,0:T(8,128)(2,1)S(1)}, u32[]{:S(2)}, u32[]{:S(2)}) collective-permute-start(bf16[1216,128]{1,0:T(8,128)(2,1)S(1)} %partner0.1.refs_10_), channel_id=1, source_target_pairs={{0,4},{4,0},{8,12},{12,8},{16,20},{20,16},{24,28},{28,24},{1,5},{5... | collective-permute-start | bytes 933896 | tf_op jit(solution)/shard_map/ppermute | solution.py:669
  49.8 15.6 %collective-permute-start.11 = (bf16[832,128]{1,0:T(8,128)(2,1)S(1)}, bf16[832,128]{1,0:T(8,128)(2,1)S(1)}, u32[]{:S(2)}, u32[]{:S(2)}) collective-permute-start(bf16[832,128]{1,0:T(8,128)(2,1)S(1)} %last.1.refs_5_), channel_id=1, source_target_pairs={{0,4},{4,0},{8,12},{12,8},{16,20},{20,16},{24,28},{28,24},{1,5},{5... | collective-permute-start | bytes 638984 | tf_op jit(solution)/shard_map/ppermute | solution.py:669
  55.3 9.8 %collective-permute-start.7 = (bf16[2,384,256]{2,1,0:T(8,128)(2,1)S(1)}, bf16[2,384,256]{2,1,0:T(8,128)(2,1)S(1)}, u32[]{:S(2)}, u32[]{:S(2)}) collective-permute-start(bf16[2,384,256]{2,1,0:T(8,128)(2,1)S(1)} %get-tuple-element.98), channel_id=1, source_target_pairs={{0,2},{1,3},{2,0},{3,1},{4,6},{5,7},{6,4},{7,5},{8,10},{9,11},{10,... | collective-permute-start | bytes 1179656 | tf_op jit(solution)/shard_map/ppermute | solution.py:669
  61.1 6.1 %collective-permute-start.10 = (bf16[640,128]{1,0:T(8,128)(2,1)S(1)}, bf16[640,128]{1,0:T(8,128)(2,1)S(1)}, u32[]{:S(2)}, u32[]{:S(2)}) collective-permute-start(bf16[640,128]{1,0:T(8,128)(2,1)S(1)} %get-tuple-element.112), channel_id=1, source_target_pairs={{0,4},{4,0},{8,12},{12,8},{16,20},{20,16},{24,28},{28,24},{1,5},{5... | collective-permute-start | bytes 491528 | tf_op jit(solution)/shard_map/ppermute | solution.py:669
  62.7 9.1 %collective-permute-start.13 = (bf16[384,256]{1,0:T(8,128)(2,1)S(1)}, bf16[384,256]{1,0:T(8,128)(2,1)S(1)}, u32[]{:S(2)}, u32[]{:S(2)}) collective-permute-start(bf16[384,256]{1,0:T(8,128)(2,1)S(1)} %get-tuple-element.115), channel_id=1, source_target_pairs={{0,1},{1,0},{2,3},{3,2},{4,5},{5,4},{6,7},{7,6},{8,9},{9,8},{10,11... | collective-permute-start | bytes 589832 | tf_op jit(solution)/shard_map/ppermute | solution.py:669
  62.7 7.5 %collective-permute-start.16 = (bf16[640,128]{1,0:T(8,128)(2,1)S(1)}, bf16[640,128]{1,0:T(8,128)(2,1)S(1)}, u32[]{:S(2)}, u32[]{:S(2)}) collective-permute-start(bf16[640,128]{1,0:T(8,128)(2,1)S(1)} %get-tuple-element.105.refs_10_), channel_id=1, source_target_pairs={{0,4},{4,0},{8,12},{12,8},{16,20},{20,16},{24,28},{28,24},{1,5},{5... | collective-permute-start | bytes 491528 | tf_op jit(solution)/shard_map/ppermute | solution.py:669
  65.1 8.0 %collective-permute-start.14 = (bf16[384,256]{1,0:T(8,128)(2,1)S(1)}, bf16[384,256]{1,0:T(8,128)(2,1)S(1)}, u32[]{:S(2)}, u32[]{:S(2)}) collective-permute-start(bf16[384,256]{1,0:T(8,128)(2,1)S(1)} %slice_bitcast_fusion), channel_id=1, source_target_pairs={{0,1},{1,0},{2,3},{3,2},{4,5},{5,4},{6,7},{7,6},{8,9},{9,8},{10,11... | collective-permute-start | bytes 589832 | tf_op jit(solution)/shard_map/ppermute | solution.py:669
  68.5 7.8 %collective-permute-start.12 = (bf16[2,384,128]{2,1,0:T(8,128)(2,1)S(1)}, bf16[2,384,128]{2,1,0:T(8,128)(2,1)S(1)}, u32[]{:S(2)}, u32[]{:S(2)}) collective-permute-start(bf16[2,384,128]{2,1,0:T(8,128)(2,1)S(1)} %get-tuple-element.114), channel_id=1, source_target_pairs={{0,2},{1,3},{2,0},{3,1},{4,6},{5,7},{6,4},{7,5},{8,10},{9,11},{10,... | collective-permute-start | bytes 589832 | tf_op jit(solution)/shard_map/ppermute | solution.py:669
  70.1 2.6 %collective-permute-start.15 = (bf16[384,128]{1,0:T(8,128)(2,1)S(1)}, bf16[384,128]{1,0:T(8,128)(2,1)S(1)}, u32[]{:S(2)}, u32[]{:S(2)}) collective-permute-start(bf16[384,128]{1,0:T(8,128)(2,1)S(1)} %get-tuple-element.118), channel_id=1, source_target_pairs={{0,1},{1,0},{2,3},{3,2},{4,5},{5,4},{6,7},{7,6},{8,9},{9,8},{10,11... | collective-permute-start | bytes 294920 | tf_op jit(solution)/shard_map/ppermute | solution.py:669
  71.2 6.0 %collective-permute-start.18 = (bf16[384,128]{1,0:T(8,128)(2,1)S(1)}, bf16[384,128]{1,0:T(8,128)(2,1)S(1)}, u32[]{:S(2)}, u32[]{:S(2)}) collective-permute-start(bf16[384,128]{1,0:T(8,128)(2,1)S(1)} %get-tuple-element.123), channel_id=1, source_target_pairs={{0,1},{1,0},{2,3},{3,2},{4,5},{5,4},{6,7},{7,6},{8,9},{9,8},{10,11... | collective-permute-start | bytes 294920 | tf_op jit(solution)/shard_map/ppermute | solution.py:669
  71.7 5.6 %collective-permute-start.19 = (bf16[384,128]{1,0:T(8,128)(2,1)S(1)}, bf16[384,128]{1,0:T(8,128)(2,1)S(1)}, u32[]{:S(2)}, u32[]{:S(2)}) collective-permute-start(bf16[384,128]{1,0:T(8,128)(2,1)S(1)} %get-tuple-element.124), channel_id=1, source_target_pairs={{0,2},{1,3},{2,0},{3,1},{4,6},{5,7},{6,4},{7,5},{8,10},{9,11},{10,... | collective-permute-start | bytes 294920 | tf_op jit(solution)/shard_map/ppermute | solution.py:669
  72.7 5.1 %collective-permute-start.20 = (bf16[384,128]{1,0:T(8,128)(2,1)S(1)}, bf16[384,128]{1,0:T(8,128)(2,1)S(1)}, u32[]{:S(2)}, u32[]{:S(2)}) collective-permute-start(bf16[384,128]{1,0:T(8,128)(2,1)S(1)} %get-tuple-element.125), channel_id=1, source_target_pairs={{0,3},{1,2},{2,1},{3,0},{4,7},{5,6},{6,5},{7,4},{8,11},{9,10},{10,... | collective-permute-start | bytes 294920 | tf_op jit(solution)/shard_map/ppermute | solution.py:669
  76.3 1.7 %collective-permute-start.17 = (bf16[384,128]{1,0:T(8,128)(2,1)S(1)}, bf16[384,128]{1,0:T(8,128)(2,1)S(1)}, u32[]{:S(2)}, u32[]{:S(2)}) collective-permute-start(bf16[384,128]{1,0:T(8,128)(2,1)S(1)} %slice_bitcast_fusion.5), channel_id=1, source_target_pairs={{0,1},{1,0},{2,3},{3,2},{4,5},{5,4},{6,7},{7,6},{8,9},{9,8},{10,11... | collective-permute-start | bytes 294920 | tf_op jit(solution)/shard_map/ppermute | solution.py:669

commit v6 on v5

--- a/solution.py
+++ b/solution.py
@@ -122,8 +122,12 @@
                 dst[h, b] = x[:, h * DH : (h + 1) * DH].reshape(RES, SUB, DH)
 
 
-def prep_kv_kernel(off_ref, k_ref, v_ref, kt, vt, kv3, *kv2):
-    regroup((k_ref, v_ref), (kt, vt))
+def prep_k_kernel(k_ref, kt):
+    regroup((k_ref,), (kt,))
+
+
+def prep_v_kernel(off_ref, v_ref, kt, vt, kv3, *kv2):
+    regroup((v_ref,), (vt,))
     for h in range(kt.shape[0]):
         o2, o3 = (shift_of(off_ref, level, h) for level in (2, 3))
         (g,) = [g for g, members in enumerate(GROUPS) if h in members]
@@ -514,7 +518,7 @@
             [src[0, rows, :] if len(src.shape) == 3 else src[rows, :] for src in pieces], axis=1
         )
         plain[rows, :] = jnp.dot(back, x, preferred_element_type=F32).astype(BF16)
-    tile = 512
+    tile = 1024
     steps = out.shape[1] // tile
 
     def copy(step):
@@ -578,13 +582,14 @@
     far = [(i, i ^ 4) for i in range(ctx_size)]
     over = [[(i, i ^ t) for i in range(4)] for t in range(4)]
 
-    kt, vt, kv3, *kv2 = call(
-        prep_kv_kernel,
+    kt = call(prep_k_kernel, [VMEM], regrouped, "prep_k")(keys)
+    vt, kv3, *kv2 = call(
+        prep_v_kernel,
         [SMEM, VMEM, VMEM],
-        [regrouped, regrouped, shape(heads, 2, *piece)]
+        [regrouped, shape(heads, 2, *piece)]
         + [shape(len(members), 2, 2, *piece) for members in GROUPS],
-        "prep_kv",
-    )(offsets, keys, values)
+        "prep_v",
+    )(offsets, values, kt)
     kv3_near = lax.ppermute(kv3, "ctx", near)
     qt, first, q23 = call(
         prep_q_kernel,
@@ -650,7 +655,7 @@
         if final:
             scratch += [
                 pltpu.VMEM((rows_here // 4, model), BF16),
-                pltpu.SemaphoreType.DMA((model // 512,)),
+                pltpu.SemaphoreType.DMA((model // 1024,)),
             ]
         return call(
             functools.partial(project_kernel, first, len(before), final),

time: 81.5 us -> 80.1 us (0.983)
  local copies, waits for them, and re-layouts: 3.71 us -> 2.34 us
    unnamed x12, local copies, waits for them, and re-layouts: 3.63 us -> 2.27 us
    pallas_call x1 -> x2, Pallas kernels: 1.66 us -> 1.78 us  [the longest x1 1.21 us: body(): call(prep_v_kernel, [SMEM, VMEM, VMEM], [regrouped, shape(heads, 2, *piec...]
  transfers between devices with their start and end apart: 21 -> 21, of which waited for: 9 -> 8; matrix products, arithmetic and copies ran while one was open for 0% -> 0% of each run, Pallas kernels for 46% -> 47%
where the time goes in v6:
time: 80.1 us; the launch traced here: 79.5 us
  Pallas kernels  42 us (52%)
  starting transfers between devices  24.1 us (30%)
  waiting for transfers between devices  10.6 us (13%)
  local copies, waits for them, and re-layouts  2.34 us (3%)
    ppermute x19, starting transfers between devices, send(): return lax.ppermute(value, axis, pairs)  19.4 us
    pallas_call x2, Pallas kernels, own(): call(functools.partial(own_kernel, members), [SMEM, VMEM, VMEM, VMEM, ANY...  11.6 us
    ppermute x19, waiting for transfers between devices, send(): return lax.ppermute(value, axis, pairs)  10.2 us
    pallas_call x2, Pallas kernels, project(): call(functools.partial(project_kernel, first, len(before), final), [VMEM]...  5.62 us
    pallas_call x2, Pallas kernels, partner(): call(functools.partial(partner_kernel, members), [SMEM] + [VMEM] * 6 + [A...  4.93 us
    pallas_call x3, Pallas kernels, finished(): call(functools.partial(finish_kernel, members, stacked), [SMEM] + [VMEM]...  4.61 us
    pallas_call x2, Pallas kernels, mine(): call(functools.partial(mine_kernel, members, which), [SMEM] + [VMEM] * (l...  4.44 us
    pallas_call x1, Pallas kernels, lower(): call(functools.partial(lower_kernel, members), [SMEM] + [VMEM] * 4 + [ANY...  3.16 us
  transfers between devices with their start and end apart: 21, of which 8 were waited for; matrix products, arithmetic and copies ran while one was open for 0% of the time, Pallas kernels for 47%

profile of v6, /device:TPU:0, one launch (start us, length us, event | category | flops | bytes accessed | tf_op | source)
XLA Modules:
  0.0 79.5 jit_solution(17216809856484498)
XLA Ops:
  0.0 1.4 %copy-done.2 = bf16[1536,512]{1,0:T(8,128)(2,1)S(1)} copy-done((bf16[1536,512]{1,0:T(8,128)(2,1)S(1)}, bf16[1536,512]{1,0:T(8,128)(2,1)}, u32[]{:S(2)}) %copy-start.2) | copy-done | bytes 1572888
  2.8 1.2 %prep_v.1 = (bf16[4,12,8,16,128]{4,3,2,1,0:T(8,128)(2,1)S(1)}, bf16[4,2,192,128]{3,2,1,0:T(8,128)(2,1)S(1)}, bf16[2,2,2,192,128]{4,3,2,1,0:T(8,128)(2,1)S(1)}, bf16[2,2,2,192,128]{4,3,2,1,0:T(8,128)(2,1)S(1)}) custom-call(s32[3,16]{1,0:T(4,128)S(1)} %copy-done.1, bf16[1536,512]{1,0:T(8,128)(2,1)S(1)} %copy-done.3, ...), custom_call_target="tpu_custom_call" | custom-call | flops 1000000000 | bytes 1 | tf_op jit(solution)/shard_map/prep_v/pallas_call | solution.py:586
  4.1 3.1 %collective-permute-start = (bf16[4,2,192,128]{3,2,1,0:T(8,128)(2,1)S(1)}, bf16[4,2,192,128]{3,2,1,0:T(8,128)(2,1)S(1)}, u32[]{:S(2)}, u32[]{:S(2)}) collective-permute-start(bf16[4,2,192,128]{3,2,1,0:T(8,128)(2,1)S(1)} %get-tuple-element.67.token), channel_id=1, source_target_pairs={{0,8},{4,12},{8,0},{12,4},{16,24},{20,28},{24,16},{28,20},{1,9},{5... | collective-permute-start | bytes 1179656 | tf_op jit(solution)/shard_map/ppermute | solution.py:593
  7.2 1.2 %prep_q.1 = (bf16[4,12,8,16,128]{4,3,2,1,0:T(8,128)(2,1)S(1)}, bf16[8,192,128]{2,1,0:T(8,128)(2,1)S(1)}, bf16[4,3,192,128]{3,2,1,0:T(8,128)(2,1)S(1)}) custom-call(s32[3,16]{1,0:T(4,128)S(1)} %copy-done.1, bf16[1536,512]{1,0:T(8,128)(2,1)S(1)} %copy-done, bf16[4,12,8,16,128]{4,3,2,1,0:T(8,128)(2,1)S(1)} %prep_k.1.kt.refs_5_, ...), custom_call_target="tpu_custom_call" | custom-call | flops 1000000000 | bytes 1 | tf_op jit(solution)/shard_map/prep_q/pallas_call | solution.py:594
  8.4 1.6 %collective-permute-start.3 = (bf16[8,192,128]{2,1,0:T(8,128)(2,1)S(1)}, bf16[8,192,128]{2,1,0:T(8,128)(2,1)S(1)}, u32[]{:S(2)}, u32[]{:S(2)}) collective-permute-start(bf16[8,192,128]{2,1,0:T(8,128)(2,1)S(1)} %get-tuple-element.83), channel_id=1, source_target_pairs={{0,4},{4,0},{8,12},{12,8},{16,20},{20,16},{24,28},{28,24},{1,5},{5... | collective-permute-start | bytes 1179656 | tf_op jit(solution)/shard_map/ppermute | solution.py:600
  10.0 5.8 %own0.1 = (f32[12,8,16,128]{3,2,1,0:T(8,128)S(1)}, f32[12,8,16,128]{3,2,1,0:T(8,128)S(1)}, f32[12,8,16,128]{3,2,1,0:T(8,128)S(1)}, f32[12,8,16,128]{3,2,1,0:T(8,128)S(1)}) custom-call(s32[3,16]{1,0:T(4,128)S(1)} %copy-done.1, bf16[4,12,8,16,128]{4,3,2,1,0:T(8,128)(2,1)S(1)} %get-tuple-element.66.qt.refs_4_, ...), custom_call_target="tpu_custom_call" | custom-call | flops 1000000000 | bytes 1 | tf_op jit(solution)/shard_map/own0/pallas_call | solution.py:605
  16.3 2.8 %collective-permute-start.1 = (bf16[2,2,2,192,128]{4,3,2,1,0:T(8,128)(2,1)S(1)}, bf16[2,2,2,192,128]{4,3,2,1,0:T(8,128)(2,1)S(1)}, u32[]{:S(2)}, u32[]{:S(2)}) collective-permute-start(bf16[2,2,2,192,128]{4,3,2,1,0:T(8,128)(2,1)S(1)} %pad_maximum_fusion.token), channel_id=1, source_target_pairs={{0,16},{4,20},{8,24},{12,28},{16,0},{20,4},{24,8},{28,12},{1,17},{... | collective-permute-start | bytes 1179656 | tf_op jit(solution)/shard_map/ppermute | solution.py:674
  19.2 1.6 %collective-permute-start.2 = (bf16[2,2,2,192,128]{4,3,2,1,0:T(8,128)(2,1)S(1)}, bf16[2,2,2,192,128]{4,3,2,1,0:T(8,128)(2,1)S(1)}, u32[]{:S(2)}, u32[]{:S(2)}) collective-permute-start(bf16[2,2,2,192,128]{4,3,2,1,0:T(8,128)(2,1)S(1)} %get-tuple-element.77), channel_id=1, source_target_pairs={{0,8},{4,12},{8,0},{12,4},{16,24},{20,28},{24,16},{28,20},{1,9},{5... | collective-permute-start | bytes 1179656 | tf_op jit(solution)/shard_map/ppermute | solution.py:674
  20.7 1.5 %collective-permute-start.4 = (bf16[4,3,192,128]{3,2,1,0:T(8,128)(2,1)S(1)}, bf16[4,3,192,128]{3,2,1,0:T(8,128)(2,1)S(1)}, u32[]{:S(2)}, u32[]{:S(2)}) collective-permute-start(bf16[4,3,192,128]{3,2,1,0:T(8,128)(2,1)S(1)} %get-tuple-element.90), channel_id=1, source_target_pairs={{0,4},{4,0},{8,12},{12,8},{16,20},{20,16},{24,28},{28,24},{1,5},{5... | collective-permute-start | bytes 1769480 | tf_op jit(solution)/shard_map/ppermute | solution.py:674
  22.3 5.8 %own2.1 = (f32[12,8,16,128]{3,2,1,0:T(8,128)S(1)}, f32[12,8,16,128]{3,2,1,0:T(8,128)S(1)}, f32[12,8,16,128]{3,2,1,0:T(8,128)S(1)}, f32[12,8,16,128]{3,2,1,0:T(8,128)S(1)}) custom-call(s32[3,16]{1,0:T(4,128)S(1)} %copy-done.1, bf16[4,12,8,16,128]{4,3,2,1,0:T(8,128)(2,1)S(1)} %get-tuple-element.66.qt.refs_4_, ...), custom_call_target="tpu_custom_call" | custom-call | flops 1000000000 | bytes 1 | tf_op jit(solution)/shard_map/own2/pallas_call | solution.py:605
  28.1 3.2 %lower.1 = (bf16[1600,128]{1,0:T(8,128)(2,1)S(1)}, f32[4,192,128]{2,1,0:T(8,128)S(1)}, f32[4,192,128]{2,1,0:T(8,128)S(1)}) custom-call(s32[3,16]{1,0:T(4,128)S(1)} %copy-done.1, bf16[8,192,128]{2,1,0:T(8,128)(2,1)S(1)} %collective-permute-done.3.got, bf16[4,12,8,16,128]{4,3,2,1,0:T(8,128)(2,1)S(1)} %get-tuple-element.66.qt.refs_4_, ...), custom_call_target="tpu_custom_call" | custom-call | flops 3000000000 | bytes 1 | tf_op jit(solution)/shard_map/lower/pallas_call | solution.py:613
  31.3 2.5 %weights.1 = (f32[12,8,16,128]{3,2,1,0:T(8,128)S(1)}, f32[12,8,16,128]{3,2,1,0:T(8,128)S(1)}, f32[12,8,16,128]{3,2,1,0:T(8,128)S(1)}, f32[12,8,16,128]{3,2,1,0:T(8,128)S(1)}, bf16[2048,2048]{1,0:T(8,128)(2,1)S(1)}) custom-call(s32[3,16]{1,0:T(4,128)S(1)} %copy-done.1, ...), custom_call_target="tpu_custom_call", output_to_operand_aliasing={{0}: (1, {}), {1}: (2, {}), {2}: (3, {}), {3}: (4, {})} | custom-call | flops 1000000000 | bytes 1 | tf_op jit(solution)/shard_map/weights/pallas_call | solution.py:685
  33.9 2.3 %collective-permute-done.1.far.refs_9_ = bf16[2,2,2,192,128]{4,3,2,1,0:T(8,128)(2,1)S(1)} collective-permute-done((bf16[2,2,2,192,128]{4,3,2,1,0:T(8,128)(2,1)S(1)}, bf16[2,2,2,192,128]{4,3,2,1,0:T(8,128)(2,1)S(1)}, u32[]{:S(2)}, u32[]{:S(2)}) %collective-permute-start.1) | collective-permute-done | bytes 393248 | tf_op jit(solution)/shard_map/ppermute | solution.py:674
  36.3 1.3 %collective-permute-start.8 = (bf16[2,2,2,192,128]{4,3,2,1,0:T(8,128)(2,1)S(1)}, bf16[2,2,2,192,128]{4,3,2,1,0:T(8,128)(2,1)S(1)}, u32[]{:S(2)}, u32[]{:S(2)}) collective-permute-start(bf16[2,2,2,192,128]{4,3,2,1,0:T(8,128)(2,1)S(1)} %get-tuple-element.101), channel_id=1, source_target_pairs={{0,8},{4,12},{8,0},{12,4},{16,24},{20,28},{24,16},{28,20},{1,9},{5... | collective-permute-start | bytes 1179656 | tf_op jit(solution)/shard_map/ppermute | solution.py:674
  37.6 2.3 %collective-permute-start.9 = (bf16[2,2,2,192,128]{4,3,2,1,0:T(8,128)(2,1)S(1)}, bf16[2,2,2,192,128]{4,3,2,1,0:T(8,128)(2,1)S(1)}, u32[]{:S(2)}, u32[]{:S(2)}) collective-permute-start(bf16[2,2,2,192,128]{4,3,2,1,0:T(8,128)(2,1)S(1)} %pad_maximum_fusion.1.token), channel_id=1, source_target_pairs={{0,16},{4,20},{8,24},{12,28},{16,0},{20,4},{24,8},{28,12},{1,17},{... | collective-permute-start | bytes 1179656 | tf_op jit(solution)/shard_map/ppermute | solution.py:674
  39.9 2.5 %partner0.1.refs_10_ = bf16[1216,128]{1,0:T(8,128)(2,1)S(1)} custom-call(s32[3,16]{1,0:T(4,128)S(1)} %copy-done.1, bf16[4,12,8,16,128]{4,3,2,1,0:T(8,128)(2,1)S(1)} %prep_k.1.kt.refs_5_, bf16[4,12,8,16,128]{4,3,2,1,0:T(8,128)(2,1)S(1)} %get-tuple-element.65.vt.refs_6_, bf16[4,3,192,128]{3,2,1,0:T(8,128)(2,1)S(1)} %collective-permute-done.4.q23, ...), custom_call_target="tpu_custom_call" | custom-call | flops 1000000000 | bytes 1 | tf_op jit(solution)/shard_map/partner0/pallas_call | solution.py:622
  42.4 1.5 %collective-permute-start.5 = (bf16[1216,128]{1,0:T(8,128)(2,1)S(1)}, bf16[1216,128]{1,0:T(8,128)(2,1)S(1)}, u32[]{:S(2)}, u32[]{:S(2)}) collective-permute-start(bf16[1216,128]{1,0:T(8,128)(2,1)S(1)} %partner0.1.refs_10_), channel_id=1, source_target_pairs={{0,4},{4,0},{8,12},{12,8},{16,20},{20,16},{24,28},{28,24},{1,5},{5... | collective-permute-start | bytes 933896 | tf_op jit(solution)/shard_map/ppermute | solution.py:674
  43.9 2.5 %mine0.1 = (f32[12,8,16,128]{3,2,1,0:T(8,128)S(1)}, f32[12,8,16,128]{3,2,1,0:T(8,128)S(1)}, f32[12,8,16,128]{3,2,1,0:T(8,128)S(1)}, f32[12,8,16,128]{3,2,1,0:T(8,128)S(1)}) custom-call(s32[3,16]{1,0:T(4,128)S(1)} %copy-done.1, ...), custom_call_target="tpu_custom_call", output_to_operand_aliasing={{0}: (1, {}), {1}: (2, {}), {2}: (3, {}), {3}: (4, {})} | custom-call | flops 10000000000 | bytes 1 | tf_op jit(solution)/shard_map/mine0/pallas_call | solution.py:631
  46.5 2.1 %last.1.refs_5_ = bf16[832,128]{1,0:T(8,128)(2,1)S(1)} custom-call(s32[3,16]{1,0:T(4,128)S(1)} %copy-done.1, bf16[1600,128]{1,0:T(8,128)(2,1)S(1)} %collective-permute-done.6.turn.refs_6_, bf16[4,12,8,16,128]{4,3,2,1,0:T(8,128)(2,1)S(1)} %prep_k.1.kt.refs_5_, bf16[4,12,8,16,128]{4,3,2,1,0:T(8,128)(2,1)S(1)} %get-tuple-element.65.vt.refs_6_, ...), custom_call_target="tpu_custom_call" | custom-call | flops 1000000000 | bytes 1 | tf_op jit(solution)/shard_map/last/pallas_call | solution.py:702
  48.7 3.1 %collective-permute-done.5.refs_4_ = bf16[1216,128]{1,0:T(8,128)(2,1)S(1)} collective-permute-done((bf16[1216,128]{1,0:T(8,128)(2,1)S(1)}, bf16[1216,128]{1,0:T(8,128)(2,1)S(1)}, u32[]{:S(2)}, u32[]{:S(2)}) %collective-permute-start.5) | collective-permute-done | bytes 311328 | tf_op jit(solution)/shard_map/ppermute | solution.py:674
  51.8 2.2 %finish0.1 = (bf16[384,256]{1,0:T(8,128)(2,1)S(1)}, bf16[384,256]{1,0:T(8,128)(2,1)S(1)}, bf16[2,384,256]{2,1,0:T(8,128)(2,1)S(1)}, bf16[8,128]{1,0:T(8,128)(2,1...) custom-call(s32[3,16]{1,0:T(4,128)S(1)} %copy-done.1, ...), custom_call_target="tpu_custom_call", output_to_operand_aliasing={{4}: (1, {}), {5}: (2, {}), {6}: (3, {}), {7}: (4, {})} | custom-call | flops 1000000000 | bytes 1 | tf_op jit(solution)/shard_map/finish0/pallas_call | solution.py:643
  54.0 1.5 %collective-permute-start.7 = (bf16[2,384,256]{2,1,0:T(8,128)(2,1)S(1)}, bf16[2,384,256]{2,1,0:T(8,128)(2,1)S(1)}, u32[]{:S(2)}, u32[]{:S(2)}) collective-permute-start(bf16[2,384,256]{2,1,0:T(8,128)(2,1)S(1)} %get-tuple-element.96), channel_id=1, source_target_pairs={{0,2},{1,3},{2,0},{3,1},{4,6},{5,7},{6,4},{7,5},{8,10},{9,11},{10,... | collective-permute-start | bytes 1179656 | tf_op jit(solution)/shard_map/ppermute | solution.py:674
  55.5 1.9 %collective-permute-done.9.far.refs_9_ = bf16[2,2,2,192,128]{4,3,2,1,0:T(8,128)(2,1)S(1)} collective-permute-done((bf16[2,2,2,192,128]{4,3,2,1,0:T(8,128)(2,1)S(1)}, bf16[2,2,2,192,128]{4,3,2,1,0:T(8,128)(2,1)S(1)}, u32[]{:S(2)}, u32[]{:S(2)}) %collective-permute-start.9) | collective-permute-done | bytes 393248 | tf_op jit(solution)/shard_map/ppermute | solution.py:674
  57.4 2.5 %partner2.1 = (bf16[640,128]{1,0:T(8,128)(2,1)S(1)}, bf16[640,128]{1,0:T(8,128)(2,1)S(1)}) custom-call(s32[3,16]{1,0:T(4,128)S(1)} %copy-done.1, bf16[4,12,8,16,128]{4,3,2,1,0:T(8,128)(2,1)S(1)} %prep_k.1.kt.refs_5_, bf16[4,12,8,16,128]{4,3,2,1,0:T(8,128)(2,1)S(1)} %get-tuple-element.65.vt.refs_6_, bf16[4,3,192,128]{3,2,1,0:T(8,128)(2,1)S(1)} %collective-permute-done.4.q23, ...), custom_call_target="tpu_custom_call" | custom-call | flops 10000000000 | bytes 1 | tf_op jit(solution)/shard_map/partner2/pallas_call | solution.py:622
  59.9 1.5 %collective-permute-start.10 = (bf16[640,128]{1,0:T(8,128)(2,1)S(1)}, bf16[640,128]{1,0:T(8,128)(2,1)S(1)}, u32[]{:S(2)}, u32[]{:S(2)}) collective-permute-start(bf16[640,128]{1,0:T(8,128)(2,1)S(1)} %get-tuple-element.110), channel_id=1, source_target_pairs={{0,4},{4,0},{8,12},{12,8},{16,20},{20,16},{24,28},{28,24},{1,5},{5... | collective-permute-start | bytes 491528 | tf_op jit(solution)/shard_map/ppermute | solution.py:674
  61.9 1.9 %mine2.1 = (f32[12,8,16,128]{3,2,1,0:T(8,128)S(1)}, f32[12,8,16,128]{3,2,1,0:T(8,128)S(1)}, f32[12,8,16,128]{3,2,1,0:T(8,128)S(1)}, f32[12,8,16,128]{3,2,1,0:T(8,128)S(1)}) custom-call(s32[3,16]{1,0:T(4,128)S(1)} %copy-done.1, ...), custom_call_target="tpu_custom_call", output_to_operand_aliasing={{0}: (1, {}), {1}: (2, {}), {2}: (3, {}), {3}: (4, {})} | custom-call | flops 1000000000 | bytes 1 | tf_op jit(solution)/shard_map/mine2/pallas_call | solution.py:631
  64.2 1.7 %collective-permute-done.10.refs_2_ = bf16[640,128]{1,0:T(8,128)(2,1)S(1)} collective-permute-done((bf16[640,128]{1,0:T(8,128)(2,1)S(1)}, bf16[640,128]{1,0:T(8,128)(2,1)S(1)}, u32[]{:S(2)}, u32[]{:S(2)}) %collective-permute-start.10) | collective-permute-done | bytes 163872 | tf_op jit(solution)/shard_map/ppermute | solution.py:674
  65.9 1.3 %finish2.1 = (bf16[384,128]{1,0:T(8,128)(2,1)S(1)}, bf16[384,128]{1,0:T(8,128)(2,1)S(1)}, bf16[2,384,128]{2,1,0:T(8,128)(2,1)S(1)}, bf16[8,128]{1,0:T(8,128)(2,1...) custom-call(s32[3,16]{1,0:T(4,128)S(1)} %copy-done.1, ...), custom_call_target="tpu_custom_call", output_to_operand_aliasing={{4}: (1, {}), {5}: (2, {})} | custom-call | flops 1000000000 | bytes 1 | tf_op jit(solution)/shard_map/finish2/pallas_call | solution.py:643
  67.3 1.6 %collective-permute-start.12 = (bf16[2,384,128]{2,1,0:T(8,128)(2,1)S(1)}, bf16[2,384,128]{2,1,0:T(8,128)(2,1)S(1)}, u32[]{:S(2)}, u32[]{:S(2)}) collective-permute-start(bf16[2,384,128]{2,1,0:T(8,128)(2,1)S(1)} %get-tuple-element.112), channel_id=1, source_target_pairs={{0,2},{1,3},{2,0},{3,1},{4,6},{5,7},{6,4},{7,5},{8,10},{9,11},{10,... | collective-permute-start | bytes 589832 | tf_op jit(solution)/shard_map/ppermute | solution.py:674
  68.9 1.0 %finish3.1 = (bf16[384,128]{1,0:T(8,128)(2,1)S(1)}, bf16[384,128]{1,0:T(8,128)(2,1)S(1)}, bf16[384,128]{1,0:T(8,128)(2,1)S(1)}, bf16[384,128]{1,0:T(8,128)(2,1)S...) custom-call(s32[3,16]{1,0:T(4,128)S(1)} %copy-done.1, ...), custom_call_target="tpu_custom_call", output_to_operand_aliasing={{4}: (1, {}), {5}: (2, {})} | custom-call | flops 1000000000 | bytes 1 | tf_op jit(solution)/shard_map/finish3/pallas_call | solution.py:643
  72.0 2.8 %project0.1.refs_6_.refs_8_ = f32[384,2048]{1,0:T(8,128)S(1)} custom-call(bf16[384,256]{1,0:T(8,128)(2,1)S(1)} %get-tuple-element.102.token.refs_0_, bf16[384,256]{1,0:T(8,128)(2,1)S(1)} %collective-permute-done.13.refs_1_, bf16[2,384,256]{2,1,0:T(8,128)(2,1)S(1)} %collective-permute-done.7.refs_2_, bf16[384,256]{1,0:T(8,128)(2,1)S(1)} %collective-permute-done.14.refs_3_, ...), custom_call_target="tpu_custom_call" | custom-call | flops 1000000000 | bytes 1 | tf_op jit(solution)/shard_map/project0/pallas_call | solution.py:660
  76.5 2.8 %project1280.1 = bf16[384,2048]{1,0:T(8,128)(2,1)} custom-call(bf16[2,384,128]{2,1,0:T(8,128)(2,1)S(1)} %collective-permute-done.12.refs_0_, bf16[384,128]{1,0:T(8,128)(2,1)S(1)} %collective-permute-done.17.refs_1_, bf16[384,128]{1,0:T(8,128)(2,1)S(1)} %get-tuple-element.119.refs_7_.refs_2_, bf16[384,128]{1,0:T(8,128)(2,1)S(1)} %collective-permute-done.18.refs_3_, ...), custom_call_target="tpu_custom_call" | custom-call | flops 1000000000 | bytes 1 | tf_op jit(solution)/shard_map/project1280/pallas_call | solution.py:660
  (46 shorter events, 6.9 us)
Async XLA Ops:
  0.0 2.0 %copy-start.1 = (s32[3,16]{1,0:T(4,128)S(1)}, s32[3,16]{1,0:T(4,128)}, u32[]{:S(2)}) copy-start(s32[3,16]{1,0:T(4,128)} %off_ref.27) | copy-start | bytes 580
  0.0 1.4 %copy-start.2 = (bf16[1536,512]{1,0:T(8,128)(2,1)S(1)}, bf16[1536,512]{1,0:T(8,128)(2,1)}, u32[]{:S(2)}) copy-start(bf16[1536,512]{1,0:T(8,128)(2,1)} %k_ref.1) | copy-start | bytes 4718596
  1.4 1.4 %copy-start.3 = (bf16[1536,512]{1,0:T(8,128)(2,1)S(1)}, bf16[1536,512]{1,0:T(8,128)(2,1)}, u32[]{:S(2)}) copy-start(bf16[1536,512]{1,0:T(8,128)(2,1)} %v_ref.1) | copy-start | bytes 4718596
  2.8 4.3 %copy-start = (bf16[1536,512]{1,0:T(8,128)(2,1)S(1)}, bf16[1536,512]{1,0:T(8,128)(2,1)}, u32[]{:S(2)}) copy-start(bf16[1536,512]{1,0:T(8,128)(2,1)} %q_ref.1) | copy-start | bytes 4718596
  4.1 12.2 %collective-permute-start = (bf16[4,2,192,128]{3,2,1,0:T(8,128)(2,1)S(1)}, bf16[4,2,192,128]{3,2,1,0:T(8,128)(2,1)S(1)}, u32[]{:S(2)}, u32[]{:S(2)}) collective-permute-start(bf16[4,2,192,128]{3,2,1,0:T(8,128)(2,1)S(1)} %get-tuple-element.67.token), channel_id=1, source_target_pairs={{0,8},{4,12},{8,0},{12,4},{16,24},{20,28},{24,16},{28,20},{1,9},{5... | collective-permute-start | bytes 1179656 | tf_op jit(solution)/shard_map/ppermute | solution.py:593
  8.4 19.7 %collective-permute-start.3 = (bf16[8,192,128]{2,1,0:T(8,128)(2,1)S(1)}, bf16[8,192,128]{2,1,0:T(8,128)(2,1)S(1)}, u32[]{:S(2)}, u32[]{:S(2)}) collective-permute-start(bf16[8,192,128]{2,1,0:T(8,128)(2,1)S(1)} %get-tuple-element.83), channel_id=1, source_target_pairs={{0,4},{4,0},{8,12},{12,8},{16,20},{20,16},{24,28},{28,24},{1,5},{5... | collective-permute-start | bytes 1179656 | tf_op jit(solution)/shard_map/ppermute | solution.py:600
  16.3 19.8 %collective-permute-start.1 = (bf16[2,2,2,192,128]{4,3,2,1,0:T(8,128)(2,1)S(1)}, bf16[2,2,2,192,128]{4,3,2,1,0:T(8,128)(2,1)S(1)}, u32[]{:S(2)}, u32[]{:S(2)}) collective-permute-start(bf16[2,2,2,192,128]{4,3,2,1,0:T(8,128)(2,1)S(1)} %pad_maximum_fusion.token), channel_id=1, source_target_pairs={{0,16},{4,20},{8,24},{12,28},{16,0},{20,4},{24,8},{28,12},{1,17},{... | collective-permute-start | bytes 1179656 | tf_op jit(solution)/shard_map/ppermute | solution.py:674
  19.2 17.2 %collective-permute-start.2 = (bf16[2,2,2,192,128]{4,3,2,1,0:T(8,128)(2,1)S(1)}, bf16[2,2,2,192,128]{4,3,2,1,0:T(8,128)(2,1)S(1)}, u32[]{:S(2)}, u32[]{:S(2)}) collective-permute-start(bf16[2,2,2,192,128]{4,3,2,1,0:T(8,128)(2,1)S(1)} %get-tuple-element.77), channel_id=1, source_target_pairs={{0,8},{4,12},{8,0},{12,4},{16,24},{20,28},{24,16},{28,20},{1,9},{5... | collective-permute-start | bytes 1179656 | tf_op jit(solution)/shard_map/ppermute | solution.py:674
  20.7 19.2 %collective-permute-start.4 = (bf16[4,3,192,128]{3,2,1,0:T(8,128)(2,1)S(1)}, bf16[4,3,192,128]{3,2,1,0:T(8,128)(2,1)S(1)}, u32[]{:S(2)}, u32[]{:S(2)}) collective-permute-start(bf16[4,3,192,128]{3,2,1,0:T(8,128)(2,1)S(1)} %get-tuple-element.90), channel_id=1, source_target_pairs={{0,4},{4,0},{8,12},{12,8},{16,20},{20,16},{24,28},{28,24},{1,5},{5... | collective-permute-start | bytes 1769480 | tf_op jit(solution)/shard_map/ppermute | solution.py:674
  22.3 9.0 %slice-start = ((s8[8388608]{0:T(1024)(128)(4,1)}), s8[4194304]{0:T(1024)(128)(4,1)S(1)}, s32[]{:S(2)}) async-start(s8[8388608]{0:T(1024)(128)(4,1)} %bitcast.12), calls=%async_computation | async-start | bytes 8388608
  28.1 3.2 %slice-start.1 = ((s8[8388608]{0:T(1024)(128)(4,1)}), s8[4194304]{0:T(1024)(128)(4,1)S(1)}, s32[]{:S(2)}) async-start(s8[8388608]{0:T(1024)(128)(4,1)} %bitcast.12), calls=%async_computation.1 | async-start | bytes 8388608
  31.3 15.2 %collective-permute-start.6 = (bf16[1600,128]{1,0:T(8,128)(2,1)S(1)}, bf16[1600,128]{1,0:T(8,128)(2,1)S(1)}, u32[]{:S(2)}, u32[]{:S(2)}) collective-permute-start(bf16[1600,128]{1,0:T(8,128)(2,1)S(1)} %get-tuple-element.86.refs_10_), channel_id=1, source_target_pairs={{0,4},{4,0},{8,12},{12,8},{16,20},{20,16},{24,28},{28,24},{1,5},{5... | collective-permute-start | bytes 1228808 | tf_op jit(solution)/shard_map/ppermute | solution.py:674
  36.3 19.2 %collective-permute-start.8 = (bf16[2,2,2,192,128]{4,3,2,1,0:T(8,128)(2,1)S(1)}, bf16[2,2,2,192,128]{4,3,2,1,0:T(8,128)(2,1)S(1)}, u32[]{:S(2)}, u32[]{:S(2)}) collective-permute-start(bf16[2,2,2,192,128]{4,3,2,1,0:T(8,128)(2,1)S(1)} %get-tuple-element.101), channel_id=1, source_target_pairs={{0,8},{4,12},{8,0},{12,4},{16,24},{20,28},{24,16},{28,20},{1,9},{5... | collective-permute-start | bytes 1179656 | tf_op jit(solution)/shard_map/ppermute | solution.py:674
  37.6 19.8 %collective-permute-start.9 = (bf16[2,2,2,192,128]{4,3,2,1,0:T(8,128)(2,1)S(1)}, bf16[2,2,2,192,128]{4,3,2,1,0:T(8,128)(2,1)S(1)}, u32[]{:S(2)}, u32[]{:S(2)}) collective-permute-start(bf16[2,2,2,192,128]{4,3,2,1,0:T(8,128)(2,1)S(1)} %pad_maximum_fusion.1.token), channel_id=1, source_target_pairs={{0,16},{4,20},{8,24},{12,28},{16,0},{20,4},{24,8},{28,12},{1,17},{... | collective-permute-start | bytes 1179656 | tf_op jit(solution)/shard_map/ppermute | solution.py:674
  42.4 9.4 %collective-permute-start.5 = (bf16[1216,128]{1,0:T(8,128)(2,1)S(1)}, bf16[1216,128]{1,0:T(8,128)(2,1)S(1)}, u32[]{:S(2)}, u32[]{:S(2)}) collective-permute-start(bf16[1216,128]{1,0:T(8,128)(2,1)S(1)} %partner0.1.refs_10_), channel_id=1, source_target_pairs={{0,4},{4,0},{8,12},{12,8},{16,20},{20,16},{24,28},{28,24},{1,5},{5... | collective-permute-start | bytes 933896 | tf_op jit(solution)/shard_map/ppermute | solution.py:674
  48.6 15.6 %collective-permute-start.11 = (bf16[832,128]{1,0:T(8,128)(2,1)S(1)}, bf16[832,128]{1,0:T(8,128)(2,1)S(1)}, u32[]{:S(2)}, u32[]{:S(2)}) collective-permute-start(bf16[832,128]{1,0:T(8,128)(2,1)S(1)} %last.1.refs_5_), channel_id=1, source_target_pairs={{0,4},{4,0},{8,12},{12,8},{16,20},{20,16},{24,28},{28,24},{1,5},{5... | collective-permute-start | bytes 638984 | tf_op jit(solution)/shard_map/ppermute | solution.py:674
  54.0 9.8 %collective-permute-start.7 = (bf16[2,384,256]{2,1,0:T(8,128)(2,1)S(1)}, bf16[2,384,256]{2,1,0:T(8,128)(2,1)S(1)}, u32[]{:S(2)}, u32[]{:S(2)}) collective-permute-start(bf16[2,384,256]{2,1,0:T(8,128)(2,1)S(1)} %get-tuple-element.96), channel_id=1, source_target_pairs={{0,2},{1,3},{2,0},{3,1},{4,6},{5,7},{6,4},{7,5},{8,10},{9,11},{10,... | collective-permute-start | bytes 1179656 | tf_op jit(solution)/shard_map/ppermute | solution.py:674
  59.9 6.1 %collective-permute-start.10 = (bf16[640,128]{1,0:T(8,128)(2,1)S(1)}, bf16[640,128]{1,0:T(8,128)(2,1)S(1)}, u32[]{:S(2)}, u32[]{:S(2)}) collective-permute-start(bf16[640,128]{1,0:T(8,128)(2,1)S(1)} %get-tuple-element.110), channel_id=1, source_target_pairs={{0,4},{4,0},{8,12},{12,8},{16,20},{20,16},{24,28},{28,24},{1,5},{5... | collective-permute-start | bytes 491528 | tf_op jit(solution)/shard_map/ppermute | solution.py:674
  61.4 9.1 %collective-permute-start.13 = (bf16[384,256]{1,0:T(8,128)(2,1)S(1)}, bf16[384,256]{1,0:T(8,128)(2,1)S(1)}, u32[]{:S(2)}, u32[]{:S(2)}) collective-permute-start(bf16[384,256]{1,0:T(8,128)(2,1)S(1)} %get-tuple-element.113), channel_id=1, source_target_pairs={{0,1},{1,0},{2,3},{3,2},{4,5},{5,4},{6,7},{7,6},{8,9},{9,8},{10,11... | collective-permute-start | bytes 589832 | tf_op jit(solution)/shard_map/ppermute | solution.py:674
  61.4 7.5 %collective-permute-start.16 = (bf16[640,128]{1,0:T(8,128)(2,1)S(1)}, bf16[640,128]{1,0:T(8,128)(2,1)S(1)}, u32[]{:S(2)}, u32[]{:S(2)}) collective-permute-start(bf16[640,128]{1,0:T(8,128)(2,1)S(1)} %get-tuple-element.103.refs_10_), channel_id=1, source_target_pairs={{0,4},{4,0},{8,12},{12,8},{16,20},{20,16},{24,28},{28,24},{1,5},{5... | collective-permute-start | bytes 491528 | tf_op jit(solution)/shard_map/ppermute | solution.py:674
  63.9 8.1 %collective-permute-start.14 = (bf16[384,256]{1,0:T(8,128)(2,1)S(1)}, bf16[384,256]{1,0:T(8,128)(2,1)S(1)}, u32[]{:S(2)}, u32[]{:S(2)}) collective-permute-start(bf16[384,256]{1,0:T(8,128)(2,1)S(1)} %slice_bitcast_fusion), channel_id=1, source_target_pairs={{0,1},{1,0},{2,3},{3,2},{4,5},{5,4},{6,7},{7,6},{8,9},{9,8},{10,11... | collective-permute-start | bytes 589832 | tf_op jit(solution)/shard_map/ppermute | solution.py:674
  67.3 7.5 %collective-permute-start.12 = (bf16[2,384,128]{2,1,0:T(8,128)(2,1)S(1)}, bf16[2,384,128]{2,1,0:T(8,128)(2,1)S(1)}, u32[]{:S(2)}, u32[]{:S(2)}) collective-permute-start(bf16[2,384,128]{2,1,0:T(8,128)(2,1)S(1)} %get-tuple-element.112), channel_id=1, source_target_pairs={{0,2},{1,3},{2,0},{3,1},{4,6},{5,7},{6,4},{7,5},{8,10},{9,11},{10,... | collective-permute-start | bytes 589832 | tf_op jit(solution)/shard_map/ppermute | solution.py:674
  68.9 2.5 %collective-permute-start.15 = (bf16[384,128]{1,0:T(8,128)(2,1)S(1)}, bf16[384,128]{1,0:T(8,128)(2,1)S(1)}, u32[]{:S(2)}, u32[]{:S(2)}) collective-permute-start(bf16[384,128]{1,0:T(8,128)(2,1)S(1)} %get-tuple-element.116), channel_id=1, source_target_pairs={{0,1},{1,0},{2,3},{3,2},{4,5},{5,4},{6,7},{7,6},{8,9},{9,8},{10,11... | collective-permute-start | bytes 294920 | tf_op jit(solution)/shard_map/ppermute | solution.py:674
  69.9 5.6 %collective-permute-start.18 = (bf16[384,128]{1,0:T(8,128)(2,1)S(1)}, bf16[384,128]{1,0:T(8,128)(2,1)S(1)}, u32[]{:S(2)}, u32[]{:S(2)}) collective-permute-start(bf16[384,128]{1,0:T(8,128)(2,1)S(1)} %get-tuple-element.121), channel_id=1, source_target_pairs={{0,1},{1,0},{2,3},{3,2},{4,5},{5,4},{6,7},{7,6},{8,9},{9,8},{10,11... | collective-permute-start | bytes 294920 | tf_op jit(solution)/shard_map/ppermute | solution.py:674
  70.5 5.7 %collective-permute-start.19 = (bf16[384,128]{1,0:T(8,128)(2,1)S(1)}, bf16[384,128]{1,0:T(8,128)(2,1)S(1)}, u32[]{:S(2)}, u32[]{:S(2)}) collective-permute-start(bf16[384,128]{1,0:T(8,128)(2,1)S(1)} %get-tuple-element.122), channel_id=1, source_target_pairs={{0,2},{1,3},{2,0},{3,1},{4,6},{5,7},{6,4},{7,5},{8,10},{9,11},{10,... | collective-permute-start | bytes 294920 | tf_op jit(solution)/shard_map/ppermute | solution.py:674
  71.4 5.1 %collective-permute-start.20 = (bf16[384,128]{1,0:T(8,128)(2,1)S(1)}, bf16[384,128]{1,0:T(8,128)(2,1)S(1)}, u32[]{:S(2)}, u32[]{:S(2)}) collective-permute-start(bf16[384,128]{1,0:T(8,128)(2,1)S(1)} %get-tuple-element.123), channel_id=1, source_target_pairs={{0,3},{1,2},{2,1},{3,0},{4,7},{5,6},{6,5},{7,4},{8,11},{9,10},{10,... | collective-permute-start | bytes 294920 | tf_op jit(solution)/shard_map/ppermute | solution.py:674
  74.8 1.7 %collective-permute-start.17 = (bf16[384,128]{1,0:T(8,128)(2,1)S(1)}, bf16[384,128]{1,0:T(8,128)(2,1)S(1)}, u32[]{:S(2)}, u32[]{:S(2)}) collective-permute-start(bf16[384,128]{1,0:T(8,128)(2,1)S(1)} %slice_bitcast_fusion.5), channel_id=1, source_target_pairs={{0,1},{1,0},{2,3},{3,2},{4,5},{5,4},{6,7},{7,6},{8,9},{9,8},{10,11... | collective-permute-start | bytes 294920 | tf_op jit(solution)/shard_map/ppermute | solution.py:674

commit v7 on v6

--- a/solution.py
+++ b/solution.py
@@ -518,16 +518,15 @@
             [src[0, rows, :] if len(src.shape) == 3 else src[rows, :] for src in pieces], axis=1
         )
         plain[rows, :] = jnp.dot(back, x, preferred_element_type=F32).astype(BF16)
-    tile = 1024
+    tile = 512
     steps = out.shape[1] // tile
 
     def copy(step):
-        cols = pl.ds(pl.multiple_of(step * tile, tile), tile)
+        cols = pl.ds(step * tile, tile)
         return pltpu.make_async_copy(out.at[:, cols], out_hbm.at[:, cols], sems.at[step])
 
-    @pl.loop(0, steps)
-    def _(step):
-        cols = pl.ds(pl.multiple_of(step * tile, tile), tile)
+    for step in range(steps):
+        cols = pl.ds(step * tile, tile)
         total = jnp.dot(
             plain[...], w_ref[first : first + depth, cols], preferred_element_type=F32
         )
@@ -538,9 +537,7 @@
             copy(step).start()
 
     if final:
-
-        @pl.loop(0, steps)
-        def _(step):
+        for step in range(steps):
             copy(step).wait()
 
 
@@ -655,7 +652,7 @@
         if final:
             scratch += [
                 pltpu.VMEM((rows_here // 4, model), BF16),
-                pltpu.SemaphoreType.DMA((model // 1024,)),
+                pltpu.SemaphoreType.DMA((model // 512,)),
             ]
         return call(
             functools.partial(project_kernel, first, len(before), final),

time: 80.1 us -> 79.6 us (level)
  no operation moved by 1% of the time
where the time goes in v7:
time: 79.6 us; the launch traced here: 79.1 us
  Pallas kernels  41.2 us (52%)
  starting transfers between devices  24 us (30%)
  waiting for transfers between devices  11 us (14%)
  local copies, waits for them, and re-layouts  2.34 us (3%)
    ppermute x19, starting transfers between devices, send(): return lax.ppermute(value, axis, pairs)  19.4 us
    pallas_call x2, Pallas kernels, own(): call(functools.partial(own_kernel, members), [SMEM, VMEM, VMEM, VMEM, ANY...  11.6 us
    ppermute x19, waiting for transfers between devices, send(): return lax.ppermute(value, axis, pairs)  10.5 us
    pallas_call x2, Pallas kernels, partner(): call(functools.partial(partner_kernel, members), [SMEM] + [VMEM] * 6 + [A...  4.94 us
    pallas_call x2, Pallas kernels, project(): call(functools.partial(project_kernel, first, len(before), final), [VMEM]...  4.82 us
    pallas_call x3, Pallas kernels, finished(): call(functools.partial(finish_kernel, members, stacked), [SMEM] + [VMEM]...  4.61 us
    pallas_call x2, Pallas kernels, mine(): call(functools.partial(mine_kernel, members, which), [SMEM] + [VMEM] * (l...  4.46 us
    pallas_call x1, Pallas kernels, lower(): call(functools.partial(lower_kernel, members), [SMEM] + [VMEM] * 4 + [ANY...  3.15 us
  transfers between devices with their start and end apart: 21, of which 8 were waited for; matrix products, arithmetic and copies ran while one was open for 0% of the time, Pallas kernels for 47%

profile of v7, /device:TPU:0, one launch (start us, length us, event | category | flops | bytes accessed | tf_op | source)
XLA Modules:
  0.0 79.1 jit_solution(7176646142109594069)
XLA Ops:
  0.0 1.4 %copy-done.2 = bf16[1536,512]{1,0:T(8,128)(2,1)S(1)} copy-done((bf16[1536,512]{1,0:T(8,128)(2,1)S(1)}, bf16[1536,512]{1,0:T(8,128)(2,1)}, u32[]{:S(2)}) %copy-start.2) | copy-done | bytes 1572888
  2.8 1.2 %prep_v.1 = (bf16[4,12,8,16,128]{4,3,2,1,0:T(8,128)(2,1)S(1)}, bf16[4,2,192,128]{3,2,1,0:T(8,128)(2,1)S(1)}, bf16[2,2,2,192,128]{4,3,2,1,0:T(8,128)(2,1)S(1)}, bf16[2,2,2,192,128]{4,3,2,1,0:T(8,128)(2,1)S(1)}) custom-call(s32[3,16]{1,0:T(4,128)S(1)} %copy-done.1, bf16[1536,512]{1,0:T(8,128)(2,1)S(1)} %copy-done.3, ...), custom_call_target="tpu_custom_call" | custom-call | flops 1000000000 | bytes 1 | tf_op jit(solution)/shard_map/prep_v/pallas_call | solution.py:583
  4.1 3.1 %collective-permute-start = (bf16[4,2,192,128]{3,2,1,0:T(8,128)(2,1)S(1)}, bf16[4,2,192,128]{3,2,1,0:T(8,128)(2,1)S(1)}, u32[]{:S(2)}, u32[]{:S(2)}) collective-permute-start(bf16[4,2,192,128]{3,2,1,0:T(8,128)(2,1)S(1)} %get-tuple-element.67.token), channel_id=1, source_target_pairs={{0,8},{4,12},{8,0},{12,4},{16,24},{20,28},{24,16},{28,20},{1,9},{5... | collective-permute-start | bytes 1179656 | tf_op jit(solution)/shard_map/ppermute | solution.py:590
  7.2 1.2 %prep_q.1 = (bf16[4,12,8,16,128]{4,3,2,1,0:T(8,128)(2,1)S(1)}, bf16[8,192,128]{2,1,0:T(8,128)(2,1)S(1)}, bf16[4,3,192,128]{3,2,1,0:T(8,128)(2,1)S(1)}) custom-call(s32[3,16]{1,0:T(4,128)S(1)} %copy-done.1, bf16[1536,512]{1,0:T(8,128)(2,1)S(1)} %copy-done, bf16[4,12,8,16,128]{4,3,2,1,0:T(8,128)(2,1)S(1)} %prep_k.1.kt.refs_5_, ...), custom_call_target="tpu_custom_call" | custom-call | flops 1000000000 | bytes 1 | tf_op jit(solution)/shard_map/prep_q/pallas_call | solution.py:591
  8.4 1.6 %collective-permute-start.3 = (bf16[8,192,128]{2,1,0:T(8,128)(2,1)S(1)}, bf16[8,192,128]{2,1,0:T(8,128)(2,1)S(1)}, u32[]{:S(2)}, u32[]{:S(2)}) collective-permute-start(bf16[8,192,128]{2,1,0:T(8,128)(2,1)S(1)} %get-tuple-element.83), channel_id=1, source_target_pairs={{0,4},{4,0},{8,12},{12,8},{16,20},{20,16},{24,28},{28,24},{1,5},{5... | collective-permute-start | bytes 1179656 | tf_op jit(solution)/shard_map/ppermute | solution.py:597
  10.0 5.8 %own0.1 = (f32[12,8,16,128]{3,2,1,0:T(8,128)S(1)}, f32[12,8,16,128]{3,2,1,0:T(8,128)S(1)}, f32[12,8,16,128]{3,2,1,0:T(8,128)S(1)}, f32[12,8,16,128]{3,2,1,0:T(8,128)S(1)}) custom-call(s32[3,16]{1,0:T(4,128)S(1)} %copy-done.1, bf16[4,12,8,16,128]{4,3,2,1,0:T(8,128)(2,1)S(1)} %get-tuple-element.66.qt.refs_4_, ...), custom_call_target="tpu_custom_call" | custom-call | flops 1000000000 | bytes 1 | tf_op jit(solution)/shard_map/own0/pallas_call | solution.py:602
  16.3 2.8 %collective-permute-start.1 = (bf16[2,2,2,192,128]{4,3,2,1,0:T(8,128)(2,1)S(1)}, bf16[2,2,2,192,128]{4,3,2,1,0:T(8,128)(2,1)S(1)}, u32[]{:S(2)}, u32[]{:S(2)}) collective-permute-start(bf16[2,2,2,192,128]{4,3,2,1,0:T(8,128)(2,1)S(1)} %pad_maximum_fusion.token), channel_id=1, source_target_pairs={{0,16},{4,20},{8,24},{12,28},{16,0},{20,4},{24,8},{28,12},{1,17},{... | collective-permute-start | bytes 1179656 | tf_op jit(solution)/shard_map/ppermute | solution.py:671
  19.2 1.6 %collective-permute-start.2 = (bf16[2,2,2,192,128]{4,3,2,1,0:T(8,128)(2,1)S(1)}, bf16[2,2,2,192,128]{4,3,2,1,0:T(8,128)(2,1)S(1)}, u32[]{:S(2)}, u32[]{:S(2)}) collective-permute-start(bf16[2,2,2,192,128]{4,3,2,1,0:T(8,128)(2,1)S(1)} %get-tuple-element.77), channel_id=1, source_target_pairs={{0,8},{4,12},{8,0},{12,4},{16,24},{20,28},{24,16},{28,20},{1,9},{5... | collective-permute-start | bytes 1179656 | tf_op jit(solution)/shard_map/ppermute | solution.py:671
  20.7 1.5 %collective-permute-start.4 = (bf16[4,3,192,128]{3,2,1,0:T(8,128)(2,1)S(1)}, bf16[4,3,192,128]{3,2,1,0:T(8,128)(2,1)S(1)}, u32[]{:S(2)}, u32[]{:S(2)}) collective-permute-start(bf16[4,3,192,128]{3,2,1,0:T(8,128)(2,1)S(1)} %get-tuple-element.90), channel_id=1, source_target_pairs={{0,4},{4,0},{8,12},{12,8},{16,20},{20,16},{24,28},{28,24},{1,5},{5... | collective-permute-start | bytes 1769480 | tf_op jit(solution)/shard_map/ppermute | solution.py:671
  22.3 5.8 %own2.1 = (f32[12,8,16,128]{3,2,1,0:T(8,128)S(1)}, f32[12,8,16,128]{3,2,1,0:T(8,128)S(1)}, f32[12,8,16,128]{3,2,1,0:T(8,128)S(1)}, f32[12,8,16,128]{3,2,1,0:T(8,128)S(1)}) custom-call(s32[3,16]{1,0:T(4,128)S(1)} %copy-done.1, bf16[4,12,8,16,128]{4,3,2,1,0:T(8,128)(2,1)S(1)} %get-tuple-element.66.qt.refs_4_, ...), custom_call_target="tpu_custom_call" | custom-call | flops 1000000000 | bytes 1 | tf_op jit(solution)/shard_map/own2/pallas_call | solution.py:602
  28.1 3.2 %lower.1 = (bf16[1600,128]{1,0:T(8,128)(2,1)S(1)}, f32[4,192,128]{2,1,0:T(8,128)S(1)}, f32[4,192,128]{2,1,0:T(8,128)S(1)}) custom-call(s32[3,16]{1,0:T(4,128)S(1)} %copy-done.1, bf16[8,192,128]{2,1,0:T(8,128)(2,1)S(1)} %collective-permute-done.3.got, bf16[4,12,8,16,128]{4,3,2,1,0:T(8,128)(2,1)S(1)} %get-tuple-element.66.qt.refs_4_, ...), custom_call_target="tpu_custom_call" | custom-call | flops 3000000000 | bytes 1 | tf_op jit(solution)/shard_map/lower/pallas_call | solution.py:610
  31.3 2.5 %weights.1 = (f32[12,8,16,128]{3,2,1,0:T(8,128)S(1)}, f32[12,8,16,128]{3,2,1,0:T(8,128)S(1)}, f32[12,8,16,128]{3,2,1,0:T(8,128)S(1)}, f32[12,8,16,128]{3,2,1,0:T(8,128)S(1)}, bf16[2048,2048]{1,0:T(8,128)(2,1)S(1)}) custom-call(s32[3,16]{1,0:T(4,128)S(1)} %copy-done.1, ...), custom_call_target="tpu_custom_call", output_to_operand_aliasing={{0}: (1, {}), {1}: (2, {}), {2}: (3, {}), {3}: (4, {})} | custom-call | flops 1000000000 | bytes 1 | tf_op jit(solution)/shard_map/weights/pallas_call | solution.py:682
  33.9 2.3 %collective-permute-done.1.far.refs_9_ = bf16[2,2,2,192,128]{4,3,2,1,0:T(8,128)(2,1)S(1)} collective-permute-done((bf16[2,2,2,192,128]{4,3,2,1,0:T(8,128)(2,1)S(1)}, bf16[2,2,2,192,128]{4,3,2,1,0:T(8,128)(2,1)S(1)}, u32[]{:S(2)}, u32[]{:S(2)}) %collective-permute-start.1) | collective-permute-done | bytes 393248 | tf_op jit(solution)/shard_map/ppermute | solution.py:671
  36.3 1.3 %collective-permute-start.8 = (bf16[2,2,2,192,128]{4,3,2,1,0:T(8,128)(2,1)S(1)}, bf16[2,2,2,192,128]{4,3,2,1,0:T(8,128)(2,1)S(1)}, u32[]{:S(2)}, u32[]{:S(2)}) collective-permute-start(bf16[2,2,2,192,128]{4,3,2,1,0:T(8,128)(2,1)S(1)} %get-tuple-element.101), channel_id=1, source_target_pairs={{0,8},{4,12},{8,0},{12,4},{16,24},{20,28},{24,16},{28,20},{1,9},{5... | collective-permute-start | bytes 1179656 | tf_op jit(solution)/shard_map/ppermute | solution.py:671
  37.6 2.3 %collective-permute-start.9 = (bf16[2,2,2,192,128]{4,3,2,1,0:T(8,128)(2,1)S(1)}, bf16[2,2,2,192,128]{4,3,2,1,0:T(8,128)(2,1)S(1)}, u32[]{:S(2)}, u32[]{:S(2)}) collective-permute-start(bf16[2,2,2,192,128]{4,3,2,1,0:T(8,128)(2,1)S(1)} %pad_maximum_fusion.1.token), channel_id=1, source_target_pairs={{0,16},{4,20},{8,24},{12,28},{16,0},{20,4},{24,8},{28,12},{1,17},{... | collective-permute-start | bytes 1179656 | tf_op jit(solution)/shard_map/ppermute | solution.py:671
  39.9 2.5 %partner0.1.refs_10_ = bf16[1216,128]{1,0:T(8,128)(2,1)S(1)} custom-call(s32[3,16]{1,0:T(4,128)S(1)} %copy-done.1, bf16[4,12,8,16,128]{4,3,2,1,0:T(8,128)(2,1)S(1)} %prep_k.1.kt.refs_5_, bf16[4,12,8,16,128]{4,3,2,1,0:T(8,128)(2,1)S(1)} %get-tuple-element.65.vt.refs_6_, bf16[4,3,192,128]{3,2,1,0:T(8,128)(2,1)S(1)} %collective-permute-done.4.q23, ...), custom_call_target="tpu_custom_call" | custom-call | flops 1000000000 | bytes 1 | tf_op jit(solution)/shard_map/partner0/pallas_call | solution.py:619
  42.4 1.5 %collective-permute-start.5 = (bf16[1216,128]{1,0:T(8,128)(2,1)S(1)}, bf16[1216,128]{1,0:T(8,128)(2,1)S(1)}, u32[]{:S(2)}, u32[]{:S(2)}) collective-permute-start(bf16[1216,128]{1,0:T(8,128)(2,1)S(1)} %partner0.1.refs_10_), channel_id=1, source_target_pairs={{0,4},{4,0},{8,12},{12,8},{16,20},{20,16},{24,28},{28,24},{1,5},{5... | collective-permute-start | bytes 933896 | tf_op jit(solution)/shard_map/ppermute | solution.py:671
  43.9 2.5 %mine0.1 = (f32[12,8,16,128]{3,2,1,0:T(8,128)S(1)}, f32[12,8,16,128]{3,2,1,0:T(8,128)S(1)}, f32[12,8,16,128]{3,2,1,0:T(8,128)S(1)}, f32[12,8,16,128]{3,2,1,0:T(8,128)S(1)}) custom-call(s32[3,16]{1,0:T(4,128)S(1)} %copy-done.1, ...), custom_call_target="tpu_custom_call", output_to_operand_aliasing={{0}: (1, {}), {1}: (2, {}), {2}: (3, {}), {3}: (4, {})} | custom-call | flops 10000000000 | bytes 1 | tf_op jit(solution)/shard_map/mine0/pallas_call | solution.py:628
  46.5 2.1 %last.1.refs_5_ = bf16[832,128]{1,0:T(8,128)(2,1)S(1)} custom-call(s32[3,16]{1,0:T(4,128)S(1)} %copy-done.1, bf16[1600,128]{1,0:T(8,128)(2,1)S(1)} %collective-permute-done.6.turn.refs_6_, bf16[4,12,8,16,128]{4,3,2,1,0:T(8,128)(2,1)S(1)} %prep_k.1.kt.refs_5_, bf16[4,12,8,16,128]{4,3,2,1,0:T(8,128)(2,1)S(1)} %get-tuple-element.65.vt.refs_6_, ...), custom_call_target="tpu_custom_call" | custom-call | flops 1000000000 | bytes 1 | tf_op jit(solution)/shard_map/last/pallas_call | solution.py:699
  48.7 3.1 %collective-permute-done.5.refs_4_ = bf16[1216,128]{1,0:T(8,128)(2,1)S(1)} collective-permute-done((bf16[1216,128]{1,0:T(8,128)(2,1)S(1)}, bf16[1216,128]{1,0:T(8,128)(2,1)S(1)}, u32[]{:S(2)}, u32[]{:S(2)}) %collective-permute-start.5) | collective-permute-done | bytes 311328 | tf_op jit(solution)/shard_map/ppermute | solution.py:671
  51.8 2.2 %finish0.1 = (bf16[384,256]{1,0:T(8,128)(2,1)S(1)}, bf16[384,256]{1,0:T(8,128)(2,1)S(1)}, bf16[2,384,256]{2,1,0:T(8,128)(2,1)S(1)}, bf16[8,128]{1,0:T(8,128)(2,1...) custom-call(s32[3,16]{1,0:T(4,128)S(1)} %copy-done.1, ...), custom_call_target="tpu_custom_call", output_to_operand_aliasing={{4}: (1, {}), {5}: (2, {}), {6}: (3, {}), {7}: (4, {})} | custom-call | flops 1000000000 | bytes 1 | tf_op jit(solution)/shard_map/finish0/pallas_call | solution.py:640
  54.0 1.5 %collective-permute-start.7 = (bf16[2,384,256]{2,1,0:T(8,128)(2,1)S(1)}, bf16[2,384,256]{2,1,0:T(8,128)(2,1)S(1)}, u32[]{:S(2)}, u32[]{:S(2)}) collective-permute-start(bf16[2,384,256]{2,1,0:T(8,128)(2,1)S(1)} %get-tuple-element.96), channel_id=1, source_target_pairs={{0,2},{1,3},{2,0},{3,1},{4,6},{5,7},{6,4},{7,5},{8,10},{9,11},{10,... | collective-permute-start | bytes 1179656 | tf_op jit(solution)/shard_map/ppermute | solution.py:671
  55.5 1.9 %collective-permute-done.9.far.refs_9_ = bf16[2,2,2,192,128]{4,3,2,1,0:T(8,128)(2,1)S(1)} collective-permute-done((bf16[2,2,2,192,128]{4,3,2,1,0:T(8,128)(2,1)S(1)}, bf16[2,2,2,192,128]{4,3,2,1,0:T(8,128)(2,1)S(1)}, u32[]{:S(2)}, u32[]{:S(2)}) %collective-permute-start.9) | collective-permute-done | bytes 393248 | tf_op jit(solution)/shard_map/ppermute | solution.py:671
  57.4 2.5 %partner2.1 = (bf16[640,128]{1,0:T(8,128)(2,1)S(1)}, bf16[640,128]{1,0:T(8,128)(2,1)S(1)}) custom-call(s32[3,16]{1,0:T(4,128)S(1)} %copy-done.1, bf16[4,12,8,16,128]{4,3,2,1,0:T(8,128)(2,1)S(1)} %prep_k.1.kt.refs_5_, bf16[4,12,8,16,128]{4,3,2,1,0:T(8,128)(2,1)S(1)} %get-tuple-element.65.vt.refs_6_, bf16[4,3,192,128]{3,2,1,0:T(8,128)(2,1)S(1)} %collective-permute-done.4.q23, ...), custom_call_target="tpu_custom_call" | custom-call | flops 10000000000 | bytes 1 | tf_op jit(solution)/shard_map/partner2/pallas_call | solution.py:619
  59.9 1.5 %collective-permute-start.10 = (bf16[640,128]{1,0:T(8,128)(2,1)S(1)}, bf16[640,128]{1,0:T(8,128)(2,1)S(1)}, u32[]{:S(2)}, u32[]{:S(2)}) collective-permute-start(bf16[640,128]{1,0:T(8,128)(2,1)S(1)} %get-tuple-element.110), channel_id=1, source_target_pairs={{0,4},{4,0},{8,12},{12,8},{16,20},{20,16},{24,28},{28,24},{1,5},{5... | collective-permute-start | bytes 491528 | tf_op jit(solution)/shard_map/ppermute | solution.py:671
  61.9 1.9 %mine2.1 = (f32[12,8,16,128]{3,2,1,0:T(8,128)S(1)}, f32[12,8,16,128]{3,2,1,0:T(8,128)S(1)}, f32[12,8,16,128]{3,2,1,0:T(8,128)S(1)}, f32[12,8,16,128]{3,2,1,0:T(8,128)S(1)}) custom-call(s32[3,16]{1,0:T(4,128)S(1)} %copy-done.1, ...), custom_call_target="tpu_custom_call", output_to_operand_aliasing={{0}: (1, {}), {1}: (2, {}), {2}: (3, {}), {3}: (4, {})} | custom-call | flops 1000000000 | bytes 1 | tf_op jit(solution)/shard_map/mine2/pallas_call | solution.py:628
  64.2 1.7 %collective-permute-done.10.refs_2_ = bf16[640,128]{1,0:T(8,128)(2,1)S(1)} collective-permute-done((bf16[640,128]{1,0:T(8,128)(2,1)S(1)}, bf16[640,128]{1,0:T(8,128)(2,1)S(1)}, u32[]{:S(2)}, u32[]{:S(2)}) %collective-permute-start.10) | collective-permute-done | bytes 163872 | tf_op jit(solution)/shard_map/ppermute | solution.py:671
  65.9 1.3 %finish2.1 = (bf16[384,128]{1,0:T(8,128)(2,1)S(1)}, bf16[384,128]{1,0:T(8,128)(2,1)S(1)}, bf16[2,384,128]{2,1,0:T(8,128)(2,1)S(1)}, bf16[8,128]{1,0:T(8,128)(2,1...) custom-call(s32[3,16]{1,0:T(4,128)S(1)} %copy-done.1, ...), custom_call_target="tpu_custom_call", output_to_operand_aliasing={{4}: (1, {}), {5}: (2, {})} | custom-call | flops 1000000000 | bytes 1 | tf_op jit(solution)/shard_map/finish2/pallas_call | solution.py:640
  67.3 1.6 %collective-permute-start.12 = (bf16[2,384,128]{2,1,0:T(8,128)(2,1)S(1)}, bf16[2,384,128]{2,1,0:T(8,128)(2,1)S(1)}, u32[]{:S(2)}, u32[]{:S(2)}) collective-permute-start(bf16[2,384,128]{2,1,0:T(8,128)(2,1)S(1)} %get-tuple-element.112), channel_id=1, source_target_pairs={{0,2},{1,3},{2,0},{3,1},{4,6},{5,7},{6,4},{7,5},{8,10},{9,11},{10,... | collective-permute-start | bytes 589832 | tf_op jit(solution)/shard_map/ppermute | solution.py:671
  68.9 1.0 %finish3.1 = (bf16[384,128]{1,0:T(8,128)(2,1)S(1)}, bf16[384,128]{1,0:T(8,128)(2,1)S(1)}, bf16[384,128]{1,0:T(8,128)(2,1)S(1)}, bf16[384,128]{1,0:T(8,128)(2,1)S...) custom-call(s32[3,16]{1,0:T(4,128)S(1)} %copy-done.1, ...), custom_call_target="tpu_custom_call", output_to_operand_aliasing={{4}: (1, {}), {5}: (2, {})} | custom-call | flops 1000000000 | bytes 1 | tf_op jit(solution)/shard_map/finish3/pallas_call | solution.py:640
  72.0 2.5 %project0.1.refs_6_.refs_8_ = f32[384,2048]{1,0:T(8,128)S(1)} custom-call(bf16[384,256]{1,0:T(8,128)(2,1)S(1)} %get-tuple-element.102.token.refs_0_, bf16[384,256]{1,0:T(8,128)(2,1)S(1)} %collective-permute-done.13.refs_1_, bf16[2,384,256]{2,1,0:T(8,128)(2,1)S(1)} %collective-permute-done.7.refs_2_, bf16[384,256]{1,0:T(8,128)(2,1)S(1)} %collective-permute-done.14.refs_3_, ...), custom_call_target="tpu_custom_call" | custom-call | flops 1000000000 | bytes 1 | tf_op jit(solution)/shard_map/project0/pallas_call | solution.py:657
  76.5 2.4 %project1280.1 = bf16[384,2048]{1,0:T(8,128)(2,1)} custom-call(bf16[2,384,128]{2,1,0:T(8,128)(2,1)S(1)} %collective-permute-done.12.refs_0_, bf16[384,128]{1,0:T(8,128)(2,1)S(1)} %collective-permute-done.17.refs_1_, bf16[384,128]{1,0:T(8,128)(2,1)S(1)} %get-tuple-element.119.refs_7_.refs_2_, bf16[384,128]{1,0:T(8,128)(2,1)S(1)} %collective-permute-done.18.refs_3_, ...), custom_call_target="tpu_custom_call" | custom-call | flops 1000000000 | bytes 1 | tf_op jit(solution)/shard_map/project1280/pallas_call | solution.py:657
  (46 shorter events, 7.2 us)
Async XLA Ops:
  0.0 2.0 %copy-start.1 = (s32[3,16]{1,0:T(4,128)S(1)}, s32[3,16]{1,0:T(4,128)}, u32[]{:S(2)}) copy-start(s32[3,16]{1,0:T(4,128)} %off_ref.27) | copy-start | bytes 580
  0.0 1.4 %copy-start.2 = (bf16[1536,512]{1,0:T(8,128)(2,1)S(1)}, bf16[1536,512]{1,0:T(8,128)(2,1)}, u32[]{:S(2)}) copy-start(bf16[1536,512]{1,0:T(8,128)(2,1)} %k_ref.1) | copy-start | bytes 4718596
  1.4 1.4 %copy-start.3 = (bf16[1536,512]{1,0:T(8,128)(2,1)S(1)}, bf16[1536,512]{1,0:T(8,128)(2,1)}, u32[]{:S(2)}) copy-start(bf16[1536,512]{1,0:T(8,128)(2,1)} %v_ref.1) | copy-start | bytes 4718596
  2.8 4.3 %copy-start = (bf16[1536,512]{1,0:T(8,128)(2,1)S(1)}, bf16[1536,512]{1,0:T(8,128)(2,1)}, u32[]{:S(2)}) copy-start(bf16[1536,512]{1,0:T(8,128)(2,1)} %q_ref.1) | copy-start | bytes 4718596
  4.1 12.2 %collective-permute-start = (bf16[4,2,192,128]{3,2,1,0:T(8,128)(2,1)S(1)}, bf16[4,2,192,128]{3,2,1,0:T(8,128)(2,1)S(1)}, u32[]{:S(2)}, u32[]{:S(2)}) collective-permute-start(bf16[4,2,192,128]{3,2,1,0:T(8,128)(2,1)S(1)} %get-tuple-element.67.token), channel_id=1, source_target_pairs={{0,8},{4,12},{8,0},{12,4},{16,24},{20,28},{24,16},{28,20},{1,9},{5... | collective-permute-start | bytes 1179656 | tf_op jit(solution)/shard_map/ppermute | solution.py:590
  8.4 19.7 %collective-permute-start.3 = (bf16[8,192,128]{2,1,0:T(8,128)(2,1)S(1)}, bf16[8,192,128]{2,1,0:T(8,128)(2,1)S(1)}, u32[]{:S(2)}, u32[]{:S(2)}) collective-permute-start(bf16[8,192,128]{2,1,0:T(8,128)(2,1)S(1)} %get-tuple-element.83), channel_id=1, source_target_pairs={{0,4},{4,0},{8,12},{12,8},{16,20},{20,16},{24,28},{28,24},{1,5},{5... | collective-permute-start | bytes 1179656 | tf_op jit(solution)/shard_map/ppermute | solution.py:597
  16.3 19.8 %collective-permute-start.1 = (bf16[2,2,2,192,128]{4,3,2,1,0:T(8,128)(2,1)S(1)}, bf16[2,2,2,192,128]{4,3,2,1,0:T(8,128)(2,1)S(1)}, u32[]{:S(2)}, u32[]{:S(2)}) collective-permute-start(bf16[2,2,2,192,128]{4,3,2,1,0:T(8,128)(2,1)S(1)} %pad_maximum_fusion.token), channel_id=1, source_target_pairs={{0,16},{4,20},{8,24},{12,28},{16,0},{20,4},{24,8},{28,12},{1,17},{... | collective-permute-start | bytes 1179656 | tf_op jit(solution)/shard_map/ppermute | solution.py:671
  19.2 17.2 %collective-permute-start.2 = (bf16[2,2,2,192,128]{4,3,2,1,0:T(8,128)(2,1)S(1)}, bf16[2,2,2,192,128]{4,3,2,1,0:T(8,128)(2,1)S(1)}, u32[]{:S(2)}, u32[]{:S(2)}) collective-permute-start(bf16[2,2,2,192,128]{4,3,2,1,0:T(8,128)(2,1)S(1)} %get-tuple-element.77), channel_id=1, source_target_pairs={{0,8},{4,12},{8,0},{12,4},{16,24},{20,28},{24,16},{28,20},{1,9},{5... | collective-permute-start | bytes 1179656 | tf_op jit(solution)/shard_map/ppermute | solution.py:671
  20.7 19.2 %collective-permute-start.4 = (bf16[4,3,192,128]{3,2,1,0:T(8,128)(2,1)S(1)}, bf16[4,3,192,128]{3,2,1,0:T(8,128)(2,1)S(1)}, u32[]{:S(2)}, u32[]{:S(2)}) collective-permute-start(bf16[4,3,192,128]{3,2,1,0:T(8,128)(2,1)S(1)} %get-tuple-element.90), channel_id=1, source_target_pairs={{0,4},{4,0},{8,12},{12,8},{16,20},{20,16},{24,28},{28,24},{1,5},{5... | collective-permute-start | bytes 1769480 | tf_op jit(solution)/shard_map/ppermute | solution.py:671
  22.3 9.0 %slice-start = ((s8[8388608]{0:T(1024)(128)(4,1)}), s8[4194304]{0:T(1024)(128)(4,1)S(1)}, s32[]{:S(2)}) async-start(s8[8388608]{0:T(1024)(128)(4,1)} %bitcast.12), calls=%async_computation | async-start | bytes 8388608
  28.1 3.2 %slice-start.1 = ((s8[8388608]{0:T(1024)(128)(4,1)}), s8[4194304]{0:T(1024)(128)(4,1)S(1)}, s32[]{:S(2)}) async-start(s8[8388608]{0:T(1024)(128)(4,1)} %bitcast.12), calls=%async_computation.1 | async-start | bytes 8388608
  31.3 15.2 %collective-permute-start.6 = (bf16[1600,128]{1,0:T(8,128)(2,1)S(1)}, bf16[1600,128]{1,0:T(8,128)(2,1)S(1)}, u32[]{:S(2)}, u32[]{:S(2)}) collective-permute-start(bf16[1600,128]{1,0:T(8,128)(2,1)S(1)} %get-tuple-element.86.refs_10_), channel_id=1, source_target_pairs={{0,4},{4,0},{8,12},{12,8},{16,20},{20,16},{24,28},{28,24},{1,5},{5... | collective-permute-start | bytes 1228808 | tf_op jit(solution)/shard_map/ppermute | solution.py:671
  36.3 19.2 %collective-permute-start.8 = (bf16[2,2,2,192,128]{4,3,2,1,0:T(8,128)(2,1)S(1)}, bf16[2,2,2,192,128]{4,3,2,1,0:T(8,128)(2,1)S(1)}, u32[]{:S(2)}, u32[]{:S(2)}) collective-permute-start(bf16[2,2,2,192,128]{4,3,2,1,0:T(8,128)(2,1)S(1)} %get-tuple-element.101), channel_id=1, source_target_pairs={{0,8},{4,12},{8,0},{12,4},{16,24},{20,28},{24,16},{28,20},{1,9},{5... | collective-permute-start | bytes 1179656 | tf_op jit(solution)/shard_map/ppermute | solution.py:671
  37.6 19.8 %collective-permute-start.9 = (bf16[2,2,2,192,128]{4,3,2,1,0:T(8,128)(2,1)S(1)}, bf16[2,2,2,192,128]{4,3,2,1,0:T(8,128)(2,1)S(1)}, u32[]{:S(2)}, u32[]{:S(2)}) collective-permute-start(bf16[2,2,2,192,128]{4,3,2,1,0:T(8,128)(2,1)S(1)} %pad_maximum_fusion.1.token), channel_id=1, source_target_pairs={{0,16},{4,20},{8,24},{12,28},{16,0},{20,4},{24,8},{28,12},{1,17},{... | collective-permute-start | bytes 1179656 | tf_op jit(solution)/shard_map/ppermute | solution.py:671
  42.4 9.4 %collective-permute-start.5 = (bf16[1216,128]{1,0:T(8,128)(2,1)S(1)}, bf16[1216,128]{1,0:T(8,128)(2,1)S(1)}, u32[]{:S(2)}, u32[]{:S(2)}) collective-permute-start(bf16[1216,128]{1,0:T(8,128)(2,1)S(1)} %partner0.1.refs_10_), channel_id=1, source_target_pairs={{0,4},{4,0},{8,12},{12,8},{16,20},{20,16},{24,28},{28,24},{1,5},{5... | collective-permute-start | bytes 933896 | tf_op jit(solution)/shard_map/ppermute | solution.py:671
  48.6 15.6 %collective-permute-start.11 = (bf16[832,128]{1,0:T(8,128)(2,1)S(1)}, bf16[832,128]{1,0:T(8,128)(2,1)S(1)}, u32[]{:S(2)}, u32[]{:S(2)}) collective-permute-start(bf16[832,128]{1,0:T(8,128)(2,1)S(1)} %last.1.refs_5_), channel_id=1, source_target_pairs={{0,4},{4,0},{8,12},{12,8},{16,20},{20,16},{24,28},{28,24},{1,5},{5... | collective-permute-start | bytes 638984 | tf_op jit(solution)/shard_map/ppermute | solution.py:671
  54.0 9.8 %collective-permute-start.7 = (bf16[2,384,256]{2,1,0:T(8,128)(2,1)S(1)}, bf16[2,384,256]{2,1,0:T(8,128)(2,1)S(1)}, u32[]{:S(2)}, u32[]{:S(2)}) collective-permute-start(bf16[2,384,256]{2,1,0:T(8,128)(2,1)S(1)} %get-tuple-element.96), channel_id=1, source_target_pairs={{0,2},{1,3},{2,0},{3,1},{4,6},{5,7},{6,4},{7,5},{8,10},{9,11},{10,... | collective-permute-start | bytes 1179656 | tf_op jit(solution)/shard_map/ppermute | solution.py:671
  59.9 6.1 %collective-permute-start.10 = (bf16[640,128]{1,0:T(8,128)(2,1)S(1)}, bf16[640,128]{1,0:T(8,128)(2,1)S(1)}, u32[]{:S(2)}, u32[]{:S(2)}) collective-permute-start(bf16[640,128]{1,0:T(8,128)(2,1)S(1)} %get-tuple-element.110), channel_id=1, source_target_pairs={{0,4},{4,0},{8,12},{12,8},{16,20},{20,16},{24,28},{28,24},{1,5},{5... | collective-permute-start | bytes 491528 | tf_op jit(solution)/shard_map/ppermute | solution.py:671
  61.4 9.1 %collective-permute-start.13 = (bf16[384,256]{1,0:T(8,128)(2,1)S(1)}, bf16[384,256]{1,0:T(8,128)(2,1)S(1)}, u32[]{:S(2)}, u32[]{:S(2)}) collective-permute-start(bf16[384,256]{1,0:T(8,128)(2,1)S(1)} %get-tuple-element.113), channel_id=1, source_target_pairs={{0,1},{1,0},{2,3},{3,2},{4,5},{5,4},{6,7},{7,6},{8,9},{9,8},{10,11... | collective-permute-start | bytes 589832 | tf_op jit(solution)/shard_map/ppermute | solution.py:671
  61.4 7.5 %collective-permute-start.16 = (bf16[640,128]{1,0:T(8,128)(2,1)S(1)}, bf16[640,128]{1,0:T(8,128)(2,1)S(1)}, u32[]{:S(2)}, u32[]{:S(2)}) collective-permute-start(bf16[640,128]{1,0:T(8,128)(2,1)S(1)} %get-tuple-element.103.refs_10_), channel_id=1, source_target_pairs={{0,4},{4,0},{8,12},{12,8},{16,20},{20,16},{24,28},{28,24},{1,5},{5... | collective-permute-start | bytes 491528 | tf_op jit(solution)/shard_map/ppermute | solution.py:671
  63.9 8.1 %collective-permute-start.14 = (bf16[384,256]{1,0:T(8,128)(2,1)S(1)}, bf16[384,256]{1,0:T(8,128)(2,1)S(1)}, u32[]{:S(2)}, u32[]{:S(2)}) collective-permute-start(bf16[384,256]{1,0:T(8,128)(2,1)S(1)} %slice_bitcast_fusion), channel_id=1, source_target_pairs={{0,1},{1,0},{2,3},{3,2},{4,5},{5,4},{6,7},{7,6},{8,9},{9,8},{10,11... | collective-permute-start | bytes 589832 | tf_op jit(solution)/shard_map/ppermute | solution.py:671
  67.3 7.1 %collective-permute-start.12 = (bf16[2,384,128]{2,1,0:T(8,128)(2,1)S(1)}, bf16[2,384,128]{2,1,0:T(8,128)(2,1)S(1)}, u32[]{:S(2)}, u32[]{:S(2)}) collective-permute-start(bf16[2,384,128]{2,1,0:T(8,128)(2,1)S(1)} %get-tuple-element.112), channel_id=1, source_target_pairs={{0,2},{1,3},{2,0},{3,1},{4,6},{5,7},{6,4},{7,5},{8,10},{9,11},{10,... | collective-permute-start | bytes 589832 | tf_op jit(solution)/shard_map/ppermute | solution.py:671
  68.9 2.5 %collective-permute-start.15 = (bf16[384,128]{1,0:T(8,128)(2,1)S(1)}, bf16[384,128]{1,0:T(8,128)(2,1)S(1)}, u32[]{:S(2)}, u32[]{:S(2)}) collective-permute-start(bf16[384,128]{1,0:T(8,128)(2,1)S(1)} %get-tuple-element.116), channel_id=1, source_target_pairs={{0,1},{1,0},{2,3},{3,2},{4,5},{5,4},{6,7},{7,6},{8,9},{9,8},{10,11... | collective-permute-start | bytes 294920 | tf_op jit(solution)/shard_map/ppermute | solution.py:671
  69.9 5.3 %collective-permute-start.18 = (bf16[384,128]{1,0:T(8,128)(2,1)S(1)}, bf16[384,128]{1,0:T(8,128)(2,1)S(1)}, u32[]{:S(2)}, u32[]{:S(2)}) collective-permute-start(bf16[384,128]{1,0:T(8,128)(2,1)S(1)} %get-tuple-element.121), channel_id=1, source_target_pairs={{0,1},{1,0},{2,3},{3,2},{4,5},{5,4},{6,7},{7,6},{8,9},{9,8},{10,11... | collective-permute-start | bytes 294920 | tf_op jit(solution)/shard_map/ppermute | solution.py:671
  70.5 5.7 %collective-permute-start.19 = (bf16[384,128]{1,0:T(8,128)(2,1)S(1)}, bf16[384,128]{1,0:T(8,128)(2,1)S(1)}, u32[]{:S(2)}, u32[]{:S(2)}) collective-permute-start(bf16[384,128]{1,0:T(8,128)(2,1)S(1)} %get-tuple-element.122), channel_id=1, source_target_pairs={{0,2},{1,3},{2,0},{3,1},{4,6},{5,7},{6,4},{7,5},{8,10},{9,11},{10,... | collective-permute-start | bytes 294920 | tf_op jit(solution)/shard_map/ppermute | solution.py:671
  71.4 5.1 %collective-permute-start.20 = (bf16[384,128]{1,0:T(8,128)(2,1)S(1)}, bf16[384,128]{1,0:T(8,128)(2,1)S(1)}, u32[]{:S(2)}, u32[]{:S(2)}) collective-permute-start(bf16[384,128]{1,0:T(8,128)(2,1)S(1)} %get-tuple-element.123), channel_id=1, source_target_pairs={{0,3},{1,2},{2,1},{3,0},{4,7},{5,6},{6,5},{7,4},{8,11},{9,10},{10,... | collective-permute-start | bytes 294920 | tf_op jit(solution)/shard_map/ppermute | solution.py:671
  74.5 2.1 %collective-permute-start.17 = (bf16[384,128]{1,0:T(8,128)(2,1)S(1)}, bf16[384,128]{1,0:T(8,128)(2,1)S(1)}, u32[]{:S(2)}, u32[]{:S(2)}) collective-permute-start(bf16[384,128]{1,0:T(8,128)(2,1)S(1)} %slice_bitcast_fusion.5), channel_id=1, source_target_pairs={{0,1},{1,0},{2,3},{3,2},{4,5},{5,4},{6,7},{7,6},{8,9},{9,8},{10,11... | collective-permute-start | bytes 294920 | tf_op jit(solution)/shard_map/ppermute | solution.py:671
